TPU v7x, 256 devices: a whole 4x4x8 slice. The times are simulated.
256 devices in a mesh: dp: 32 (over z, y_lo, core), grp: 8 (over x, y_hi).
Axes of the slice: x: 4, y: 4 (y_hi: 2, y_lo: 2; y = y_hi * 2 + y_lo), z: 8, core: 2. Of those that a mesh axis runs over, the one named last changes fastest.
Arguments:
- hidden_acts: bfloat16 [4, 16384, 11008], P(None, 'dp', 'grp'), may hold values from -30 to 30
- out_grads: bfloat16 [4, 16384, 4096], P(None, 'dp', 'grp'), may hold values from -30 to 30
- weight_grad: bfloat16 [4, 11008, 4096], P(None, 'grp', 'dp'), may hold values from -6 to 6
- owner_a: int32 [4, 64], P(None, 'grp'), may hold values from 0 to 31, as said below
- gradient_block_owner: int32 [4, 32], P(None, 'grp'), may hold values from 0 to 31, as said below
Outputs:
- precond_grad: bfloat16 [4, 11008, 4096], P(None, 'grp', 'dp')
- store_a: bfloat16 [8, 32, 2, 172, 172], P('grp', 'dp')
- store_g: bfloat16 [8, 32, 2, 128, 128], P('grp', 'dp')
Inputs may be any that keep to these rules, and one draw needn't show every extreme that they name: `owner_a`: within the blocks of one grp index (all layers together), each dp index owns at most 2 input-side blocks, and one owns exactly 2. `gradient_block_owner`: within the blocks of one grp index (all layers together), each dp index owns at most 2 output-side blocks, and one owns exactly 2.
All inputs are finite; a program needn't handle non-finite values.
Results may differ from a plain program's by a relative error of at most 0.0064.
Values may be sent and summed in bfloat16 or wider, within the bound.
No kernel may reach another device: no remote copies, remote signals or barrier semaphores. Data moves between devices by JAX's collectives and lax.ppermute only.
A program may use at most 128 MiB of HBM per device.

v0:
```python
import jax
import jax.numpy as jnp
from jax import lax
from jax.sharding import PartitionSpec as P

D = 4096
FF = 11008
ITERS = 12
BA = 172
BG = 128


damping_share = 0.01


def spread(value, axis, source):
    kept = jnp.where(lax.axis_index(axis) == source, value, 0).astype(value.dtype)
    return lax.psum(kept, axis)


def inverse_roots(blocks, filler):
    width = blocks.shape[-1]
    identity = jnp.eye(width, dtype=jnp.float32)
    trace_raw = jnp.trace(blocks, axis1=1, axis2=2)
    damped = blocks + (damping_share * trace_raw / width + filler)[:, None, None] * identity
    total = jnp.trace(damped, axis1=1, axis2=2)
    start_y = damped / total[:, None, None]
    start_z = jnp.broadcast_to(identity, damped.shape)

    def sweep(index, carry):
        left_y, left_z = carry
        poly = 1.5 * identity - 0.5 * jnp.einsum(
            "nij,njk->nik", left_z, left_y, precision=lax.Precision.HIGHEST
        )
        next_y = jnp.einsum("nij,njk->nik", left_y, poly, precision=lax.Precision.HIGHEST)
        next_z = jnp.einsum("nij,njk->nik", poly, left_z, precision=lax.Precision.HIGHEST)
        return (next_y, next_z)

    final_y, final_z = lax.fori_loop(0, ITERS, sweep, (start_y, start_z))
    return (final_z / jnp.sqrt(total)[:, None, None]).astype(jnp.bfloat16)


def owner_ranks(owners):
    places = jnp.arange(owners.shape[0], dtype=jnp.int32)
    same = owners[:, None] == owners[None, :]
    earlier = places[None, :] < places[:, None]
    return jnp.sum(jnp.logical_and(same, earlier), axis=1)


def local_covariance(acts, width, scale):
    layers, rows, features = acts.shape
    blocks = acts.reshape(layers, rows, features // width, width)
    partial_cov = jnp.einsum("ltkb,ltkc->lkbc", blocks, blocks, preferred_element_type=jnp.float32)
    return (partial_cov * scale).reshape(layers * (features // width), width, width)


def dispatch_blocks(blocks, slot_indices, total_slots):
    width = blocks.shape[-1]
    empty = jnp.zeros((total_slots, width, width), jnp.float32)
    return empty.at[slot_indices].set(blocks)


def pick_roots(gathered, slot_indices):
    places = jnp.arange(gathered.shape[0], dtype=jnp.int32)
    selector = (slot_indices[:, None] == places[None, :]).astype(jnp.bfloat16)
    picked = jnp.einsum("cs,sij->cij", selector, gathered, preferred_element_type=jnp.float32)
    return picked.astype(jnp.bfloat16)


def slot_active_flags(slot_indices, owner_position, block_slots):
    wanted = owner_position * block_slots + jnp.arange(block_slots, dtype=jnp.int32)
    return jnp.any(wanted[:, None] == slot_indices[None, :], axis=1).astype(jnp.float32)


def owned_roots(blocks, slot_indices, owner_position, block_slots):
    live_flags = slot_active_flags(slot_indices, owner_position, block_slots)
    roots = inverse_roots(blocks, 1.0 - live_flags)
    return roots * live_flags.astype(jnp.bfloat16)[:, None, None]


def shards(hidden_acts, out_grads, weight_grad, owner_a, gradient_block_owner):
    layers = hidden_acts.shape[0]
    dp_count = lax.axis_size("dp")
    grp_count = lax.axis_size("grp")
    devices_all = dp_count * grp_count
    owner_position = lax.axis_index("dp")
    column = lax.axis_index("grp")
    scale = 1.0 / (hidden_acts.shape[1] * dp_count)
    slots_a = 2 * ((layers * (FF // BA) + devices_all - 1) // devices_all)
    slots_g = 2 * ((layers * (D // BG) + devices_all - 1) // devices_all)
    cov_a = local_covariance(hidden_acts, BA, scale)
    cov_g = local_covariance(out_grads, BG, scale)
    flat_a = owner_a.reshape(-1)
    flat_g = gradient_block_owner.reshape(-1)
    slot_a = flat_a * slots_a + owner_ranks(flat_a)
    slot_g = flat_g * slots_g + owner_ranks(flat_g)
    routed_a = dispatch_blocks(cov_a, slot_a, dp_count * slots_a)
    summed_a = lax.psum_scatter(routed_a, "dp", scatter_dimension=0, tiled=True)
    kept_a = owned_roots(summed_a, slot_a, owner_position, slots_a)
    all_a = lax.all_gather(kept_a, "dp", axis=0, tiled=True)
    column_a = pick_roots(all_a, slot_a)
    routed_g = dispatch_blocks(cov_g, slot_g, dp_count * slots_g)
    summed_g = lax.psum_scatter(routed_g, "dp", scatter_dimension=0, tiled=True)
    kept_g = owned_roots(summed_g, slot_g, owner_position, slots_g)
    all_g = lax.all_gather(kept_g, "dp", axis=0, tiled=True)
    column_g = pick_roots(all_g, slot_g)
    per_column_g = flat_g.shape[0] // layers
    column_g = column_g.reshape(layers, per_column_g, BG, BG)
    out_cols = weight_grad.shape[2]
    blocks_here = out_cols // BG
    wanted_start = owner_position * blocks_here - column * per_column_g
    wanted_start = jnp.clip(wanted_start, 0, per_column_g - blocks_here)
    candidate = lax.dynamic_slice_in_dim(column_g, wanted_start, blocks_here, 1)
    source_column = owner_position * blocks_here // per_column_g
    right_side = spread(candidate, "grp", source_column)
    in_rows = weight_grad.shape[1]
    tiles = weight_grad.reshape(layers, in_rows, blocks_here, BG)
    mid = jnp.einsum(
        "lfjb,ljbc->lfjc", tiles, right_side, preferred_element_type=jnp.float32
    ).astype(jnp.bfloat16)
    mid = mid.reshape(layers, in_rows // BA, BA, out_cols)
    left_side = column_a.reshape(layers, in_rows // BA, BA, BA)
    result = jnp.einsum(
        "lkab,lkbd->lkad", left_side, mid, preferred_element_type=jnp.float32
    ).astype(jnp.bfloat16)
    precond_grad = result.reshape(layers, in_rows, out_cols)
    return (
        precond_grad,
        kept_a.reshape(1, 1, slots_a, BA, BA),
        kept_g.reshape(1, 1, slots_g, BG, BG),
    )


def solution(mesh):
    return jax.shard_map(
        shards,
        mesh=mesh,
        in_specs=(
            P(None, "dp", "grp"),
            P(None, "dp", "grp"),
            P(None, "grp", "dp"),
            P(None, "grp"),
            P(None, "grp"),
        ),
        out_specs=(
            P(None, "grp", "dp"),
            P("grp", "dp", None, None, None),
            P("grp", "dp", None, None, None),
        ),
        check_vma=False,
    )
```

profile of v0, /device:TPU:30, one launch (start us, length us, event | category | flops | bytes accessed | tf_op | source)
XLA Modules:
  0.0 539.4 jit_solution(4941645616682092907)
XLA Ops:
  9.9 2.4 broadcast_in_dim.38
  12.3 3.0 scatter_fusion.1
  15.6 121.8 %reduce-scatter.5.cloned.1.call-done = f32[2,128,128]{2,1,0:T(8,128)} async-done(((f32[64,128,128]{2,1,0:T(8,128)}), f32[2,128,128]{2,1,0:T(8,128)}) %reduce-scatter.5.cloned.1.call-update) | async-done | bytes 131088 | tf_op jit(solution)/shard_map/reduce_scatter | solution.py:103
  137.4 1.0 select_reduce_fusion.3
  138.4 1.1 select_reduce_fusion.2
  140.7 13.5 %while.27 = (s32[]{:T(128)}, f32[2,128,128]{1,2,0:T(8,128)S(1)}, f32[2,128,128]{2,1,0:T(8,128)S(1)}, s32[]{:T(128)}) while((s32[]{:T(128)}, f32[2,128,128]{1,2,0:T(8,128)S(1)}, f32[2,128,128]{2,1,0:T(8,128)S(1)}, s32[]{:T(128)}) %tuple.55), condition=%wide.region_15.16_spmd.clone, body=%wide.region_14.15_spmd.clone.sunk | while | flops 151093248 | bytes 1835061 | solution.py:39
  155.2 7.8 %reshape.193 = bf16[4,512,8,172]{1,3,2,0:T(8,128)(2,1)} reshape(bf16[4,512,1376]{1,2,0:T(8,128)(2,1)} %param.9) | data formatting | bytes 11272192 | tf_op jit(solution)/shard_map/reshape | solution.py:52
  163.1 8.5 %broadcast_multiply_fusion = f32[4,8,172,172]{3,2,1,0:T(8,128)} fusion(bf16[4,512,8,172]{1,3,2,0:T(8,128)(2,1)} %reshape.193), kind=kOutput, calls=%fused_computation.19 | convolution fusion | flops 970355200 | bytes 9422848 | tf_op jit(solution)/shard_map/ltkb,ltkc->lkbc/dot_general | solution.py:53
  171.6 5.8 %broadcast_in_dim.34 = f32[64,172,172]{2,1,0:T(8,128)} broadcast(f32[]{:T(128)} %constant.47.clone.1), dimensions={} | broadcast | bytes 7573508 | tf_op jit(solution)/shard_map/broadcast_in_dim | solution.py:59
  177.3 13.1 %scatter_fusion = f32[64,172,172]{2,1,0:T(8,128)} fusion(f32[64,172,172]{2,1,0:T(8,128)} %broadcast_in_dim.34, s32[32]{0:T(128)S(1)} %fusion.44, f32[32,172,172]{2,1,0:T(8,128)} %bitcast.97), kind=kCustom, calls=%fused_computation | custom fusion | bytes 11360384 | tf_op jit(solution)/shard_map/scatter | solution.py:60
  190.8 30.2 %all-gather.5.cloned.1.call-done = bf16[64,128,128]{2,1,0:T(8,128)(2,1)} async-done(((bf16[2,128,128]{2,1,0:T(8,128)(2,1)}), bf16[64,128,128]{2,1,0:T(8,128)(2,1)}) %all-gather.5.cloned.1.call-update) | async-done | bytes 2097168 | tf_op jit(solution)/shard_map/all_gather | solution.py:105
  221.0 2.8 fusion.26
  225.1 135.3 %reduce-scatter.3.cloned.1.call-done = f32[2,172,172]{2,1,0:T(8,128)} async-done(((f32[64,172,172]{2,1,0:T(8,128)}), f32[2,172,172]{2,1,0:T(8,128)}) %reduce-scatter.3.cloned.1.call-update) | async-done | bytes 236688 | tf_op jit(solution)/shard_map/reduce_scatter | solution.py:98
  360.4 1.1 select_reduce_fusion.1
  361.6 1.2 select_reduce_fusion
  362.8 1.1 fusion.29
  364.1 24.2 %while.26 = (s32[]{:T(128)}, f32[2,172,172]{1,2,0:T(8,128)S(1)}, f32[2,172,172]{2,1,0:T(8,128)S(1)}, s32[]{:T(128)}) while((s32[]{:T(128)}, f32[2,172,172]{1,2,0:T(8,128)S(1)}, f32[2,172,172]{2,1,0:T(8,128)S(1)}, s32[]{:T(128)}) %tuple.58), condition=%wide.region_7.8_spmd.clone, body=%wide.region_6.7_spmd.clone.sunk | while | flops 366545760 | bytes 3313461 | solution.py:39
  389.9 60.9 %all-reduce.2.cloned.1.call-done = bf16[4,128,128]{2,1,0:T(8,128)(2,1)} async-done(((bf16[4,128,128]{2,1,0:T(8,128)(2,1)}), bf16[4,128,128]{2,1,0:T(8,128)(2,1)}) %all-reduce.2.cloned.1.call-update) | async-done | bytes 131088 | tf_op jit(solution)/shard_map/psum | solution.py:18
  450.8 3.0 fusion.12
  453.7 3.2 reshape.201
  457.9 64.4 %all-gather.3.cloned.1.call-done = bf16[64,172,172]{2,1,0:T(8,128)(2,1)} async-done(((bf16[2,172,172]{2,1,0:T(8,128)(2,1)}), bf16[64,172,172]{2,1,0:T(8,128)(2,1)}) %all-gather.3.cloned.1.call-update) | async-done | bytes 3786768 | tf_op jit(solution)/shard_map/all_gather | solution.py:100
  522.3 4.4 convert_bitcast_fusion
  526.7 3.0 fusion.20
  529.7 3.2 reshape.202
  (196 shorter events, 45.7 us)
Async XLA Ops:
  7.2 1.9 copy-start
  7.2 130.2 %reduce-scatter.5.cloned.1.call-start = ((), (), s32[]{:S(2)}) async-start(), calls=%async_computation.4 | async-start | bytes 4325376 | tf_op jit(solution)/shard_map/reduce_scatter | solution.py:103
  15.3 205.7 %all-gather.5.cloned.1.call-start = ((), (), s32[]{:S(2)}) async-start(), calls=%async_computation.5 | async-start | bytes 2162688 | tf_op jit(solution)/shard_map/all_gather | solution.py:105
  140.6 14.4 %copy-start.2 = (s32[4,8]{1,0:T(4,128)S(1)}, s32[4,8]{1,0:T(4,128)}, u32[]{:S(2)}) copy-start(s32[4,8]{1,0:T(4,128)} %param.12) | copy-start | bytes 388
  155.0 205.5 %reduce-scatter.3.cloned.1.call-start = ((), (), s32[]{:S(2)}) async-start(), calls=%async_computation.2 | async-start | bytes 11894784 | tf_op jit(solution)/shard_map/reduce_scatter | solution.py:98
  190.5 260.3 %all-reduce.2.cloned.1.call-start = ((), (), s32[]{:S(2)}) async-start(), calls=%async_computation.6 | async-start | bytes 262144 | tf_op jit(solution)/shard_map/psum | solution.py:18
  224.9 297.5 %all-gather.3.cloned.1.call-start = ((), (), s32[]{:S(2)}) async-start(), calls=%async_computation.3 | async-start | bytes 5947392 | tf_op jit(solution)/shard_map/all_gather | solution.py:100
  457.9 68.8 %copy-start.1 = (bf16[4,8,172,128]{3,2,1,0:T(8,128)(2,1)S(1)}, bf16[4,8,172,128]{3,2,1,0:T(8,128)(2,1)}, u32[]{:S(2)}) copy-start(bf16[4,8,172,128]{3,2,1,0:T(8,128)(2,1)} %reshape.201) | copy-start | bytes 4227076
Sparse Core Ops, SparseCore 0:
  15.4 121.9 reduce-scatter.4
  155.1 65.8 all-gather.4
  223.6 136.7 reduce-scatter.2
  363.5 87.2 all-reduce.1
  452.6 69.6 all-gather.2
where the time goes:
time: 542 us; the launch traced here: 539 us
  waiting for transfers between devices  413 us (76%)
  matrix products  57.5 us (11%)
  local copies, waits for them, and re-layouts  42 us (8%)
  between operations  14 us (3%)
  other arithmetic  11.4 us (2%)
    reduce_scatter x1, waiting for transfers between devices, shards(): summed_a = lax.psum_scatter(routed_a, 'dp', scatter_dimension=0, tiled=True)  135 us
    reduce_scatter x1, waiting for transfers between devices, shards(): summed_g = lax.psum_scatter(routed_g, 'dp', scatter_dimension=0, tiled=True)  122 us
    all_gather x1, waiting for transfers between devices, shards(): all_a = lax.all_gather(kept_a, 'dp', axis=0, tiled=True)  64.4 us
    psum x1, waiting for transfers between devices, spread(): return lax.psum(kept, axis)  60.9 us
    all_gather x1, waiting for transfers between devices, shards(): all_g = lax.all_gather(kept_g, 'dp', axis=0, tiled=True)  30.2 us
    scatter x2, local copies, waits for them, and re-layouts, dispatch_blocks(): return empty.at[slot_indices].set(blocks)  16.1 us
    dot_general x24, matrix products, sweep(): jnp.einsum('nij,njk->nik', left_y, poly, precision=lax.Precision.HIGHEST)  15.3 us
  transfers between devices with their start and end apart: 5, of which 5 were waited for; matrix products, arithmetic and copies ran while one was open for 14% of the time, Pallas kernels for 0%

commit v1 on v0

v1 whole, which is shorter than its diff:
```python
import functools

import jax
import jax.numpy as jnp
from jax import lax
from jax.experimental import pallas as pl
from jax.experimental.pallas import tpu as pltpu
from jax.sharding import PartitionSpec as P

ITERS = 12
BA = 172
BG = 128
LAYERS = 4
HALF = 64
NARROW = BA - BG
RA = 144
RG = 64
MSG = RA + RG
PAIR = RA + RG + RA
DIAG = 136
GATHERED = RA + RG // 2
TAIL = 128
WIRE = jnp.float16
WIRE_SCALE = 512.0

damping_share = 0.01

PARAMS = pltpu.CompilerParams(vmem_limit_bytes=48 << 20)


def iota(shape, dim):
    return lax.broadcasted_iota(jnp.int32, shape, dim)


def pack_square(top, bottom):
    row, lane = iota((HALF, BG), 0), iota((HALF, BG), 1)
    turned = pltpu.roll(bottom, HALF, 1)
    folded = jnp.where((lane < HALF) & (row >= lane), turned, top)
    diagonal = jnp.sum(jnp.where(row == lane, top, 0.0), axis=0, keepdims=True)
    return folded, diagonal


def unpack_square(folded, diagonal):
    row, lane = iota((HALF, BG), 0), iota((HALF, BG), 1)
    top = jnp.where(lane > row, folded, jnp.where(lane == row, 0.5 * diagonal, 0.0))
    left = jnp.where(lane < row, folded, jnp.where(lane == row, 0.5 * folded, 0.0))
    bottom = pltpu.roll(left, HALF, 1)
    once = jnp.concatenate([top, bottom], axis=0)
    return once + once.T


def pack_wide(full, spare):
    folded, diagonal = pack_square(full[0:HALF, 0:BG], full[HALF:BG, 0:BG])
    low = full[BG : BG + 48, 0:BG]
    corner = full[BG : BG + 48, BG:256]
    corner = corner[0:24] + pltpu.roll(corner[24:48], HALF, 1)
    both = diagonal + pltpu.roll(spare, HALF, 1)
    last = jnp.where(iota((8, BG), 0) == 0, both, 0.0)
    return folded, low, jnp.concatenate([corner, last], axis=0)


def unpack_wide(packed):
    square = unpack_square(packed[0:HALF], packed[DIAG : DIAG + 1])
    low = packed[HALF : HALF + 48]
    tall = jnp.concatenate([low, jnp.zeros((80, BG), jnp.float32)], axis=0).T
    corner = packed[112:136]
    lane, row = iota((24, BG), 1), iota((24, BG), 0)
    first = jnp.where(lane < NARROW, corner, 0.0)
    second = jnp.where((lane < NARROW) & (row < NARROW - 24), pltpu.roll(corner, HALF, 1), 0.0)
    corner = jnp.concatenate([first, second], axis=0)
    return jnp.concatenate(
        [jnp.concatenate([square, tall], axis=1), jnp.concatenate([low, corner], axis=1)], axis=0
    )


def cov_kernel(scale, sel_ref, h_ref, g_ref, o_ref, wide):
    wide[...] = jnp.zeros_like(wide)
    squares = []
    for m in range(4):
        x = g_ref[m]
        c = lax.dot_general(x, x, (((0,), (0,)), ((), ())), preferred_element_type=jnp.float32)
        squares.append(pack_square(c[0:HALF] * scale, c[HALF:BG] * scale))
    for k in range(8):
        x = h_ref[0, BA * k : BA * (k + 1), :]
        c = lax.dot_general(x, x, (((1,), (1,)), ((), ())), preferred_element_type=jnp.float32)
        wide[k, 0:BA, 0:BA] = c * scale
    z = sel_ref[1]
    for m in range(4):
        folded, spare = squares[m]
        o_ref[0, lax.rem(m - z + 8, 4), RA : RA + RG] = folded
        for k in (m, m + 4):
            shift = lax.rem(k - z + 8, 8)
            place, base = lax.rem(shift, 4), pl.multiple_of((shift // 4) * MSG, 16)
            folded, low, corner = pack_wide(wide.at[k], spare)
            o_ref[0, place, pl.ds(base, HALF)] = folded
            o_ref[0, place, pl.ds(base + HALF, 48)] = low
            o_ref[0, place, pl.ds(base + 112, 32)] = corner


def covariances(turned, grads, core, z, scale):
    rows, features = turned.shape[2], turned.shape[1]
    return pl.pallas_call(
        functools.partial(cov_kernel, scale),
        grid_spec=pltpu.PrefetchScalarGridSpec(
            num_scalar_prefetch=1,
            grid=(2,),
            in_specs=[
                pl.BlockSpec((1, features, rows), lambda i, s: (2 * s[0] + i, 0, 0)),
                pl.BlockSpec((LAYERS, rows, BG), lambda i, s: (0, 0, 2 * i + s[0])),
            ],
            out_specs=pl.BlockSpec((1, 4, PAIR, BG), lambda i, s: (i, 0, 0, 0)),
            scratch_shapes=[pltpu.VMEM((8, 176, 256), jnp.float32)],
        ),
        out_shape=jax.ShapeDtypeStruct((2, 4, PAIR, BG), jnp.float32),
        compiler_params=PARAMS,
        cost_estimate=pl.CostEstimate(flops=2 * 10**9, bytes_accessed=6 * 10**6, transcendentals=0),
        name="covariances",
    )(jnp.stack([core, z]), turned, grads)


def parts_of(x):
    high = x.astype(jnp.bfloat16)
    return high, (x - high.astype(jnp.float32)).astype(jnp.bfloat16)


def times(a, b):
    def one(i, j):
        return jnp.dot(a[i], b[j], preferred_element_type=jnp.float32)

    return (one(0, 1) + one(1, 0)) + one(0, 0)


def roots_kernel(z_ref, total_ref, packed_ref, wide, square):
    total = total_ref[...]
    spare = pltpu.roll(total[DIAG : DIAG + 1], HALF, 1)
    blocks = [unpack_wide(total[0:RA])[0:BA, 0:BA], unpack_square(total[RA:MSG], spare)]
    eyes, ys, totals = [], [], []
    for c in blocks:
        width = c.shape[0]
        eye = (iota(c.shape, 0) == iota(c.shape, 1)).astype(jnp.float32)
        damped = c + (damping_share * jnp.sum(c * eye) / width) * eye
        trace = jnp.sum(damped * eye)
        eyes.append(eye)
        ys.append(damped / trace)
        totals.append(trace)
    both = range(2)
    zs = [1.5 * eyes[i] - 0.5 * ys[i] for i in both]
    ys = [times(parts_of(ys[i]), parts_of(zs[i])) for i in both]

    def sweep(_, carry):
        ys, zs = carry
        sy, sz = [parts_of(y) for y in ys], [parts_of(z) for z in zs]
        sp = [parts_of(1.5 * eyes[i] - 0.5 * times(sz[i], sy[i])) for i in both]
        return [times(sy[i], sp[i]) for i in both], [times(sp[i], sz[i]) for i in both]

    ys, zs = lax.fori_loop(0, ITERS - 2, sweep, (ys, zs))
    sz = [parts_of(z) for z in zs]
    sp = [parts_of(1.5 * eyes[i] - 0.5 * times(sz[i], parts_of(ys[i]))) for i in both]
    roots = [times(sp[i], sz[i]) / jnp.sqrt(totals[i]) for i in both]
    wide[...] = jnp.zeros_like(wide)
    wide[0:BA, 0:BA] = roots[0]
    square[...], spare = pack_square(roots[1][0:HALF], roots[1][HALF:BG])
    folded, low, corner = pack_wide(wide, spare)
    packed_ref[0:HALF] = folded.astype(jnp.bfloat16)
    packed_ref[HALF:112] = low.astype(jnp.bfloat16)
    packed_ref[112:RA] = corner.astype(jnp.bfloat16)
    start = pl.multiple_of((z_ref[0] // 4) * (RG // 2), RG // 2)
    packed_ref[RA:GATHERED] = square[pl.ds(start, RG // 2)].astype(jnp.bfloat16)


def inverse_roots(total, z):
    whole = pl.BlockSpec(memory_space=pltpu.VMEM)
    return pl.pallas_call(
        roots_kernel,
        in_specs=[pl.BlockSpec(memory_space=pltpu.SMEM), whole],
        out_specs=whole,
        out_shape=jax.ShapeDtypeStruct((GATHERED, BG), jnp.bfloat16),
        scratch_shapes=[pltpu.VMEM((176, 256), jnp.float32), pltpu.VMEM((RG, BG), jnp.float32)],
        compiler_params=PARAMS,
        name="inverse_roots",
    )(z.reshape(1), total)


def unpack_halves(first, second):
    folded = jnp.concatenate([first[16:48], second[16:48]], axis=0)
    return unpack_square(folded, pltpu.roll(first[DIAG - TAIL : DIAG - TAIL + 1], HALF, 1))


def apply_kernel(at_ref, w_ref, a_ref, rights_ref, out_ref, sa_ref, sg_ref, right, mid):
    z, y, c, g = (at_ref[i] for i in range(4))

    def place(z_of, y_of, c_of):
        away = lax.rem(z - z_of + 8, 8)
        middle = (away == 0) | (away == 4)
        holder = jnp.where(middle, c_of, (away > 4).astype(jnp.int32))
        step = jnp.where(away > 4, 8 - away, away)
        slot = jnp.where(middle, 7 * (away // 4), 2 * step - 1 + jnp.bitwise_xor(c_of, holder))
        return jnp.bitwise_xor(holder, c), jnp.bitwise_xor(y_of, y), slot

    for d in range(8):
        right[lax.rem(g - (1 - 2 * c) * d + 8, 8)] = rights_ref[d].astype(jnp.float32)
    for layer in range(LAYERS):
        root = unpack_halves(right[layer], right[layer + 4]).astype(jnp.bfloat16)
        product = jnp.dot(w_ref[layer], root, preferred_element_type=jnp.float32)
        mid[layer] = product.astype(jnp.bfloat16).astype(jnp.float32)
        for quad in range(2):
            results = []
            for k in range(4 * quad, 4 * quad + 4):
                i, j, slot = place(k, layer % 2, layer // 2)
                left = unpack_wide(a_ref[i, j, slot, 0:RA].astype(jnp.float32))
                left = left[0:BA, 0:BA].astype(jnp.bfloat16)
                x = mid[layer, BA * k : BA * (k + 1)].astype(jnp.bfloat16)
                results.append(jnp.dot(left, x, preferred_element_type=jnp.float32))
            out_ref[layer, 4 * BA * quad : 4 * BA * (quad + 1)] = jnp.concatenate(
                results, axis=0
            ).astype(jnp.bfloat16)
    for r in range(2):
        block = at_ref[4 + r]
        held = jnp.maximum(block, 0)
        layer = held // 8
        i, j, slot = place(lax.rem(held, 8), lax.rem(layer, 2), layer // 2)
        root = unpack_wide(a_ref[i, j, slot, 0:RA].astype(jnp.float32))[0:BA, 0:BA]
        sa_ref[r] = jnp.where(block >= 0, root, 0.0).astype(jnp.bfloat16)
        block = at_ref[6 + r]
        held = jnp.maximum(block, 0)
        layer, k = held // 4, lax.rem(held, 4)
        halves = []
        for half in range(2):
            i, j, slot = place(layer + 4 * half, k // 2, lax.rem(k, 2))
            halves.append(a_ref[i, j, slot, TAIL:GATHERED].astype(jnp.float32))
        root = unpack_halves(*halves)
        sg_ref[r] = jnp.where(block >= 0, root, 0.0).astype(jnp.bfloat16)


def apply_roots(at, weight_grad, lefts, rights):
    whole = pl.BlockSpec(memory_space=pltpu.VMEM)
    rows = weight_grad.shape[1]
    return pl.pallas_call(
        apply_kernel,
        in_specs=[pl.BlockSpec(memory_space=pltpu.SMEM)] + [whole] * 3,
        out_specs=[whole] * 3,
        out_shape=[
            jax.ShapeDtypeStruct(weight_grad.shape, jnp.bfloat16),
            jax.ShapeDtypeStruct((2, BA, BA), jnp.bfloat16),
            jax.ShapeDtypeStruct((2, BG, BG), jnp.bfloat16),
        ],
        scratch_shapes=[
            pltpu.VMEM((8, GATHERED - TAIL, BG), jnp.float32),
            pltpu.VMEM((LAYERS, rows, BG), jnp.float32),
        ],
        compiler_params=PARAMS,
        name="apply_roots",
    )(at, weight_grad, lefts, rights)


def owned_blocks(owners, position):
    flat = owners.reshape(-1)
    mine = flat == position
    rank = jnp.cumsum(mine.astype(jnp.int32)) - 1
    places = jnp.arange(flat.shape[0], dtype=jnp.int32)
    return [jnp.max(jnp.where(mine & (rank == r), places, -1)) for r in range(2)]


def along_z(shift, away=False):
    return [(i, (i + 4 * shift * (1 - 2 * (i % 2) if away else 1)) % 32) for i in range(32)]


OVER_CORE = [(i, i ^ 1) for i in range(32)]
OVER_Y = [(i, i ^ 2) for i in range(32)]
EXCHANGE = [
    ((z * 4 + r) * 8 + g, (g * 4 + r) * 8 + z) for z in range(8) for r in range(4) for g in range(8)
]


def narrow(x):
    return (x * WIRE_SCALE).astype(WIRE)


def widen(x):
    return x.astype(jnp.float32) * (1.0 / WIRE_SCALE)


def shards(hidden_acts, out_grads, weight_grad, owner_a, gradient_block_owner):
    position = lax.axis_index("dp")
    column = lax.axis_index("grp")
    z, y, core = position // 4, lax.rem(position // 2, 2), lax.rem(position, 2)
    scale = 1.0 / (hidden_acts.shape[1] * lax.axis_size("dp"))
    turned = jnp.swapaxes(hidden_acts, 1, 2)

    theirs = covariances(turned, out_grads, 1 - core, z, scale)
    got = lax.ppermute(theirs, "dp", OVER_CORE)
    mine = covariances(turned, out_grads, core, z, scale)

    def summed(at):
        one = lax.dynamic_index_in_dim(mine, at, 0, False)
        return one + lax.dynamic_index_in_dim(got, at, 0, False)

    got_y = lax.ppermute(narrow(summed(1 - y)), "dp", OVER_Y)
    kept = summed(y) + widen(got_y)

    def message(s):
        a = kept[s % 4, (s // 4) * MSG : (s // 4) * MSG + RA]
        return jnp.concatenate([a, kept[s % 4, RA:MSG]], axis=0)

    arrived = [lax.ppermute(narrow(message(s)), "dp", along_z(s)) for s in range(1, 8)]
    total = message(0) + sum(widen(x) for x in arrived)
    packed = inverse_roots(total, z)

    pair = jnp.stack([packed, lax.ppermute(packed, "dp", OVER_CORE)])
    near = [lax.ppermute(pair, "dp", along_z(s, True)) for s in range(1, 4)]
    far = lax.ppermute(packed, "dp", along_z(4))
    held = jnp.concatenate([packed[None], *near, far[None]])
    others = lax.ppermute(jnp.stack([x[1, TAIL:] for x in near]), "dp", OVER_CORE)
    tails = [packed[TAIL:]] + [x[0, TAIL:] for x in near] + [far[TAIL:]]
    tails = jnp.stack(tails + [others[2], others[1], others[0]])
    rights = lax.ppermute(tails, ("dp", "grp"), EXCHANGE)
    lefts = jnp.stack([held, lax.ppermute(held, "dp", OVER_Y)])
    lefts = jnp.stack([lefts, lax.ppermute(lefts, "dp", OVER_CORE)])

    at = jnp.stack(
        [z, y, core, column]
        + owned_blocks(owner_a, position)
        + owned_blocks(gradient_block_owner, position)
    ).astype(jnp.int32)
    precond_grad, store_a, store_g = apply_roots(at, weight_grad, lefts, rights)
    return precond_grad, store_a[None, None], store_g[None, None]


def solution(mesh):
    return jax.shard_map(
        shards,
        mesh=mesh,
        in_specs=(
            P(None, "dp", "grp"),
            P(None, "dp", "grp"),
            P(None, "grp", "dp"),
            P(None, "grp"),
            P(None, "grp"),
        ),
        out_specs=(
            P(None, "grp", "dp"),
            P("grp", "dp", None, None, None),
            P("grp", "dp", None, None, None),
        ),
        check_vma=False,
    )
```

time: 542 us -> 102 us (0.19)
  waiting for transfers between devices: 413 us -> 36 us
  matrix products: 57.5 us -> 0 us
  local copies, waits for them, and re-layouts: 42 us -> 5.7 us
  starting transfers between devices: 0.39 us -> 33.9 us
  Pallas kernels: 0 us -> 20.2 us
  between operations: 14 us -> 0.88 us
  other arithmetic: 11.4 us -> 4.74 us
    reduce_scatter x2 -> x0, waiting for transfers between devices: 257 us -> none  [the longest x1 135 us: shards(): summed_a = lax.psum_scatter(routed_a, 'dp', scatter_dimension=0, tiled=True)]
    all_gather x2 -> x0, waiting for transfers between devices: 94.6 us -> none  [the longest x1 64.4 us: shards(): all_a = lax.all_gather(kept_a, 'dp', axis=0, tiled=True)]
    psum x1 -> x0, waiting for transfers between devices: 60.9 us -> none  [spread(): return lax.psum(kept, axis)]
    dot_general x78 -> x0, matrix products: 57.5 us -> none  [the longest x24 15.3 us: sweep(): jnp.einsum('nij,njk->nik', left_y, poly, precision=lax.Precision.HIGHEST)]
    ppermute x0 -> x18, waiting for transfers between devices: none -> 36 us  [the longest x1 11.7 us: shards(): rights = lax.ppermute(tails, ('dp', 'grp'), EXCHANGE)]
    ppermute x0 -> x18, starting transfers between devices: none -> 33.9 us  [the longest x7 17.5 us: shards(): lax.ppermute(narrow(message(s)), 'dp', along_z(s))]
    pallas_call x0 -> x4, Pallas kernels: none -> 20.2 us  [the longest x1 8.35 us: inverse_roots(): pl.pallas_call(roots_kernel, in_specs=[pl.BlockSpec(memory_space=pltpu.SM...]
    scatter x2 -> x0, local copies, waits for them, and re-layouts: 16.1 us -> none  [dispatch_blocks(): return empty.at[slot_indices].set(blocks)]
  transfers between devices with their start and end apart: 5 -> 18, of which waited for: 5 -> 8; matrix products, arithmetic and copies ran while one was open for 14% -> 5% of each run, Pallas kernels for 0% -> 4%
where the time goes in v1:
time: 102 us; the launch traced here: 101 us
  waiting for transfers between devices  36 us (35%)
  starting transfers between devices  33.9 us (33%)
  Pallas kernels  20.2 us (20%)
  local copies, waits for them, and re-layouts  5.7 us (6%)
  other arithmetic  4.74 us (5%)
    ppermute x7, starting transfers between devices, shards(): lax.ppermute(narrow(message(s)), 'dp', along_z(s))  17.5 us
    ppermute x1, waiting for transfers between devices, shards(): rights = lax.ppermute(tails, ('dp', 'grp'), EXCHANGE)  11.7 us
    ppermute x1, waiting for transfers between devices, shards(): got_y = lax.ppermute(narrow(summed(1 - y)), 'dp', OVER_Y)  8.95 us
    pallas_call x1, Pallas kernels, inverse_roots(): pl.pallas_call(roots_kernel, in_specs=[pl.BlockSpec(memory_space=pltpu.SM...  8.35 us
    pallas_call x2, Pallas kernels, covariances(): pl.pallas_call(functools.partial(cov_kernel, scale), grid_spec=pltpu.Pref...  8.26 us
    ppermute x1, waiting for transfers between devices, shards(): lefts = jnp.stack([held, lax.ppermute(held, 'dp', OVER_Y)])  7.18 us
    ppermute x1, starting transfers between devices, shards(): rights = lax.ppermute(tails, ('dp', 'grp'), EXCHANGE)  6.36 us
    ppermute x3, waiting for transfers between devices, shards(): near = [lax.ppermute(pair, 'dp', along_z(s, True)) for s in range(1, 4)]  5.63 us
  transfers between devices with their start and end apart: 18, of which 8 were waited for; matrix products, arithmetic and copies ran while one was open for 5% of the time, Pallas kernels for 4%

profile of v1, /device:TPU:30, one launch (start us, length us, event | category | flops | bytes accessed | tf_op | source)
XLA Modules:
  0.0 101.5 jit_solution(16300226762779390989)
XLA Ops:
  0.7 1.6 %copy-done = bf16[4,512,512]{2,1,0:T(8,128)(2,1)S(1)} copy-done((bf16[4,512,512]{2,1,0:T(8,128)(2,1)S(1)}, bf16[4,512,512]{2,1,0:T(8,128)(2,1)}, u32[]{:S(2)}) %copy-start) | copy-done | bytes 2097176
  2.3 4.6 %covariances.3 = f32[2,4,352,128]{3,2,1,0:T(8,128)} custom-call(s32[2]{0:T(128)S(1)} %pad_add_fusion.1.sel_ref, bf16[4,1376,512]{2,1,0:T(8,128)(2,1)} %bitcast.60, bf16[4,512,512]{2,1,0:T(8,128)(2,1)S(1)} %copy-done), custom_call_target="tpu_custom_call" | custom-call | flops 2000000000 | bytes 6000000 | tf_op jit(solution)/shard_map/covariances/pallas_call | solution.py:102
  7.4 3.7 %covariances.2 = f32[2,4,352,128]{3,2,1,0:T(8,128)S(1)} custom-call(s32[2]{0:T(128)S(1)} %pad_add_fusion.sel_ref, bf16[4,1376,512]{2,1,0:T(8,128)(2,1)} %bitcast.61, bf16[4,512,512]{2,1,0:T(8,128)(2,1)S(1)} %copy-done.1), custom_call_target="tpu_custom_call" | custom-call | flops 2000000000 | bytes 6000000 | tf_op jit(solution)/shard_map/covariances/pallas_call | solution.py:102
  11.1 1.2 %fusion = f16[4,352,128]{2,1,0:T(8,128)(2,1)S(1)} fusion(f32[2,4,352,128]{3,2,1,0:T(8,128)} %collective-permute-done, s32[]{:T(128)S(6)} %select_n.42, f32[2,4,352,128]{3,2,1,0:T(8,128)S(1)} %covariances.2), kind=kLoop, calls=%fused_computation.4 | loop fusion | flops 540672 | bytes 1802244 | tf_op jit(solution)/shard_map/convert_element_type | solution.py:276
  14.3 9.0 %collective-permute-done.1 = f16[4,352,128]{2,1,0:T(8,128)(2,1)S(1)} collective-permute-done((f16[4,352,128]{2,1,0:T(8,128)(2,1)S(1)}, f16[4,352,128]{2,1,0:T(8,128)(2,1)S(1)}, u32[]{:S(2)}, u32[]{:S(2)}) %collective-permute-start.1) | collective-permute-done | bytes 360480 | tf_op jit(solution)/shard_map/ppermute | solution.py:298
  23.3 1.2 %bitcast_add_fusion = f32[4,352,128]{2,1,0:T(8,128)S(1)} fusion(f16[4,352,128]{2,1,0:T(8,128)(2,1)S(1)} %collective-permute-done.1, f32[2,4,352,128]{3,2,1,0:T(8,128)} %collective-permute-done, s32[]{:T(128)S(6)} %select_n.41, f32[2,4,352,128]{3,2,1,0:T(8,128)S(1)} %covariances.2), kind=kLoop, calls=%fused_computation.2 | loop fusion | flops 720896 | bytes 2523140 | tf_op jit(solution)/shard_map/add | solution.py:299
  24.6 5.9 %collective-permute-start.8 = (f16[208,128]{1,0:T(8,128)(2,1)S(1)}, f16[208,128]{1,0:T(8,128)(2,1)S(1)}, u32[]{:S(2)}, u32[]{:S(2)}) collective-permute-start(f16[208,128]{1,0:T(8,128)(2,1)S(1)} %get-tuple-element.52), channel_id=1, source_target_pairs={{0,224},{8,232},{16,240},{24,248},{32,0},{40,8},{48,16},{56,24},{6... | collective-permute-start | bytes 159752 | tf_op jit(solution)/shard_map/ppermute | solution.py:305
  30.5 1.5 %collective-permute-start.7 = (f16[208,128]{1,0:T(8,128)(2,1)S(1)}, f16[208,128]{1,0:T(8,128)(2,1)S(1)}, u32[]{:S(2)}, u32[]{:S(2)}) collective-permute-start(f16[208,128]{1,0:T(8,128)(2,1)S(1)} %get-tuple-element.50), channel_id=1, source_target_pairs={{0,192},{8,200},{16,208},{24,216},{32,224},{40,232},{48,240},{56,2... | collective-permute-start | bytes 159752 | tf_op jit(solution)/shard_map/ppermute | solution.py:305
  32.7 5.1 %collective-permute-start.5 = (f16[208,128]{1,0:T(8,128)(2,1)S(1)}, f16[208,128]{1,0:T(8,128)(2,1)S(1)}, u32[]{:S(2)}, u32[]{:S(2)}) collective-permute-start(f16[208,128]{1,0:T(8,128)(2,1)S(1)} %fusion.15), channel_id=1, source_target_pairs={{0,128},{8,136},{16,144},{24,152},{32,160},{40,168},{48,176},{56,1... | collective-permute-start | bytes 159752 | tf_op jit(solution)/shard_map/ppermute | solution.py:305
  37.8 2.5 %collective-permute-start.3 = (f16[208,128]{1,0:T(8,128)(2,1)S(1)}, f16[208,128]{1,0:T(8,128)(2,1)S(1)}, u32[]{:S(2)}, u32[]{:S(2)}) collective-permute-start(f16[208,128]{1,0:T(8,128)(2,1)S(1)} %get-tuple-element.49), channel_id=1, source_target_pairs={{0,64},{8,72},{16,80},{24,88},{32,96},{40,104},{48,112},{56,120},{... | collective-permute-start | bytes 159752 | tf_op jit(solution)/shard_map/ppermute | solution.py:305
  40.2 1.9 %collective-permute-start.2 = (f16[208,128]{1,0:T(8,128)(2,1)S(1)}, f16[208,128]{1,0:T(8,128)(2,1)S(1)}, u32[]{:S(2)}, u32[]{:S(2)}) collective-permute-start(f16[208,128]{1,0:T(8,128)(2,1)S(1)} %get-tuple-element.47), channel_id=1, source_target_pairs={{0,32},{8,40},{16,48},{24,56},{32,64},{40,72},{48,80},{56,88},{64,... | collective-permute-start | bytes 159752 | tf_op jit(solution)/shard_map/ppermute | solution.py:305
  42.9 2.6 %stack.84.at_ref = s32[8]{0:T(128)S(1)} concatenate(s32[1]{0:T(128)} %bitcast.z_ref, s32[1]{0:T(128)} %bitcast.1, s32[1]{0:T(128)} %bitcast.2, s32[1]{0:T(128)} %bitcast.3, s32[1]{0:T(128)} %bitcast.4, s32[1]{0:T(128)} %bitcast.5, s32[1]{0:T(128)} %bitcast.6, s32[1]{0:T(128)} %bitcast.7), dimensions={0} | concatenate | bytes 64 | tf_op jit(solution)/shard_map/stack | solution.py:320
  46.1 1.9 %collective-permute-done.3 = f16[208,128]{1,0:T(8,128)(2,1)S(1)} collective-permute-done((f16[208,128]{1,0:T(8,128)(2,1)S(1)}, f16[208,128]{1,0:T(8,128)(2,1)S(1)}, u32[]{:S(2)}, u32[]{:S(2)}) %collective-permute-start.3) | collective-permute-done | bytes 53280 | tf_op jit(solution)/shard_map/ppermute | solution.py:305
  48.0 8.3 %inverse_roots.1 = bf16[176,128]{1,0:T(8,128)(2,1)S(1)} custom-call(s32[1]{0:T(128)} %bitcast.z_ref, f32[208,128]{1,0:T(8,128)S(1)} %fusion.13.total_ref), custom_call_target="tpu_custom_call" | custom-call | tf_op jit(solution)/shard_map/inverse_roots/pallas_call | solution.py:173
  56.5 3.6 %collective-permute-start.13 = (bf16[176,128]{1,0:T(8,128)(2,1)S(1)}, bf16[176,128]{1,0:T(8,128)(2,1)S(1)}, u32[]{:S(2)}, u32[]{:S(2)}) collective-permute-start(bf16[176,128]{1,0:T(8,128)(2,1)S(1)} %inverse_roots.1), channel_id=1, source_target_pairs={{0,128},{8,136},{16,144},{24,152},{32,160},{40,168},{48,176},{56,1... | collective-permute-start | bytes 135176 | tf_op jit(solution)/shard_map/ppermute | solution.py:311
  61.0 1.0 %collective-permute-start.11 = (bf16[2,176,128]{2,1,0:T(8,128)(2,1)S(1)}, bf16[2,176,128]{2,1,0:T(8,128)(2,1)S(1)}, u32[]{:S(2)}, u32[]{:S(2)}) collective-permute-start(bf16[2,176,128]{2,1,0:T(8,128)(2,1)S(1)} %pad_maximum_fusion.10), channel_id=1, source_target_pairs={{0,64},{8,200},{16,80},{24,216},{32,96},{40,232},{48,112},{56,248}... | collective-permute-start | bytes 270344 | tf_op jit(solution)/shard_map/ppermute | solution.py:310
  62.0 2.7 %collective-permute-start.12 = (bf16[2,176,128]{2,1,0:T(8,128)(2,1)S(1)}, bf16[2,176,128]{2,1,0:T(8,128)(2,1)S(1)}, u32[]{:S(2)}, u32[]{:S(2)}) collective-permute-start(bf16[2,176,128]{2,1,0:T(8,128)(2,1)S(1)} %pad_maximum_fusion.10), channel_id=1, source_target_pairs={{0,96},{8,168},{16,112},{24,184},{32,128},{40,200},{48,144},{56,21... | collective-permute-start | bytes 270344 | tf_op jit(solution)/shard_map/ppermute | solution.py:310
  64.7 1.5 %collective-permute-done.10 = bf16[2,176,128]{2,1,0:T(8,128)(2,1)S(1)} collective-permute-done((bf16[2,176,128]{2,1,0:T(8,128)(2,1)S(1)}, bf16[2,176,128]{2,1,0:T(8,128)(2,1)S(1)}, u32[]{:S(2)}, u32[]{:S(2)}) %collective-permute-start.10) | collective-permute-done | bytes 90144 | tf_op jit(solution)/shard_map/ppermute | solution.py:310
  66.2 1.6 %collective-permute-done.11 = bf16[2,176,128]{2,1,0:T(8,128)(2,1)S(1)} collective-permute-done((bf16[2,176,128]{2,1,0:T(8,128)(2,1)S(1)}, bf16[2,176,128]{2,1,0:T(8,128)(2,1)S(1)}, u32[]{:S(2)}, u32[]{:S(2)}) %collective-permute-start.11) | collective-permute-done | bytes 90144 | tf_op jit(solution)/shard_map/ppermute | solution.py:310
  67.7 2.6 %collective-permute-done.12 = bf16[2,176,128]{2,1,0:T(8,128)(2,1)S(1)} collective-permute-done((bf16[2,176,128]{2,1,0:T(8,128)(2,1)S(1)}, bf16[2,176,128]{2,1,0:T(8,128)(2,1)S(1)}, u32[]{:S(2)}, u32[]{:S(2)}) %collective-permute-start.12) | collective-permute-done | bytes 90144 | tf_op jit(solution)/shard_map/ppermute | solution.py:310
  71.3 7.2 %collective-permute-done.14 = bf16[8,176,128]{2,1,0:T(8,128)(2,1)S(1)} collective-permute-done((bf16[8,176,128]{2,1,0:T(8,128)(2,1)S(1)}, bf16[8,176,128]{2,1,0:T(8,128)(2,1)S(1)}, u32[]{:S(2)}, u32[]{:S(2)}) %collective-permute-start.14) | collective-permute-done | bytes 360480 | tf_op jit(solution)/shard_map/ppermute | solution.py:317
  78.8 6.4 %collective-permute-start.17 = (bf16[8,48,128]{2,1,0:T(8,128)(2,1)S(1)}, bf16[8,48,128]{2,1,0:T(8,128)(2,1)S(1)}, u32[]{:S(2)}, u32[]{:S(2)}) collective-permute-start(bf16[8,48,128]{2,1,0:T(8,128)(2,1)S(1)} %constant_dynamic-update-slice_fusion.4), channel_id=1, source_target_pairs={{0,0},{1,32},{2,64},{3,96},{4,128},{5,160},{6,192},{7,224},{8,8},{... | collective-permute-start | bytes 294920 | tf_op jit(solution)/shard_map/ppermute | solution.py:316
  85.3 11.7 %collective-permute-done.17.rights_ref = bf16[8,48,128]{2,1,0:T(8,128)(2,1)S(1)} collective-permute-done((bf16[8,48,128]{2,1,0:T(8,128)(2,1)S(1)}, bf16[8,48,128]{2,1,0:T(8,128)(2,1)S(1)}, u32[]{:S(2)}, u32[]{:S(2)}) %collective-permute-start.17) | collective-permute-done | bytes 98336 | tf_op jit(solution)/shard_map/ppermute | solution.py:316
  97.1 3.6 %apply_roots.1 = (bf16[4,1376,128]{2,1,0:T(8,128)(2,1)}, bf16[2,172,172]{2,1,0:T(8,128)(2,1)S(1)}, bf16[2,128,128]{2,1,0:T(8,128)(2,1)}) custom-call(s32[8]{0:T(128)S(1)} %stack.84.at_ref, bf16[4,1376,128]{2,1,0:T(8,128)(2,1)S(1)} %copy-done.2, bf16[2,2,8,176,128]{4,3,2,1,0:T(8,128)(2,1)S(1)} %pad_maximum_fusion.a_ref, ...), custom_call_target="tpu_custom_call" | custom-call | tf_op jit(solution)/shard_map/apply_roots/pallas_call | solution.py:238
  (70 shorter events, 7.7 us)
Async XLA Ops:
  0.7 1.6 %copy-start = (bf16[4,512,512]{2,1,0:T(8,128)(2,1)S(1)}, bf16[4,512,512]{2,1,0:T(8,128)(2,1)}, u32[]{:S(2)}) copy-start(bf16[4,512,512]{2,1,0:T(8,128)(2,1)} %g_ref.3) | copy-start | bytes 6291460
  2.3 4.6 %copy-start.3 = (s32[4,8]{1,0:T(4,128)S(1)}, s32[4,8]{1,0:T(4,128)}, u32[]{:S(2)}) copy-start(s32[4,8]{1,0:T(4,128)} %param.8) | copy-start | bytes 388
  2.3 5.1 %copy-start.1 = (bf16[4,512,512]{2,1,0:T(8,128)(2,1)S(1)}, bf16[4,512,512]{2,1,0:T(8,128)(2,1)}, u32[]{:S(2)}) copy-start(bf16[4,512,512]{2,1,0:T(8,128)(2,1)} %g_ref.3) | copy-start | bytes 6291460
  6.9 4.2 %collective-permute-start = (f32[2,4,352,128]{3,2,1,0:T(8,128)}, f32[2,4,352,128]{3,2,1,0:T(8,128)}, u32[]{:S(2)}, u32[]{:S(2)}) collective-permute-start(f32[2,4,352,128]{3,2,1,0:T(8,128)} %covariances.3), channel_id=1, source_target_pairs={{0,8},{8,0},{16,24},{24,16},{32,40},{40,32},{48,56},{56,48},{64,72... | collective-permute-start | bytes 4325384 | tf_op jit(solution)/shard_map/ppermute | solution.py:291
  11.1 2.1 %copy-start.4 = (s32[4,4]{1,0:T(4,128)S(1)}, s32[4,4]{1,0:T(4,128)}, u32[]{:S(2)}) copy-start(s32[4,4]{1,0:T(4,128)} %param.9) | copy-start | bytes 196
  12.3 10.9 %collective-permute-start.1 = (f16[4,352,128]{2,1,0:T(8,128)(2,1)S(1)}, f16[4,352,128]{2,1,0:T(8,128)(2,1)S(1)}, u32[]{:S(2)}, u32[]{:S(2)}) collective-permute-start(f16[4,352,128]{2,1,0:T(8,128)(2,1)S(1)} %fusion), channel_id=1, source_target_pairs={{0,16},{8,24},{16,0},{24,8},{32,48},{40,56},{48,32},{56,40},{64,80... | collective-permute-start | bytes 1081352 | tf_op jit(solution)/shard_map/ppermute | solution.py:298
  24.6 13.2 %collective-permute-start.8 = (f16[208,128]{1,0:T(8,128)(2,1)S(1)}, f16[208,128]{1,0:T(8,128)(2,1)S(1)}, u32[]{:S(2)}, u32[]{:S(2)}) collective-permute-start(f16[208,128]{1,0:T(8,128)(2,1)S(1)} %get-tuple-element.52), channel_id=1, source_target_pairs={{0,224},{8,232},{16,240},{24,248},{32,0},{40,8},{48,16},{56,24},{6... | collective-permute-start | bytes 159752 | tf_op jit(solution)/shard_map/ppermute | solution.py:305
  30.5 9.7 %collective-permute-start.7 = (f16[208,128]{1,0:T(8,128)(2,1)S(1)}, f16[208,128]{1,0:T(8,128)(2,1)S(1)}, u32[]{:S(2)}, u32[]{:S(2)}) collective-permute-start(f16[208,128]{1,0:T(8,128)(2,1)S(1)} %get-tuple-element.50), channel_id=1, source_target_pairs={{0,192},{8,200},{16,208},{24,216},{32,224},{40,232},{48,240},{56,2... | collective-permute-start | bytes 159752 | tf_op jit(solution)/shard_map/ppermute | solution.py:305
  32.1 13.4 %collective-permute-start.6 = (f16[208,128]{1,0:T(8,128)(2,1)S(1)}, f16[208,128]{1,0:T(8,128)(2,1)S(1)}, u32[]{:S(2)}, u32[]{:S(2)}) collective-permute-start(f16[208,128]{1,0:T(8,128)(2,1)S(1)} %get-tuple-element.48), channel_id=1, source_target_pairs={{0,160},{8,168},{16,176},{24,184},{32,192},{40,200},{48,208},{56,2... | collective-permute-start | bytes 159752 | tf_op jit(solution)/shard_map/ppermute | solution.py:305
  32.7 12.8 %collective-permute-start.5 = (f16[208,128]{1,0:T(8,128)(2,1)S(1)}, f16[208,128]{1,0:T(8,128)(2,1)S(1)}, u32[]{:S(2)}, u32[]{:S(2)}) collective-permute-start(f16[208,128]{1,0:T(8,128)(2,1)S(1)} %fusion.15), channel_id=1, source_target_pairs={{0,128},{8,136},{16,144},{24,152},{32,160},{40,168},{48,176},{56,1... | collective-permute-start | bytes 159752 | tf_op jit(solution)/shard_map/ppermute | solution.py:305
  37.8 8.3 %collective-permute-start.4 = (f16[208,128]{1,0:T(8,128)(2,1)S(1)}, f16[208,128]{1,0:T(8,128)(2,1)S(1)}, u32[]{:S(2)}, u32[]{:S(2)}) collective-permute-start(f16[208,128]{1,0:T(8,128)(2,1)S(1)} %get-tuple-element.51), channel_id=1, source_target_pairs={{0,96},{8,104},{16,112},{24,120},{32,128},{40,136},{48,144},{56,15... | collective-permute-start | bytes 159752 | tf_op jit(solution)/shard_map/ppermute | solution.py:305
  37.8 10.2 %collective-permute-start.3 = (f16[208,128]{1,0:T(8,128)(2,1)S(1)}, f16[208,128]{1,0:T(8,128)(2,1)S(1)}, u32[]{:S(2)}, u32[]{:S(2)}) collective-permute-start(f16[208,128]{1,0:T(8,128)(2,1)S(1)} %get-tuple-element.49), channel_id=1, source_target_pairs={{0,64},{8,72},{16,80},{24,88},{32,96},{40,104},{48,112},{56,120},{... | collective-permute-start | bytes 159752 | tf_op jit(solution)/shard_map/ppermute | solution.py:305
  40.2 7.7 %collective-permute-start.2 = (f16[208,128]{1,0:T(8,128)(2,1)S(1)}, f16[208,128]{1,0:T(8,128)(2,1)S(1)}, u32[]{:S(2)}, u32[]{:S(2)}) collective-permute-start(f16[208,128]{1,0:T(8,128)(2,1)S(1)} %get-tuple-element.47), channel_id=1, source_target_pairs={{0,32},{8,40},{16,48},{24,56},{32,64},{40,72},{48,80},{56,88},{64,... | collective-permute-start | bytes 159752 | tf_op jit(solution)/shard_map/ppermute | solution.py:305
  56.4 3.7 %collective-permute-start.9 = (bf16[176,128]{1,0:T(8,128)(2,1)S(1)}, bf16[176,128]{1,0:T(8,128)(2,1)S(1)}, u32[]{:S(2)}, u32[]{:S(2)}) collective-permute-start(bf16[176,128]{1,0:T(8,128)(2,1)S(1)} %inverse_roots.1), channel_id=1, source_target_pairs={{0,8},{8,0},{16,24},{24,16},{32,40},{40,32},{48,56},{56,48},{64,72... | collective-permute-start | bytes 135176 | tf_op jit(solution)/shard_map/ppermute | solution.py:309
  56.5 13.8 %collective-permute-start.13 = (bf16[176,128]{1,0:T(8,128)(2,1)S(1)}, bf16[176,128]{1,0:T(8,128)(2,1)S(1)}, u32[]{:S(2)}, u32[]{:S(2)}) collective-permute-start(bf16[176,128]{1,0:T(8,128)(2,1)S(1)} %inverse_roots.1), channel_id=1, source_target_pairs={{0,128},{8,136},{16,144},{24,152},{32,160},{40,168},{48,176},{56,1... | collective-permute-start | bytes 135176 | tf_op jit(solution)/shard_map/ppermute | solution.py:311
  60.1 6.0 %collective-permute-start.10 = (bf16[2,176,128]{2,1,0:T(8,128)(2,1)S(1)}, bf16[2,176,128]{2,1,0:T(8,128)(2,1)S(1)}, u32[]{:S(2)}, u32[]{:S(2)}) collective-permute-start(bf16[2,176,128]{2,1,0:T(8,128)(2,1)S(1)} %pad_maximum_fusion.10), channel_id=1, source_target_pairs={{0,32},{8,232},{16,48},{24,248},{32,64},{40,8},{48,80},{56,24},{64... | collective-permute-start | bytes 270344 | tf_op jit(solution)/shard_map/ppermute | solution.py:310
  61.0 6.7 %collective-permute-start.11 = (bf16[2,176,128]{2,1,0:T(8,128)(2,1)S(1)}, bf16[2,176,128]{2,1,0:T(8,128)(2,1)S(1)}, u32[]{:S(2)}, u32[]{:S(2)}) collective-permute-start(bf16[2,176,128]{2,1,0:T(8,128)(2,1)S(1)} %pad_maximum_fusion.10), channel_id=1, source_target_pairs={{0,64},{8,200},{16,80},{24,216},{32,96},{40,232},{48,112},{56,248}... | collective-permute-start | bytes 270344 | tf_op jit(solution)/shard_map/ppermute | solution.py:310
  62.0 8.3 %collective-permute-start.12 = (bf16[2,176,128]{2,1,0:T(8,128)(2,1)S(1)}, bf16[2,176,128]{2,1,0:T(8,128)(2,1)S(1)}, u32[]{:S(2)}, u32[]{:S(2)}) collective-permute-start(bf16[2,176,128]{2,1,0:T(8,128)(2,1)S(1)} %pad_maximum_fusion.10), channel_id=1, source_target_pairs={{0,96},{8,168},{16,112},{24,184},{32,128},{40,200},{48,144},{56,21... | collective-permute-start | bytes 270344 | tf_op jit(solution)/shard_map/ppermute | solution.py:310
  70.4 8.2 %collective-permute-start.14 = (bf16[8,176,128]{2,1,0:T(8,128)(2,1)S(1)}, bf16[8,176,128]{2,1,0:T(8,128)(2,1)S(1)}, u32[]{:S(2)}, u32[]{:S(2)}) collective-permute-start(bf16[8,176,128]{2,1,0:T(8,128)(2,1)S(1)} %bitcast_dynamic-update-slice_fusion), channel_id=1, source_target_pairs={{0,16},{8,24},{16,0},{24,8},{32,48},{40,56},{48,32},{56,40},{64,80... | collective-permute-start | bytes 1081352 | tf_op jit(solution)/shard_map/ppermute | solution.py:317
  71.2 7.5 %collective-permute-start.16 = (bf16[3,48,128]{2,1,0:T(8,128)(2,1)S(1)}, bf16[3,48,128]{2,1,0:T(8,128)(2,1)S(1)}, u32[]{:S(2)}, u32[]{:S(2)}) collective-permute-start(bf16[3,48,128]{2,1,0:T(8,128)(2,1)S(1)} %pad_maximum_fusion.11), channel_id=1, source_target_pairs={{0,8},{8,0},{16,24},{24,16},{32,40},{40,32},{48,56},{56,48},{64,72... | collective-permute-start | bytes 110600 | tf_op jit(solution)/shard_map/ppermute | solution.py:313
  78.6 6.5 %collective-permute-start.15 = (bf16[2,8,176,128]{3,2,1,0:T(8,128)(2,1)S(1)}, bf16[2,8,176,128]{3,2,1,0:T(8,128)(2,1)S(1)}, u32[]{:S(2)}, u32[]{:S(2)}) collective-permute-start(bf16[2,8,176,128]{3,2,1,0:T(8,128)(2,1)S(1)} %get-tuple-element.28), channel_id=1, source_target_pairs={{0,8},{8,0},{16,24},{24,16},{32,40},{40,32},{48,56},{56,48},{64,72... | collective-permute-start | bytes 2162696 | tf_op jit(solution)/shard_map/ppermute | solution.py:318
  78.8 18.3 %collective-permute-start.17 = (bf16[8,48,128]{2,1,0:T(8,128)(2,1)S(1)}, bf16[8,48,128]{2,1,0:T(8,128)(2,1)S(1)}, u32[]{:S(2)}, u32[]{:S(2)}) collective-permute-start(bf16[8,48,128]{2,1,0:T(8,128)(2,1)S(1)} %constant_dynamic-update-slice_fusion.4), channel_id=1, source_target_pairs={{0,0},{1,32},{2,64},{3,96},{4,128},{5,160},{6,192},{7,224},{8,8},{... | collective-permute-start | bytes 294920 | tf_op jit(solution)/shard_map/ppermute | solution.py:316
  85.2 11.9 %copy-start.2 = (bf16[4,1376,128]{2,1,0:T(8,128)(2,1)S(1)}, bf16[4,1376,128]{2,1,0:T(8,128)(2,1)}, u32[]{:S(2)}) copy-start(bf16[4,1376,128]{2,1,0:T(8,128)(2,1)} %w_ref.1) | copy-start | bytes 4227076

commit v2 on v1

v2 whole, which is shorter than its diff:
```python
import functools

import jax
import jax.numpy as jnp
from jax import lax
from jax.experimental import pallas as pl
from jax.experimental.pallas import tpu as pltpu
from jax.sharding import PartitionSpec as P

ITERS = 12
BA = 172
BG = 128
LAYERS = 4
HALF = 64
NARROW = BA - BG
RA = 144
RG = 64
MSG = RA + RG
PAIR = RA + RG + RA
DIAG = 136
GATHERED = RA + RG // 2
TAILS = 144
WIRE = jnp.float16
WIRE_SCALE = 256.0

damping_share = 0.01

CHEAP = pl.CostEstimate(flops=10**4, bytes_accessed=10**4, transcendentals=0)
PARAMS = pltpu.CompilerParams(vmem_limit_bytes=48 << 20)


def iota(shape, dim):
    return lax.broadcasted_iota(jnp.int32, shape, dim)


def pack_square(top, bottom):
    row, lane = iota((HALF, BG), 0), iota((HALF, BG), 1)
    turned = pltpu.roll(bottom, HALF, 1)
    folded = jnp.where((lane < HALF) & (row >= lane), turned, top)
    diagonal = jnp.sum(jnp.where(row == lane, top, 0.0), axis=0, keepdims=True)
    return folded, diagonal


def unpack_square(folded, diagonal):
    row, lane = iota((HALF, BG), 0), iota((HALF, BG), 1)
    top = jnp.where(lane > row, folded, jnp.where(lane == row, 0.5 * diagonal, 0.0))
    left = jnp.where(lane < row, folded, jnp.where(lane == row, 0.5 * folded, 0.0))
    bottom = pltpu.roll(left, HALF, 1)
    once = jnp.concatenate([top, bottom], axis=0)
    return once + once.T


def pack_wide(full, spare):
    folded, diagonal = pack_square(full[0:HALF, 0:BG], full[HALF:BG, 0:BG])
    low = full[BG : BG + 48, 0:BG]
    corner = full[BG : BG + 48, BG:256]
    corner = corner[0:24] + pltpu.roll(corner[24:48], HALF, 1)
    both = diagonal + pltpu.roll(spare, HALF, 1)
    last = jnp.where(iota((8, BG), 0) == 0, both, 0.0)
    return folded, low, jnp.concatenate([corner, last], axis=0)


def unpack_wide(packed):
    square = unpack_square(packed[0:HALF], packed[DIAG : DIAG + 1])
    low = packed[HALF : HALF + 48]
    tall = jnp.concatenate([low, jnp.zeros((80, BG), jnp.float32)], axis=0).T
    corner = packed[112:136]
    lane, row = iota((24, BG), 1), iota((24, BG), 0)
    first = jnp.where(lane < NARROW, corner, 0.0)
    second = jnp.where((lane < NARROW) & (row < NARROW - 24), pltpu.roll(corner, HALF, 1), 0.0)
    corner = jnp.concatenate([first, second], axis=0)
    return jnp.concatenate(
        [jnp.concatenate([square, tall], axis=1), jnp.concatenate([low, corner], axis=1)], axis=0
    )


def cov_kernel(scale, at_ref, h_ref, g_ref, o_ref, wide):
    z = at_ref[1]
    spares = []
    for layer in range(LAYERS):
        x = g_ref[layer]
        c = lax.dot_general(x, x, (((0,), (0,)), ((), ())), preferred_element_type=jnp.float32)
        folded, spare = pack_square(c[0:HALF] * scale, c[HALF:BG] * scale)
        spares.append(spare)
        turn = lax.rem(layer // 2 - z // 2 + 4, 2)
        o_ref[0, lax.rem(layer - z + 8, 2), turn, RA : RA + RG] = folded
    for k in range(8):
        x = h_ref[0, BA * k : BA * (k + 1), :]
        c = lax.dot_general(x, x, (((1,), (1,)), ((), ())), preferred_element_type=jnp.float32)
        wide[k, BG:176] = jnp.zeros((48, 256), jnp.float32)
        wide[k, 0:BA, 0:BA] = c * scale
    for k in range(8):
        turn = lax.rem(k // 2 - z // 2 + 4, 4)
        odd, place = lax.rem(k - z + 8, 2), lax.rem(turn, 2)
        base = pl.multiple_of((turn // 2) * MSG, 16)
        folded, low, corner = pack_wide(wide.at[k], spares[k % 4])
        o_ref[0, odd, place, pl.ds(base, HALF)] = folded
        o_ref[0, odd, place, pl.ds(base + HALF, 48)] = low
        o_ref[0, odd, place, pl.ds(base + 112, 32)] = corner


def covariances(turned, grads, core, z, scale):
    rows, features = turned.shape[2], turned.shape[1]
    shape = (2, 2, 2, PAIR, BG)
    return pl.pallas_call(
        functools.partial(cov_kernel, scale),
        grid_spec=pltpu.PrefetchScalarGridSpec(
            num_scalar_prefetch=1,
            grid=(2,),
            in_specs=[
                pl.BlockSpec((1, features, rows), lambda i, s: (2 * s[0] + i, 0, 0)),
                pl.BlockSpec((LAYERS, rows, BG), lambda i, s: (0, 0, 2 * i + s[0])),
            ],
            out_specs=pl.BlockSpec((1,) + shape[1:], lambda i, s: (i, 0, 0, 0, 0)),
            scratch_shapes=[pltpu.VMEM((8, 176, 256), jnp.float32)],
        ),
        out_shape=jax.ShapeDtypeStruct(shape, jnp.float32),
        compiler_params=PARAMS,
        cost_estimate=CHEAP,
        name="covariances",
    )(jnp.stack([core, z]), turned, grads)


def parts_of(x):
    high = x.astype(jnp.bfloat16)
    return high, (x - high.astype(jnp.float32)).astype(jnp.bfloat16)


def times(a, b):
    def one(i, j):
        return jnp.dot(a[i], b[j], preferred_element_type=jnp.float32)

    return (one(0, 1) + one(1, 0)) + one(0, 0)


def roots_kernel(z_ref, total_ref, packed_ref, wide, square):
    total = total_ref[...]
    spare = pltpu.roll(total[DIAG : DIAG + 1], HALF, 1)
    blocks = [unpack_wide(total[0:RA])[0:BA, 0:BA], unpack_square(total[RA:MSG], spare)]
    eyes, ys, totals = [], [], []
    for c in blocks:
        width = c.shape[0]
        eye = (iota(c.shape, 0) == iota(c.shape, 1)).astype(jnp.float32)
        damped = c + (damping_share * jnp.sum(c * eye) / width) * eye
        trace = jnp.sum(damped * eye)
        eyes.append(eye)
        ys.append(damped / trace)
        totals.append(trace)
    both = range(2)
    zs = [1.5 * eyes[i] - 0.5 * ys[i] for i in both]
    ys = [times(parts_of(ys[i]), parts_of(zs[i])) for i in both]

    def sweep(_, carry):
        ys, zs = carry
        sy, sz = [parts_of(y) for y in ys], [parts_of(z) for z in zs]
        sp = [parts_of(1.5 * eyes[i] - 0.5 * times(sz[i], sy[i])) for i in both]
        return [times(sy[i], sp[i]) for i in both], [times(sp[i], sz[i]) for i in both]

    ys, zs = lax.fori_loop(0, ITERS - 2, sweep, (ys, zs))
    sz = [parts_of(z) for z in zs]
    sp = [parts_of(1.5 * eyes[i] - 0.5 * times(sz[i], parts_of(ys[i]))) for i in both]
    roots = [times(sp[i], sz[i]) / jnp.sqrt(totals[i]) for i in both]
    wide[...] = jnp.zeros_like(wide)
    wide[0:BA, 0:BA] = roots[0]
    square[...], spare = pack_square(roots[1][0:HALF], roots[1][HALF:BG])
    folded, low, corner = pack_wide(wide, spare)
    packed_ref[0:HALF] = folded.astype(jnp.bfloat16)
    packed_ref[HALF:112] = low.astype(jnp.bfloat16)
    packed_ref[112:RA] = corner.astype(jnp.bfloat16)
    start = pl.multiple_of((z_ref[0] // 4) * (RG // 2), RG // 2)
    packed_ref[RA:GATHERED] = square[pl.ds(start, RG // 2)].astype(jnp.bfloat16)


def inverse_roots(total, z):
    whole = pl.BlockSpec(memory_space=pltpu.VMEM)
    return pl.pallas_call(
        roots_kernel,
        in_specs=[pl.BlockSpec(memory_space=pltpu.SMEM), whole],
        out_specs=whole,
        out_shape=jax.ShapeDtypeStruct((GATHERED, BG), jnp.bfloat16),
        scratch_shapes=[pltpu.VMEM((176, 256), jnp.float32), pltpu.VMEM((RG, BG), jnp.float32)],
        compiler_params=PARAMS,
        cost_estimate=CHEAP,
        name="inverse_roots",
    )(z.reshape(1), total)


def unpack_halves(first, second, spare):
    return unpack_square(jnp.concatenate([first, second], axis=0), pltpu.roll(spare, HALF, 1))


def owned_blocks(owners_ref, per_layer, position):
    first = second = jnp.int32(-1)
    for place in range(LAYERS * per_layer):
        mine = owners_ref[place // per_layer, place % per_layer] == position
        second = jnp.where(mine & (first >= 0), place, second)
        first = jnp.where(mine & (first < 0), place, first)
    return first, second


def right_kernel(g_ref, w_ref, even_ref, odd_ref, mid_ref, right, spares):
    for odd, ref in enumerate((even_ref, odd_ref)):
        for turn in range(4):
            source = lax.rem(jnp.bitwise_xor(g_ref[0], odd) - 2 * turn + 8, 8)
            right[source] = ref[32 * turn : 32 * (turn + 1)].astype(jnp.float32)
            spares[source] = ref[128:144].astype(jnp.float32)[turn : turn + 1]
    for layer in range(LAYERS):
        root = unpack_halves(right[layer], right[layer + 4], spares[layer]).astype(jnp.bfloat16)
        product = jnp.dot(w_ref[layer], root, preferred_element_type=jnp.float32)
        mid_ref[layer] = product.astype(jnp.bfloat16).astype(jnp.float32)


def multiply_right(column, weight_grad, even, odd):
    whole = pl.BlockSpec(memory_space=pltpu.VMEM)
    return pl.pallas_call(
        right_kernel,
        in_specs=[pl.BlockSpec(memory_space=pltpu.SMEM)] + [whole] * 3,
        out_specs=whole,
        out_shape=jax.ShapeDtypeStruct(weight_grad.shape, jnp.float32),
        scratch_shapes=[
            pltpu.VMEM((8, RG // 2, BG), jnp.float32),
            pltpu.VMEM((8, 1, BG), jnp.float32),
        ],
        compiler_params=PARAMS,
        cost_estimate=pl.CostEstimate(
            flops=2 * 10**10, bytes_accessed=6 * 10**6, transcendentals=0
        ),
        name="multiply_right",
    )(column, weight_grad, even, odd)


def apply_kernel(
    at_ref, oa_ref, og_ref, mid_ref, own_ref, beside_ref, out_ref, sa_ref, sg_ref, a_ref
):
    z, y, c = (at_ref[i] for i in range(3))
    position = 4 * z + 2 * y + c
    owned_a, owned_g = owned_blocks(oa_ref, 8, position), owned_blocks(og_ref, 4, position)

    def place(z_of, y_of, c_of):
        odd = lax.rem(z - z_of + 8, 2)
        start = jnp.where(odd == 1, jnp.bitwise_xor(z, 1), z)
        turn = lax.rem(start - z_of + 8, 8) // 2
        return jnp.bitwise_xor(c_of, c), 4 * (2 * odd + jnp.bitwise_xor(y_of, y)) + turn

    for i, ref in enumerate((own_ref, beside_ref)):
        for slot in range(16):
            a_ref[i, slot] = ref[GATHERED * slot : GATHERED * (slot + 1)]
    for layer in range(LAYERS):
        for quad in range(2):
            results = []
            for k in range(4 * quad, 4 * quad + 4):
                i, slot = place(k, layer % 2, layer // 2)
                left = unpack_wide(a_ref[i, slot, 0:RA].astype(jnp.float32))
                left = left[0:BA, 0:BA].astype(jnp.bfloat16)
                x = mid_ref[layer, BA * k : BA * (k + 1)].astype(jnp.bfloat16)
                results.append(jnp.dot(left, x, preferred_element_type=jnp.float32))
            out_ref[layer, 4 * BA * quad : 4 * BA * (quad + 1)] = jnp.concatenate(
                results, axis=0
            ).astype(jnp.bfloat16)
    stored = []
    for r in range(2):
        block = owned_a[r]
        held = jnp.maximum(block, 0)
        layer = held // 8
        i, slot = place(lax.rem(held, 8), lax.rem(layer, 2), layer // 2)
        root = unpack_wide(a_ref[i, slot, 0:RA].astype(jnp.float32))[0:BA, 0:BA]
        stored.append(jnp.where(block >= 0, root, 0.0))
        block = owned_g[r]
        held = jnp.maximum(block, 0)
        layer, k = held // 4, lax.rem(held, 4)
        halves = []
        for half in range(2):
            i, slot = place(layer + 4 * half, k // 2, lax.rem(k, 2))
            halves.append(a_ref[i, slot, RA - 16 : GATHERED].astype(jnp.float32))
        spare = halves[0][DIAG - RA + 16 : DIAG - RA + 17]
        root = unpack_halves(halves[0][16:48], halves[1][16:48], spare)
        sg_ref[r] = jnp.where(block >= 0, root, 0.0).astype(jnp.bfloat16)
    sa_ref[...] = jnp.stack(stored, axis=1).astype(jnp.bfloat16)


def apply_roots(at, owner_a, owner_g, mid, *gathered):
    whole = pl.BlockSpec(memory_space=pltpu.VMEM)
    return pl.pallas_call(
        apply_kernel,
        in_specs=[pl.BlockSpec(memory_space=pltpu.SMEM)] * 3 + [whole] * 3,
        out_specs=[whole] * 3,
        out_shape=[
            jax.ShapeDtypeStruct(mid.shape, jnp.bfloat16),
            jax.ShapeDtypeStruct((BA, 2, BA), jnp.bfloat16),
            jax.ShapeDtypeStruct((2, BG, BG), jnp.bfloat16),
        ],
        scratch_shapes=[pltpu.VMEM((2, 16, GATHERED, BG), jnp.bfloat16)],
        compiler_params=PARAMS,
        cost_estimate=CHEAP,
        name="apply_roots",
    )(at, owner_a, owner_g, mid, *gathered)


def along_z(shift):
    return [(i, (i + 4 * shift) % 32) for i in range(32)]


OVER_CORE = [(i, i ^ 1) for i in range(32)]
OVER_Y = [(i, i ^ 2) for i in range(32)]
OVER_Z = [(i, i ^ 4) for i in range(32)]
OVER_BOTH = [(i, i ^ 6) for i in range(32)]
EXCHANGE, EXCHANGE_ODD = (
    [
        ((z * 4 + r) * 8 + g, (g * 4 + (r ^ 1)) * 8 + (z ^ odd))
        for z in range(8)
        for r in range(4)
        for g in range(8)
    ]
    for odd in range(2)
)


def tails_of(messages):
    rows = [x[RA:GATHERED] for x in messages] + [x[DIAG : DIAG + 1] for x in messages]
    return jnp.concatenate(rows + [jnp.zeros((12, BG), jnp.bfloat16)])


def narrow(x):
    return (x * WIRE_SCALE).astype(WIRE)


def widen(x):
    return x.astype(jnp.float32) * (1.0 / WIRE_SCALE)


def shards(hidden_acts, out_grads, weight_grad, owner_a, gradient_block_owner):
    position = lax.axis_index("dp")
    column = lax.axis_index("grp")
    z, y, core = position // 4, lax.rem(position // 2, 2), lax.rem(position, 2)
    scale = 1.0 / (hidden_acts.shape[1] * lax.axis_size("dp"))
    turned = jnp.swapaxes(hidden_acts, 1, 2)

    theirs = covariances(turned, out_grads, 1 - core, z, scale)
    got = lax.ppermute(theirs, "dp", OVER_CORE)
    mine = covariances(turned, out_grads, core, z, scale)

    def chip_sum(of_y):
        one = lax.dynamic_index_in_dim(mine, of_y, 0, False)
        return one + lax.dynamic_index_in_dim(got, of_y, 0, False)

    other, own = chip_sum(1 - y), chip_sum(y)
    got_both = lax.ppermute(narrow(other[1]), "dp", OVER_BOTH)
    got_y = lax.ppermute(narrow(other[0]), "dp", OVER_Y)
    got_z = lax.ppermute(narrow(own[1]), "dp", OVER_Z)
    kept = (own[0] + widen(got_y)) + (widen(got_both) + widen(got_z))

    def message(turn):
        start = (turn // 2) * MSG
        return jnp.concatenate(
            [kept[turn % 2, start : start + RA], kept[turn % 2, RA:MSG]], axis=0
        )

    arrived = [lax.ppermute(narrow(message(t)), "dp", along_z(2 * t)) for t in range(1, 4)]
    total = message(0) + sum(widen(x) for x in arrived)
    packed = inverse_roots(total, z)

    held = [packed] + [lax.ppermute(packed, "dp", along_z(2 * t)) for t in range(1, 4)]
    tails = lax.ppermute(tails_of(held), "dp", OVER_CORE)
    held = jnp.concatenate(held)
    got_y = lax.ppermute(held, "dp", OVER_Y)
    got_z = lax.ppermute(held, "dp", OVER_Z)
    got_both = lax.ppermute(held, "dp", OVER_BOTH)
    tails = [lax.ppermute(tails, ("dp", "grp"), pairs) for pairs in (EXCHANGE, EXCHANGE_ODD)]
    gathered = jnp.concatenate([held, got_y, got_z, got_both])
    beside = lax.ppermute(gathered, "dp", OVER_CORE)

    at = jnp.stack([z, y, core])
    mid = multiply_right(column.reshape(1), weight_grad, *tails)
    precond_grad, store_a, store_g = apply_roots(
        at, owner_a, gradient_block_owner, mid, gathered, beside
    )
    return precond_grad, jnp.swapaxes(store_a, 0, 1)[None, None], store_g[None, None]


def solution(mesh):
    return jax.shard_map(
        shards,
        mesh=mesh,
        in_specs=(
            P(None, "dp", "grp"),
            P(None, "dp", "grp"),
            P(None, "grp", "dp"),
            P(None, "grp"),
            P(None, "grp"),
        ),
        out_specs=(
            P(None, "grp", "dp"),
            P("grp", "dp", None, None, None),
            P("grp", "dp", None, None, None),
        ),
        check_vma=False,
    )
```

time: 102 us -> 85.1 us (0.83)
  the two profiles are of different devices: /device:TPU:30 before, /device:TPU:5 now
where the time goes in v2:
time: 85.1 us; the launch traced here: 84.9 us
  starting transfers between devices  39.3 us (46%)
  waiting for transfers between devices  20.7 us (24%)
  Pallas kernels  20 us (24%)
  other arithmetic  2.02 us (2%)
  local copies, waits for them, and re-layouts  1.96 us (2%)
  between operations  0.91 us (1%)
    ppermute x2, starting transfers between devices, shards(): lax.ppermute(tails, ('dp', 'grp'), pairs)  10.4 us
    ppermute x3, starting transfers between devices, shards(): lax.ppermute(narrow(message(t)), 'dp', along_z(2 * t))  10.3 us
    pallas_call x1, Pallas kernels, inverse_roots(): pl.pallas_call(roots_kernel, in_specs=[pl.BlockSpec(memory_space=pltpu.SM...  8.35 us
    pallas_call x2, Pallas kernels, covariances(): pl.pallas_call(functools.partial(cov_kernel, scale), grid_spec=pltpu.Pref...  7.33 us
    ppermute x3, starting transfers between devices, shards(): lax.ppermute(packed, 'dp', along_z(2 * t))  6.76 us
    ppermute x2, waiting for transfers between devices, shards(): lax.ppermute(tails, ('dp', 'grp'), pairs)  5.49 us
    ppermute x1, starting transfers between devices, shards(): tails = lax.ppermute(tails_of(held), 'dp', OVER_CORE)  4.59 us
    ppermute x1, waiting for transfers between devices, shards(): got_y = lax.ppermute(narrow(other[0]), 'dp', OVER_Y)  3.87 us
  transfers between devices with their start and end apart: 17, of which 9 were waited for; matrix products, arithmetic and copies ran while one was open for 1% of the time, Pallas kernels for 5%

profile of v2, /device:TPU:5, one launch (start us, length us, event | category | flops | bytes accessed | tf_op | source)
XLA Modules:
  0.0 84.9 jit_solution(11474859526904383088)
XLA Ops:
  0.7 1.6 %copy-done = bf16[4,512,512]{2,1,0:T(8,128)(2,1)S(1)} copy-done((bf16[4,512,512]{2,1,0:T(8,128)(2,1)S(1)}, bf16[4,512,512]{2,1,0:T(8,128)(2,1)}, u32[]{:S(2)}) %copy-start) | copy-done | bytes 2097176
  2.3 3.7 %covariances.3 = f32[2,2,2,352,128]{4,3,2,1,0:T(8,128)S(1)} custom-call(s32[2]{0:T(128)S(1)} %pad_add_fusion.2.at_ref, bf16[4,1376,512]{2,1,0:T(8,128)(2,1)} %bitcast.34, bf16[4,512,512]{2,1,0:T(8,128)(2,1)S(1)} %copy-done), custom_call_target="tpu_custom_call" | custom-call | flops 10000 | bytes 10000 | tf_op jit(solution)/shard_map/covariances/pallas_call | solution.py:105
  6.9 3.6 %covariances.2 = f32[2,2,2,352,128]{4,3,2,1,0:T(8,128)S(1)} custom-call(s32[2]{0:T(128)S(1)} %pad_add_fusion.1.at_ref, bf16[4,1376,512]{2,1,0:T(8,128)(2,1)} %bitcast.35, bf16[4,512,512]{2,1,0:T(8,128)(2,1)S(1)} %copy-done.1), custom_call_target="tpu_custom_call" | custom-call | flops 10000 | bytes 10000 | tf_op jit(solution)/shard_map/covariances/pallas_call | solution.py:105
  10.5 1.5 %dynamic-slice_add_fusion = (f32[1,2,2,352,128]{4,3,2,1,0:T(8,128)S(1)}, f32[1,2,2,352,128]{4,3,2,1,0:T(8,128)S(1)}) fusion(f32[2,2,2,352,128]{4,3,2,1,0:T(8,128)} %collective-permute-done, s32[]{:T(128)S(6)} %select_n.20, f32[2,2,2,352,128]{4,3,2,1,0:T(8,128)S(1)} %covariances.2, s32[]{:T(128)S(6)} %select_n.19), kind=kLoop, calls=%fused_computation | loop fusion | flops 360448 | bytes 4325384 | tf_op jit(solution)/shard_map/add | solution.py:344
  12.2 1.7 %collective-permute-start.3 = (f16[2,352,128]{2,1,0:T(8,128)(2,1)S(1)}, f16[2,352,128]{2,1,0:T(8,128)(2,1)S(1)}, u32[]{:S(2)}, u32[]{:S(2)}) collective-permute-start(f16[2,352,128]{2,1,0:T(8,128)(2,1)S(1)} %fusion.7), channel_id=1, source_target_pairs={{0,32},{8,40},{16,48},{24,56},{32,0},{40,8},{48,16},{56,24},{64,96... | collective-permute-start | bytes 540680 | tf_op jit(solution)/shard_map/ppermute | solution.py:349
  13.9 1.3 %collective-permute-start.1 = (f16[2,352,128]{2,1,0:T(8,128)(2,1)S(1)}, f16[2,352,128]{2,1,0:T(8,128)(2,1)S(1)}, u32[]{:S(2)}, u32[]{:S(2)}) collective-permute-start(f16[2,352,128]{2,1,0:T(8,128)(2,1)S(1)} %get-tuple-element.11), channel_id=1, source_target_pairs={{0,16},{8,24},{16,0},{24,8},{32,48},{40,56},{48,32},{56,40},{64,80... | collective-permute-start | bytes 540680 | tf_op jit(solution)/shard_map/ppermute | solution.py:348
  15.2 3.5 %collective-permute-done.3 = f16[2,352,128]{2,1,0:T(8,128)(2,1)S(1)} collective-permute-done((f16[2,352,128]{2,1,0:T(8,128)(2,1)S(1)}, f16[2,352,128]{2,1,0:T(8,128)(2,1)S(1)}, u32[]{:S(2)}, u32[]{:S(2)}) %collective-permute-start.3) | collective-permute-done | bytes 180256 | tf_op jit(solution)/shard_map/ppermute | solution.py:349
  18.7 3.9 %collective-permute-done.1 = f16[2,352,128]{2,1,0:T(8,128)(2,1)S(1)} collective-permute-done((f16[2,352,128]{2,1,0:T(8,128)(2,1)S(1)}, f16[2,352,128]{2,1,0:T(8,128)(2,1)S(1)}, u32[]{:S(2)}, u32[]{:S(2)}) %collective-permute-start.1) | collective-permute-done | bytes 180256 | tf_op jit(solution)/shard_map/ppermute | solution.py:348
  22.5 1.1 %collective-permute-done.2 = f16[2,352,128]{2,1,0:T(8,128)(2,1)S(1)} collective-permute-done((f16[2,352,128]{2,1,0:T(8,128)(2,1)S(1)}, f16[2,352,128]{2,1,0:T(8,128)(2,1)S(1)}, u32[]{:S(2)}, u32[]{:S(2)}) %collective-permute-start.2) | collective-permute-done | bytes 180256 | tf_op jit(solution)/shard_map/ppermute | solution.py:347
  23.8 6.7 %collective-permute-start.5 = (f16[208,128]{1,0:T(8,128)(2,1)S(1)}, f16[208,128]{1,0:T(8,128)(2,1)S(1)}, u32[]{:S(2)}, u32[]{:S(2)}) collective-permute-start(f16[208,128]{1,0:T(8,128)(2,1)S(1)} %fusion.14), channel_id=1, source_target_pairs={{0,128},{8,136},{16,144},{24,152},{32,160},{40,168},{48,176},{56,1... | collective-permute-start | bytes 159752 | tf_op jit(solution)/shard_map/ppermute | solution.py:358
  30.5 1.3 %collective-permute-start.4 = (f16[208,128]{1,0:T(8,128)(2,1)S(1)}, f16[208,128]{1,0:T(8,128)(2,1)S(1)}, u32[]{:S(2)}, u32[]{:S(2)}) collective-permute-start(f16[208,128]{1,0:T(8,128)(2,1)S(1)} %get-tuple-element.19), channel_id=1, source_target_pairs={{0,64},{8,72},{16,80},{24,88},{32,96},{40,104},{48,112},{56,120},{... | collective-permute-start | bytes 159752 | tf_op jit(solution)/shard_map/ppermute | solution.py:358
  31.8 2.4 %collective-permute-start.6 = (f16[208,128]{1,0:T(8,128)(2,1)S(1)}, f16[208,128]{1,0:T(8,128)(2,1)S(1)}, u32[]{:S(2)}, u32[]{:S(2)}) collective-permute-start(f16[208,128]{1,0:T(8,128)(2,1)S(1)} %get-tuple-element.20), channel_id=1, source_target_pairs={{0,192},{8,200},{16,208},{24,216},{32,224},{40,232},{48,240},{56,2... | collective-permute-start | bytes 159752 | tf_op jit(solution)/shard_map/ppermute | solution.py:358
  34.2 1.9 %collective-permute-done.4 = f16[208,128]{1,0:T(8,128)(2,1)S(1)} collective-permute-done((f16[208,128]{1,0:T(8,128)(2,1)S(1)}, f16[208,128]{1,0:T(8,128)(2,1)S(1)}, u32[]{:S(2)}, u32[]{:S(2)}) %collective-permute-start.4) | collective-permute-done | bytes 53280 | tf_op jit(solution)/shard_map/ppermute | solution.py:358
  36.4 8.3 %inverse_roots.1 = bf16[176,128]{1,0:T(8,128)(2,1)S(1)} custom-call(s32[1]{0:T(128)} %bitcast.z_ref, f32[208,128]{1,0:T(8,128)S(1)} %fusion.12.total_ref), custom_call_target="tpu_custom_call" | custom-call | flops 10000 | bytes 10000 | tf_op jit(solution)/shard_map/inverse_roots/pallas_call | solution.py:176
  44.7 3.6 %collective-permute-start.9 = (bf16[176,128]{1,0:T(8,128)(2,1)S(1)}, bf16[176,128]{1,0:T(8,128)(2,1)S(1)}, u32[]{:S(2)}, u32[]{:S(2)}) collective-permute-start(bf16[176,128]{1,0:T(8,128)(2,1)S(1)} %inverse_roots.1), channel_id=1, source_target_pairs={{0,192},{8,200},{16,208},{24,216},{32,224},{40,232},{48,240},{56,2... | collective-permute-start | bytes 135176 | tf_op jit(solution)/shard_map/ppermute | solution.py:362
  48.3 0.9 %collective-permute-start.8 = (bf16[176,128]{1,0:T(8,128)(2,1)S(1)}, bf16[176,128]{1,0:T(8,128)(2,1)S(1)}, u32[]{:S(2)}, u32[]{:S(2)}) collective-permute-start(bf16[176,128]{1,0:T(8,128)(2,1)S(1)} %inverse_roots.1), channel_id=1, source_target_pairs={{0,128},{8,136},{16,144},{24,152},{32,160},{40,168},{48,176},{56,1... | collective-permute-start | bytes 135176 | tf_op jit(solution)/shard_map/ppermute | solution.py:362
  49.2 2.3 %collective-permute-start.7 = (bf16[176,128]{1,0:T(8,128)(2,1)S(1)}, bf16[176,128]{1,0:T(8,128)(2,1)S(1)}, u32[]{:S(2)}, u32[]{:S(2)}) collective-permute-start(bf16[176,128]{1,0:T(8,128)(2,1)S(1)} %inverse_roots.1), channel_id=1, source_target_pairs={{0,64},{8,72},{16,80},{24,88},{32,96},{40,104},{48,112},{56,120},{... | collective-permute-start | bytes 135176 | tf_op jit(solution)/shard_map/ppermute | solution.py:362
  51.5 3.6 %collective-permute-done.8 = bf16[176,128]{1,0:T(8,128)(2,1)S(1)} collective-permute-done((bf16[176,128]{1,0:T(8,128)(2,1)S(1)}, bf16[176,128]{1,0:T(8,128)(2,1)S(1)}, u32[]{:S(2)}, u32[]{:S(2)}) %collective-permute-start.8) | collective-permute-done | bytes 45088 | tf_op jit(solution)/shard_map/ppermute | solution.py:362
  55.4 2.6 %collective-permute-start.15 = (bf16[704,128]{1,0:T(8,128)(2,1)S(1)}, bf16[704,128]{1,0:T(8,128)(2,1)S(1)}, u32[]{:S(2)}, u32[]{:S(2)}) collective-permute-start(bf16[704,128]{1,0:T(8,128)(2,1)S(1)} %pad_maximum_fusion), channel_id=1, source_target_pairs={{0,48},{8,56},{16,32},{24,40},{32,16},{40,24},{48,0},{56,8},{64,11... | collective-permute-start | bytes 540680 | tf_op jit(solution)/shard_map/ppermute | solution.py:367
  58.6 4.6 %collective-permute-start.10 = (bf16[144,128]{1,0:T(8,128)(2,1)S(1)}, bf16[144,128]{1,0:T(8,128)(2,1)S(1)}, u32[]{:S(2)}, u32[]{:S(2)}) collective-permute-start(bf16[144,128]{1,0:T(8,128)(2,1)S(1)} %concatenate.26), channel_id=1, source_target_pairs={{0,8},{8,0},{16,24},{24,16},{32,40},{40,32},{48,56},{56,48},{64,72... | collective-permute-start | bytes 110600 | tf_op jit(solution)/shard_map/ppermute | solution.py:363
  64.1 6.7 %collective-permute-start.12 = (bf16[144,128]{1,0:T(8,128)(2,1)S(1)}, bf16[144,128]{1,0:T(8,128)(2,1)S(1)}, u32[]{:S(2)}, u32[]{:S(2)}) collective-permute-start(bf16[144,128]{1,0:T(8,128)(2,1)S(1)} %collective-permute-done.10), channel_id=1, source_target_pairs={{0,9},{1,41},{2,73},{3,105},{4,137},{5,169},{6,201},{7,233},{8,1},... | collective-permute-start | bytes 110600 | tf_op jit(solution)/shard_map/ppermute | solution.py:368
  70.8 3.6 %collective-permute-start.11 = (bf16[144,128]{1,0:T(8,128)(2,1)S(1)}, bf16[144,128]{1,0:T(8,128)(2,1)S(1)}, u32[]{:S(2)}, u32[]{:S(2)}) collective-permute-start(bf16[144,128]{1,0:T(8,128)(2,1)S(1)} %collective-permute-done.10), channel_id=1, source_target_pairs={{0,8},{1,40},{2,72},{3,104},{4,136},{5,168},{6,200},{7,232},{8,0},... | collective-permute-start | bytes 110600 | tf_op jit(solution)/shard_map/ppermute | solution.py:368
  75.1 5.5 %collective-permute-done.11.even_ref = bf16[144,128]{1,0:T(8,128)(2,1)S(1)} collective-permute-done((bf16[144,128]{1,0:T(8,128)(2,1)S(1)}, bf16[144,128]{1,0:T(8,128)(2,1)S(1)}, u32[]{:S(2)}, u32[]{:S(2)}) %collective-permute-start.11) | collective-permute-done | bytes 36896 | tf_op jit(solution)/shard_map/ppermute | solution.py:368
  81.3 3.6 %apply_roots.1 = (bf16[4,1376,128]{2,1,0:T(8,128)(2,1)}, bf16[172,2,172]{2,1,0:T(2,128)(2,1)}, bf16[2,128,128]{2,1,0:T(8,128)(2,1)}) custom-call(s32[3]{0:T(128)S(1)} %pad_add_fusion.at_ref, s32[4,8]{1,0:T(4,128)S(1)} %copy-done.2, s32[4,4]{1,0:T(4,128)S(1)} %copy-done.3, f32[4,1376,128]{2,1,0:T(8,128)S(1)} %multiply_right.1.mid_ref, ...), custom_call_target="tpu_custom_call" | custom-call | flops 10000 | bytes 10000 | tf_op jit(solution)/shard_map/apply_roots/pallas_call | solution.py:283
  (55 shorter events, 4.5 us)
Async XLA Ops:
  0.7 1.6 %copy-start = (bf16[4,512,512]{2,1,0:T(8,128)(2,1)S(1)}, bf16[4,512,512]{2,1,0:T(8,128)(2,1)}, u32[]{:S(2)}) copy-start(bf16[4,512,512]{2,1,0:T(8,128)(2,1)} %g_ref.3) | copy-start | bytes 6291460
  2.3 4.6 %copy-start.1 = (bf16[4,512,512]{2,1,0:T(8,128)(2,1)S(1)}, bf16[4,512,512]{2,1,0:T(8,128)(2,1)}, u32[]{:S(2)}) copy-start(bf16[4,512,512]{2,1,0:T(8,128)(2,1)} %g_ref.3) | copy-start | bytes 6291460
  6.0 4.5 %collective-permute-start = (f32[2,2,2,352,128]{4,3,2,1,0:T(8,128)S(1)}, f32[2,2,2,352,128]{4,3,2,1,0:T(8,128)}, u32[]{:S(2)}, u32[]{:S(2)}) collective-permute-start(f32[2,2,2,352,128]{4,3,2,1,0:T(8,128)S(1)} %covariances.3), channel_id=1, source_target_pairs={{0,8},{8,0},{16,24},{24,16},{32,40},{40,32},{48,56},{56,48},{64,72... | collective-permute-start | bytes 4325384 | tf_op jit(solution)/shard_map/ppermute | solution.py:339
  12.2 6.5 %collective-permute-start.3 = (f16[2,352,128]{2,1,0:T(8,128)(2,1)S(1)}, f16[2,352,128]{2,1,0:T(8,128)(2,1)S(1)}, u32[]{:S(2)}, u32[]{:S(2)}) collective-permute-start(f16[2,352,128]{2,1,0:T(8,128)(2,1)S(1)} %fusion.7), channel_id=1, source_target_pairs={{0,32},{8,40},{16,48},{24,56},{32,0},{40,8},{48,16},{56,24},{64,96... | collective-permute-start | bytes 540680 | tf_op jit(solution)/shard_map/ppermute | solution.py:349
  13.9 8.7 %collective-permute-start.1 = (f16[2,352,128]{2,1,0:T(8,128)(2,1)S(1)}, f16[2,352,128]{2,1,0:T(8,128)(2,1)S(1)}, u32[]{:S(2)}, u32[]{:S(2)}) collective-permute-start(f16[2,352,128]{2,1,0:T(8,128)(2,1)S(1)} %get-tuple-element.11), channel_id=1, source_target_pairs={{0,16},{8,24},{16,0},{24,8},{32,48},{40,56},{48,32},{56,40},{64,80... | collective-permute-start | bytes 540680 | tf_op jit(solution)/shard_map/ppermute | solution.py:348
  15.2 8.4 %collective-permute-start.2 = (f16[2,352,128]{2,1,0:T(8,128)(2,1)S(1)}, f16[2,352,128]{2,1,0:T(8,128)(2,1)S(1)}, u32[]{:S(2)}, u32[]{:S(2)}) collective-permute-start(f16[2,352,128]{2,1,0:T(8,128)(2,1)S(1)} %get-tuple-element.12), channel_id=1, source_target_pairs={{0,48},{8,56},{16,32},{24,40},{32,16},{40,24},{48,0},{56,8},{64,11... | collective-permute-start | bytes 540680 | tf_op jit(solution)/shard_map/ppermute | solution.py:347
  23.8 56.8 %copy-start.4 = (bf16[4,1376,128]{2,1,0:T(8,128)(2,1)S(1)}, bf16[4,1376,128]{2,1,0:T(8,128)(2,1)}, u32[]{:S(2)}) copy-start(bf16[4,1376,128]{2,1,0:T(8,128)(2,1)} %w_ref.1) | copy-start | bytes 4227076
  23.8 10.4 %collective-permute-start.5 = (f16[208,128]{1,0:T(8,128)(2,1)S(1)}, f16[208,128]{1,0:T(8,128)(2,1)S(1)}, u32[]{:S(2)}, u32[]{:S(2)}) collective-permute-start(f16[208,128]{1,0:T(8,128)(2,1)S(1)} %fusion.14), channel_id=1, source_target_pairs={{0,128},{8,136},{16,144},{24,152},{32,160},{40,168},{48,176},{56,1... | collective-permute-start | bytes 159752 | tf_op jit(solution)/shard_map/ppermute | solution.py:358
  30.5 5.6 %collective-permute-start.4 = (f16[208,128]{1,0:T(8,128)(2,1)S(1)}, f16[208,128]{1,0:T(8,128)(2,1)S(1)}, u32[]{:S(2)}, u32[]{:S(2)}) collective-permute-start(f16[208,128]{1,0:T(8,128)(2,1)S(1)} %get-tuple-element.19), channel_id=1, source_target_pairs={{0,64},{8,72},{16,80},{24,88},{32,96},{40,104},{48,112},{56,120},{... | collective-permute-start | bytes 159752 | tf_op jit(solution)/shard_map/ppermute | solution.py:358
  31.8 4.6 %collective-permute-start.6 = (f16[208,128]{1,0:T(8,128)(2,1)S(1)}, f16[208,128]{1,0:T(8,128)(2,1)S(1)}, u32[]{:S(2)}, u32[]{:S(2)}) collective-permute-start(f16[208,128]{1,0:T(8,128)(2,1)S(1)} %get-tuple-element.20), channel_id=1, source_target_pairs={{0,192},{8,200},{16,208},{24,216},{32,224},{40,232},{48,240},{56,2... | collective-permute-start | bytes 159752 | tf_op jit(solution)/shard_map/ppermute | solution.py:358
  44.7 6.8 %collective-permute-start.9 = (bf16[176,128]{1,0:T(8,128)(2,1)S(1)}, bf16[176,128]{1,0:T(8,128)(2,1)S(1)}, u32[]{:S(2)}, u32[]{:S(2)}) collective-permute-start(bf16[176,128]{1,0:T(8,128)(2,1)S(1)} %inverse_roots.1), channel_id=1, source_target_pairs={{0,192},{8,200},{16,208},{24,216},{32,224},{40,232},{48,240},{56,2... | collective-permute-start | bytes 135176 | tf_op jit(solution)/shard_map/ppermute | solution.py:362
  48.3 6.8 %collective-permute-start.8 = (bf16[176,128]{1,0:T(8,128)(2,1)S(1)}, bf16[176,128]{1,0:T(8,128)(2,1)S(1)}, u32[]{:S(2)}, u32[]{:S(2)}) collective-permute-start(bf16[176,128]{1,0:T(8,128)(2,1)S(1)} %inverse_roots.1), channel_id=1, source_target_pairs={{0,128},{8,136},{16,144},{24,152},{32,160},{40,168},{48,176},{56,1... | collective-permute-start | bytes 135176 | tf_op jit(solution)/shard_map/ppermute | solution.py:362
  49.2 6.1 %collective-permute-start.7 = (bf16[176,128]{1,0:T(8,128)(2,1)S(1)}, bf16[176,128]{1,0:T(8,128)(2,1)S(1)}, u32[]{:S(2)}, u32[]{:S(2)}) collective-permute-start(bf16[176,128]{1,0:T(8,128)(2,1)S(1)} %inverse_roots.1), channel_id=1, source_target_pairs={{0,64},{8,72},{16,80},{24,88},{32,96},{40,104},{48,112},{56,120},{... | collective-permute-start | bytes 135176 | tf_op jit(solution)/shard_map/ppermute | solution.py:362
  55.4 19.2 %collective-permute-start.15 = (bf16[704,128]{1,0:T(8,128)(2,1)S(1)}, bf16[704,128]{1,0:T(8,128)(2,1)S(1)}, u32[]{:S(2)}, u32[]{:S(2)}) collective-permute-start(bf16[704,128]{1,0:T(8,128)(2,1)S(1)} %pad_maximum_fusion), channel_id=1, source_target_pairs={{0,48},{8,56},{16,32},{24,40},{32,16},{40,24},{48,0},{56,8},{64,11... | collective-permute-start | bytes 540680 | tf_op jit(solution)/shard_map/ppermute | solution.py:367
  58.0 16.5 %collective-permute-start.14 = (bf16[704,128]{1,0:T(8,128)(2,1)S(1)}, bf16[704,128]{1,0:T(8,128)(2,1)S(1)}, u32[]{:S(2)}, u32[]{:S(2)}) collective-permute-start(bf16[704,128]{1,0:T(8,128)(2,1)S(1)} %pad_maximum_fusion), channel_id=1, source_target_pairs={{0,32},{8,40},{16,48},{24,56},{32,0},{40,8},{48,16},{56,24},{64,96... | collective-permute-start | bytes 540680 | tf_op jit(solution)/shard_map/ppermute | solution.py:366
  58.0 16.5 %collective-permute-start.13 = (bf16[704,128]{1,0:T(8,128)(2,1)S(1)}, bf16[704,128]{1,0:T(8,128)(2,1)S(1)}, u32[]{:S(2)}, u32[]{:S(2)}) collective-permute-start(bf16[704,128]{1,0:T(8,128)(2,1)S(1)} %pad_maximum_fusion), channel_id=1, source_target_pairs={{0,16},{8,24},{16,0},{24,8},{32,48},{40,56},{48,32},{56,40},{64,80... | collective-permute-start | bytes 540680 | tf_op jit(solution)/shard_map/ppermute | solution.py:365
  58.6 5.5 %collective-permute-start.10 = (bf16[144,128]{1,0:T(8,128)(2,1)S(1)}, bf16[144,128]{1,0:T(8,128)(2,1)S(1)}, u32[]{:S(2)}, u32[]{:S(2)}) collective-permute-start(bf16[144,128]{1,0:T(8,128)(2,1)S(1)} %concatenate.26), channel_id=1, source_target_pairs={{0,8},{8,0},{16,24},{24,16},{32,40},{40,32},{48,56},{56,48},{64,72... | collective-permute-start | bytes 110600 | tf_op jit(solution)/shard_map/ppermute | solution.py:363
  64.1 11.0 %collective-permute-start.12 = (bf16[144,128]{1,0:T(8,128)(2,1)S(1)}, bf16[144,128]{1,0:T(8,128)(2,1)S(1)}, u32[]{:S(2)}, u32[]{:S(2)}) collective-permute-start(bf16[144,128]{1,0:T(8,128)(2,1)S(1)} %collective-permute-done.10), channel_id=1, source_target_pairs={{0,9},{1,41},{2,73},{3,105},{4,137},{5,169},{6,201},{7,233},{8,1},... | collective-permute-start | bytes 110600 | tf_op jit(solution)/shard_map/ppermute | solution.py:368
  70.8 9.7 %collective-permute-start.11 = (bf16[144,128]{1,0:T(8,128)(2,1)S(1)}, bf16[144,128]{1,0:T(8,128)(2,1)S(1)}, u32[]{:S(2)}, u32[]{:S(2)}) collective-permute-start(bf16[144,128]{1,0:T(8,128)(2,1)S(1)} %collective-permute-done.10), channel_id=1, source_target_pairs={{0,8},{1,40},{2,72},{3,104},{4,136},{5,168},{6,200},{7,232},{8,0},... | collective-permute-start | bytes 110600 | tf_op jit(solution)/shard_map/ppermute | solution.py:368
  74.6 6.6 %collective-permute-start.16 = (bf16[2816,128]{1,0:T(8,128)(2,1)S(1)}, bf16[2816,128]{1,0:T(8,128)(2,1)S(1)}, u32[]{:S(2)}, u32[]{:S(2)}) collective-permute-start(bf16[2816,128]{1,0:T(8,128)(2,1)S(1)} %constant_dynamic-update-slice_fusion.own_ref), channel_id=1, source_target_pairs={{0,8},{8,0},{16,24},{24,16},{32,40},{40,32},{48,56},{56,48},{64,72... | collective-permute-start | bytes 2162696 | tf_op jit(solution)/shard_map/ppermute | solution.py:370
  80.5 0.7 copy-start.2
  80.5 0.7 copy-start.3

commit v3 on v2

--- a/solution.py
+++ b/solution.py
@@ -82,17 +82,17 @@
         c = lax.dot_general(x, x, (((0,), (0,)), ((), ())), preferred_element_type=jnp.float32)
         folded, spare = pack_square(c[0:HALF] * scale, c[HALF:BG] * scale)
         spares.append(spare)
-        turn = lax.rem(layer // 2 - z // 2 + 4, 2)
-        o_ref[0, lax.rem(layer - z + 8, 2), turn, RA : RA + RG] = folded
+        turn = (layer // 2 - (z >> 1)) & 1
+        o_ref[0, (layer ^ z) & 1, turn, RA : RA + RG] = folded
     for k in range(8):
         x = h_ref[0, BA * k : BA * (k + 1), :]
         c = lax.dot_general(x, x, (((1,), (1,)), ((), ())), preferred_element_type=jnp.float32)
         wide[k, BG:176] = jnp.zeros((48, 256), jnp.float32)
         wide[k, 0:BA, 0:BA] = c * scale
     for k in range(8):
-        turn = lax.rem(k // 2 - z // 2 + 4, 4)
-        odd, place = lax.rem(k - z + 8, 2), lax.rem(turn, 2)
-        base = pl.multiple_of((turn // 2) * MSG, 16)
+        turn = (k // 2 - (z >> 1)) & 3
+        odd, place = (k ^ z) & 1, turn & 1
+        base = pl.multiple_of((turn >> 1) * MSG, 16)
         folded, low, corner = pack_wide(wide.at[k], spares[k % 4])
         o_ref[0, odd, place, pl.ds(base, HALF)] = folded
         o_ref[0, odd, place, pl.ds(base + HALF, 48)] = low
@@ -167,7 +167,7 @@
     packed_ref[0:HALF] = folded.astype(jnp.bfloat16)
     packed_ref[HALF:112] = low.astype(jnp.bfloat16)
     packed_ref[112:RA] = corner.astype(jnp.bfloat16)
-    start = pl.multiple_of((z_ref[0] // 4) * (RG // 2), RG // 2)
+    start = pl.multiple_of((z_ref[0] >> 2) * (RG // 2), RG // 2)
     packed_ref[RA:GATHERED] = square[pl.ds(start, RG // 2)].astype(jnp.bfloat16)
 
 
@@ -198,10 +198,11 @@
     return first, second
 
 
-def right_kernel(g_ref, w_ref, even_ref, odd_ref, mid_ref, right, spares):
+def right_kernel(at_ref, w_ref, even_ref, odd_ref, mid_ref, right, spares):
+    start = source_of(at_ref[0], at_ref[1])
     for odd, ref in enumerate((even_ref, odd_ref)):
         for turn in range(4):
-            source = lax.rem(jnp.bitwise_xor(g_ref[0], odd) - 2 * turn + 8, 8)
+            source = ((start ^ odd) - 2 * turn) & 7
             right[source] = ref[32 * turn : 32 * (turn + 1)].astype(jnp.float32)
             spares[source] = ref[128:144].astype(jnp.float32)[turn : turn + 1]
     for layer in range(LAYERS):
@@ -210,7 +211,7 @@
         mid_ref[layer] = product.astype(jnp.bfloat16).astype(jnp.float32)
 
 
-def multiply_right(column, weight_grad, even, odd):
+def multiply_right(at, weight_grad, even, odd):
     whole = pl.BlockSpec(memory_space=pltpu.VMEM)
     return pl.pallas_call(
         right_kernel,
@@ -226,25 +227,25 @@
             flops=2 * 10**10, bytes_accessed=6 * 10**6, transcendentals=0
         ),
         name="multiply_right",
-    )(column, weight_grad, even, odd)
+    )(at, weight_grad, even, odd)
 
 
 def apply_kernel(
-    at_ref, oa_ref, og_ref, mid_ref, own_ref, beside_ref, out_ref, sa_ref, sg_ref, a_ref
+    at_ref, oa_ref, og_ref, mid_ref, own_ref, first_ref, rest_ref, out_ref, sa_ref, sg_ref, a_ref
 ):
     z, y, c = (at_ref[i] for i in range(3))
     position = 4 * z + 2 * y + c
     owned_a, owned_g = owned_blocks(oa_ref, 8, position), owned_blocks(og_ref, 4, position)
 
     def place(z_of, y_of, c_of):
-        odd = lax.rem(z - z_of + 8, 2)
-        start = jnp.where(odd == 1, jnp.bitwise_xor(z, 1), z)
-        turn = lax.rem(start - z_of + 8, 8) // 2
-        return jnp.bitwise_xor(c_of, c), 4 * (2 * odd + jnp.bitwise_xor(y_of, y)) + turn
-
-    for i, ref in enumerate((own_ref, beside_ref)):
-        for slot in range(16):
-            a_ref[i, slot] = ref[GATHERED * slot : GATHERED * (slot + 1)]
+        odd = (z ^ z_of) & 1
+        turn = (((z ^ odd) - z_of) & 7) >> 1
+        return c_of ^ c, 8 * odd + 4 * (y_of ^ y) + turn
+
+    for slot in range(16):
+        a_ref[0, slot] = own_ref[GATHERED * slot : GATHERED * (slot + 1)]
+        ref, start = (first_ref, slot) if slot < 4 else (rest_ref, slot - 4)
+        a_ref[1, slot] = ref[GATHERED * start : GATHERED * (start + 1)]
     for layer in range(LAYERS):
         for quad in range(2):
             results = []
@@ -261,16 +262,16 @@
     for r in range(2):
         block = owned_a[r]
         held = jnp.maximum(block, 0)
-        layer = held // 8
-        i, slot = place(lax.rem(held, 8), lax.rem(layer, 2), layer // 2)
+        layer = held >> 3
+        i, slot = place(held & 7, layer & 1, layer >> 1)
         root = unpack_wide(a_ref[i, slot, 0:RA].astype(jnp.float32))[0:BA, 0:BA]
         stored.append(jnp.where(block >= 0, root, 0.0))
         block = owned_g[r]
         held = jnp.maximum(block, 0)
-        layer, k = held // 4, lax.rem(held, 4)
+        layer, k = held >> 2, held & 3
         halves = []
         for half in range(2):
-            i, slot = place(layer + 4 * half, k // 2, lax.rem(k, 2))
+            i, slot = place(layer + 4 * half, k >> 1, k & 1)
             halves.append(a_ref[i, slot, RA - 16 : GATHERED].astype(jnp.float32))
         spare = halves[0][DIAG - RA + 16 : DIAG - RA + 17]
         root = unpack_halves(halves[0][16:48], halves[1][16:48], spare)
@@ -282,7 +283,7 @@
     whole = pl.BlockSpec(memory_space=pltpu.VMEM)
     return pl.pallas_call(
         apply_kernel,
-        in_specs=[pl.BlockSpec(memory_space=pltpu.SMEM)] * 3 + [whole] * 3,
+        in_specs=[pl.BlockSpec(memory_space=pltpu.SMEM)] * 3 + [whole] * 4,
         out_specs=[whole] * 3,
         out_shape=[
             jax.ShapeDtypeStruct(mid.shape, jnp.bfloat16),
@@ -304,15 +305,23 @@
 OVER_Y = [(i, i ^ 2) for i in range(32)]
 OVER_Z = [(i, i ^ 4) for i in range(32)]
 OVER_BOTH = [(i, i ^ 6) for i in range(32)]
-EXCHANGE, EXCHANGE_ODD = (
-    [
-        ((z * 4 + r) * 8 + g, (g * 4 + (r ^ 1)) * 8 + (z ^ odd))
-        for z in range(8)
-        for r in range(4)
-        for g in range(8)
-    ]
-    for odd in range(2)
-)
+AWAY = (4, 6, 3, 1, 2, 0, 5, 7)
+
+
+def source_of(z, g):
+    place = 2 * (((g >> 1) - (z >> 1)) & 3) + ((g ^ z) & 1)
+    away = sum(jnp.where(place == i, AWAY[i], 0) for i in range(8))
+    return (z + away) & 7
+
+
+def from_column(odd):
+    pairs = []
+    for z in range(8):
+        for g in range(8):
+            away = AWAY[2 * ((g // 2 - z // 2) % 4) + (g + z) % 2]
+            source = (z + away) % 8 ^ odd
+            pairs += [((source * 4 + r) * 8 + z, (z * 4 + r) * 8 + g) for r in range(4)]
+    return sorted(pairs)
 
 
 def tails_of(messages):
@@ -360,19 +369,20 @@
     packed = inverse_roots(total, z)
 
     held = [packed] + [lax.ppermute(packed, "dp", along_z(2 * t)) for t in range(1, 4)]
-    tails = lax.ppermute(tails_of(held), "dp", OVER_CORE)
+    tails = tails_of(held)
     held = jnp.concatenate(held)
     got_y = lax.ppermute(held, "dp", OVER_Y)
     got_z = lax.ppermute(held, "dp", OVER_Z)
     got_both = lax.ppermute(held, "dp", OVER_BOTH)
-    tails = [lax.ppermute(tails, ("dp", "grp"), pairs) for pairs in (EXCHANGE, EXCHANGE_ODD)]
+    first, tails = lax.optimization_barrier((lax.ppermute(held, "dp", OVER_CORE), tails))
+    tails = [lax.ppermute(tails, ("dp", "grp"), pairs) for pairs in map(from_column, (0, 1))]
     gathered = jnp.concatenate([held, got_y, got_z, got_both])
-    beside = lax.ppermute(gathered, "dp", OVER_CORE)
+    rest = lax.ppermute(gathered[4 * GATHERED :], "dp", OVER_CORE)
 
     at = jnp.stack([z, y, core])
-    mid = multiply_right(column.reshape(1), weight_grad, *tails)
+    mid = multiply_right(jnp.stack([z, column]), weight_grad, *tails)
     precond_grad, store_a, store_g = apply_roots(
-        at, owner_a, gradient_block_owner, mid, gathered, beside
+        at, owner_a, gradient_block_owner, mid, gathered, first, rest
     )
     return precond_grad, jnp.swapaxes(store_a, 0, 1)[None, None], store_g[None, None]
 

time: 85.1 us -> 82 us (0.964)
  the two profiles are of different devices: /device:TPU:5 before, /device:TPU:30 now
where the time goes in v3:
time: 82 us; the launch traced here: 81.9 us
  starting transfers between devices  29.9 us (36%)
  waiting for transfers between devices  26.3 us (32%)
  Pallas kernels  20.6 us (25%)
  other arithmetic  2.12 us (3%)
  local copies, waits for them, and re-layouts  1.97 us (2%)
  between operations  0.95 us (1%)
    ppermute x3, starting transfers between devices, shards(): lax.ppermute(narrow(message(t)), 'dp', along_z(2 * t))  10.6 us
    pallas_call x1, Pallas kernels, inverse_roots(): pl.pallas_call(roots_kernel, in_specs=[pl.BlockSpec(memory_space=pltpu.SM...  8.35 us
    ppermute x2, waiting for transfers between devices, shards(): lax.ppermute(tails, ('dp', 'grp'), pairs)  7.71 us
    pallas_call x2, Pallas kernels, covariances(): pl.pallas_call(functools.partial(cov_kernel, scale), grid_spec=pltpu.Pref...  7.36 us
    ppermute x3, starting transfers between devices, shards(): lax.ppermute(packed, 'dp', along_z(2 * t))  6.48 us
    ppermute x3, waiting for transfers between devices, shards(): lax.ppermute(packed, 'dp', along_z(2 * t))  5.72 us
    ppermute x2, starting transfers between devices, shards(): lax.ppermute(tails, ('dp', 'grp'), pairs)  5.53 us
    ppermute x1, waiting for transfers between devices, shards(): got_y = lax.ppermute(narrow(other[0]), 'dp', OVER_Y)  5.03 us
  transfers between devices with their start and end apart: 17, of which 8 were waited for; matrix products, arithmetic and copies ran while one was open for 1% of the time, Pallas kernels for 6%

profile of v3, /device:TPU:30, one launch (start us, length us, event | category | flops | bytes accessed | tf_op | source)
XLA Modules:
  0.0 81.9 jit_solution(12294858504034811557)
XLA Ops:
  0.7 1.6 %copy-done = bf16[4,512,512]{2,1,0:T(8,128)(2,1)S(1)} copy-done((bf16[4,512,512]{2,1,0:T(8,128)(2,1)S(1)}, bf16[4,512,512]{2,1,0:T(8,128)(2,1)}, u32[]{:S(2)}) %copy-start) | copy-done | bytes 2097176
  2.3 3.7 %covariances.3 = f32[2,2,2,352,128]{4,3,2,1,0:T(8,128)S(1)} custom-call(s32[2]{0:T(128)S(1)} %pad_add_fusion.3.at_ref, bf16[4,1376,512]{2,1,0:T(8,128)(2,1)} %bitcast.34, bf16[4,512,512]{2,1,0:T(8,128)(2,1)S(1)} %copy-done), custom_call_target="tpu_custom_call" | custom-call | flops 10000 | bytes 10000 | tf_op jit(solution)/shard_map/covariances/pallas_call | solution.py:105
  6.2 3.6 %covariances.2 = f32[2,2,2,352,128]{4,3,2,1,0:T(8,128)S(1)} custom-call(s32[2]{0:T(128)S(1)} %pad_add_fusion.2.at_ref, bf16[4,1376,512]{2,1,0:T(8,128)(2,1)} %bitcast.35, bf16[4,512,512]{2,1,0:T(8,128)(2,1)S(1)} %copy-done.1), custom_call_target="tpu_custom_call" | custom-call | flops 10000 | bytes 10000 | tf_op jit(solution)/shard_map/covariances/pallas_call | solution.py:105
  9.9 1.5 %dynamic-slice_add_fusion = (f32[1,2,2,352,128]{4,3,2,1,0:T(8,128)S(1)}, f32[1,2,2,352,128]{4,3,2,1,0:T(8,128)S(1)}) fusion(f32[2,2,2,352,128]{4,3,2,1,0:T(8,128)} %collective-permute-done, s32[]{:T(128)S(6)} %select_n.20, f32[2,2,2,352,128]{4,3,2,1,0:T(8,128)S(1)} %covariances.2, s32[]{:T(128)S(6)} %select_n.19), kind=kLoop, calls=%fused_computation | loop fusion | flops 360448 | bytes 4325384 | tf_op jit(solution)/shard_map/add | solution.py:353
  11.5 2.0 %collective-permute-start.3 = (f16[2,352,128]{2,1,0:T(8,128)(2,1)S(1)}, f16[2,352,128]{2,1,0:T(8,128)(2,1)S(1)}, u32[]{:S(2)}, u32[]{:S(2)}) collective-permute-start(f16[2,352,128]{2,1,0:T(8,128)(2,1)S(1)} %fusion.7), channel_id=1, source_target_pairs={{0,32},{8,40},{16,48},{24,56},{32,0},{40,8},{48,16},{56,24},{64,96... | collective-permute-start | bytes 540680 | tf_op jit(solution)/shard_map/ppermute | solution.py:358
  14.3 0.8 %collective-permute-start.2 = (f16[2,352,128]{2,1,0:T(8,128)(2,1)S(1)}, f16[2,352,128]{2,1,0:T(8,128)(2,1)S(1)}, u32[]{:S(2)}, u32[]{:S(2)}) collective-permute-start(f16[2,352,128]{2,1,0:T(8,128)(2,1)S(1)} %get-tuple-element.16), channel_id=1, source_target_pairs={{0,48},{8,56},{16,32},{24,40},{32,16},{40,24},{48,0},{56,8},{64,11... | collective-permute-start | bytes 540680 | tf_op jit(solution)/shard_map/ppermute | solution.py:356
  15.1 3.9 %collective-permute-done.3 = f16[2,352,128]{2,1,0:T(8,128)(2,1)S(1)} collective-permute-done((f16[2,352,128]{2,1,0:T(8,128)(2,1)S(1)}, f16[2,352,128]{2,1,0:T(8,128)(2,1)S(1)}, u32[]{:S(2)}, u32[]{:S(2)}) %collective-permute-start.3) | collective-permute-done | bytes 180256 | tf_op jit(solution)/shard_map/ppermute | solution.py:358
  19.0 5.0 %collective-permute-done.1 = f16[2,352,128]{2,1,0:T(8,128)(2,1)S(1)} collective-permute-done((f16[2,352,128]{2,1,0:T(8,128)(2,1)S(1)}, f16[2,352,128]{2,1,0:T(8,128)(2,1)S(1)}, u32[]{:S(2)}, u32[]{:S(2)}) %collective-permute-start.1) | collective-permute-done | bytes 180256 | tf_op jit(solution)/shard_map/ppermute | solution.py:357
  24.2 6.4 %collective-permute-start.5 = (f16[208,128]{1,0:T(8,128)(2,1)S(1)}, f16[208,128]{1,0:T(8,128)(2,1)S(1)}, u32[]{:S(2)}, u32[]{:S(2)}) collective-permute-start(f16[208,128]{1,0:T(8,128)(2,1)S(1)} %fusion.14), channel_id=1, source_target_pairs={{0,128},{8,136},{16,144},{24,152},{32,160},{40,168},{48,176},{56,1... | collective-permute-start | bytes 159752 | tf_op jit(solution)/shard_map/ppermute | solution.py:367
  30.6 1.5 %collective-permute-start.4 = (f16[208,128]{1,0:T(8,128)(2,1)S(1)}, f16[208,128]{1,0:T(8,128)(2,1)S(1)}, u32[]{:S(2)}, u32[]{:S(2)}) collective-permute-start(f16[208,128]{1,0:T(8,128)(2,1)S(1)} %get-tuple-element.23), channel_id=1, source_target_pairs={{0,64},{8,72},{16,80},{24,88},{32,96},{40,104},{48,112},{56,120},{... | collective-permute-start | bytes 159752 | tf_op jit(solution)/shard_map/ppermute | solution.py:367
  32.2 2.7 %collective-permute-start.6 = (f16[208,128]{1,0:T(8,128)(2,1)S(1)}, f16[208,128]{1,0:T(8,128)(2,1)S(1)}, u32[]{:S(2)}, u32[]{:S(2)}) collective-permute-start(f16[208,128]{1,0:T(8,128)(2,1)S(1)} %get-tuple-element.24), channel_id=1, source_target_pairs={{0,192},{8,200},{16,208},{24,216},{32,224},{40,232},{48,240},{56,2... | collective-permute-start | bytes 159752 | tf_op jit(solution)/shard_map/ppermute | solution.py:367
  34.9 2.1 %collective-permute-done.4 = f16[208,128]{1,0:T(8,128)(2,1)S(1)} collective-permute-done((f16[208,128]{1,0:T(8,128)(2,1)S(1)}, f16[208,128]{1,0:T(8,128)(2,1)S(1)}, u32[]{:S(2)}, u32[]{:S(2)}) %collective-permute-start.4) | collective-permute-done | bytes 53280 | tf_op jit(solution)/shard_map/ppermute | solution.py:367
  37.8 8.3 %inverse_roots.1 = bf16[176,128]{1,0:T(8,128)(2,1)S(1)} custom-call(s32[1]{0:T(128)} %bitcast.z_ref, f32[208,128]{1,0:T(8,128)S(1)} %fusion.12.total_ref), custom_call_target="tpu_custom_call" | custom-call | flops 10000 | bytes 10000 | tf_op jit(solution)/shard_map/inverse_roots/pallas_call | solution.py:176
  46.2 4.0 %collective-permute-start.9 = (bf16[176,128]{1,0:T(8,128)(2,1)S(1)}, bf16[176,128]{1,0:T(8,128)(2,1)S(1)}, u32[]{:S(2)}, u32[]{:S(2)}) collective-permute-start(bf16[176,128]{1,0:T(8,128)(2,1)S(1)} %inverse_roots.1), channel_id=1, source_target_pairs={{0,192},{8,200},{16,208},{24,216},{32,224},{40,232},{48,240},{56,2... | collective-permute-start | bytes 135176 | tf_op jit(solution)/shard_map/ppermute | solution.py:371
  51.0 1.7 %collective-permute-start.7 = (bf16[176,128]{1,0:T(8,128)(2,1)S(1)}, bf16[176,128]{1,0:T(8,128)(2,1)S(1)}, u32[]{:S(2)}, u32[]{:S(2)}) collective-permute-start(bf16[176,128]{1,0:T(8,128)(2,1)S(1)} %inverse_roots.1), channel_id=1, source_target_pairs={{0,64},{8,72},{16,80},{24,88},{32,96},{40,104},{48,112},{56,120},{... | collective-permute-start | bytes 135176 | tf_op jit(solution)/shard_map/ppermute | solution.py:371
  52.7 5.7 %collective-permute-done.8 = bf16[176,128]{1,0:T(8,128)(2,1)S(1)} collective-permute-done((bf16[176,128]{1,0:T(8,128)(2,1)S(1)}, bf16[176,128]{1,0:T(8,128)(2,1)S(1)}, u32[]{:S(2)}, u32[]{:S(2)}) %collective-permute-start.8) | collective-permute-done | bytes 45088 | tf_op jit(solution)/shard_map/ppermute | solution.py:371
  59.1 1.4 %collective-permute-start.14 = (bf16[704,128]{1,0:T(8,128)(2,1)S(1)}, bf16[704,128]{1,0:T(8,128)(2,1)S(1)}, u32[]{:S(2)}, u32[]{:S(2)}) collective-permute-start(bf16[704,128]{1,0:T(8,128)(2,1)S(1)} %pad_maximum_fusion.1), channel_id=1, source_target_pairs={{0,32},{8,40},{16,48},{24,56},{32,0},{40,8},{48,16},{56,24},{64,96... | collective-permute-start | bytes 540680 | tf_op jit(solution)/shard_map/ppermute | solution.py:375
  60.5 1.5 %collective-permute-start.13 = (bf16[704,128]{1,0:T(8,128)(2,1)S(1)}, bf16[704,128]{1,0:T(8,128)(2,1)S(1)}, u32[]{:S(2)}, u32[]{:S(2)}) collective-permute-start(bf16[704,128]{1,0:T(8,128)(2,1)S(1)} %pad_maximum_fusion.1), channel_id=1, source_target_pairs={{0,16},{8,24},{16,0},{24,8},{32,48},{40,56},{48,32},{56,40},{64,80... | collective-permute-start | bytes 540680 | tf_op jit(solution)/shard_map/ppermute | solution.py:374
  62.3 1.1 %collective-permute-done.10.first_ref = bf16[704,128]{1,0:T(8,128)(2,1)S(1)} collective-permute-done((bf16[704,128]{1,0:T(8,128)(2,1)S(1)}, bf16[704,128]{1,0:T(8,128)(2,1)S(1)}, u32[]{:S(2)}, u32[]{:S(2)}) %collective-permute-start.10) | collective-permute-done | bytes 180256 | tf_op jit(solution)/shard_map/ppermute | solution.py:377
  63.9 5.1 %collective-permute-start.11 = (bf16[144,128]{1,0:T(8,128)(2,1)S(1)}, bf16[144,128]{1,0:T(8,128)(2,1)S(1)}, u32[]{:S(2)}, u32[]{:S(2)}) collective-permute-start(bf16[144,128]{1,0:T(8,128)(2,1)S(1)} %concatenate.30), channel_id=1, source_target_pairs={{0,5},{1,38},{2,67},{3,97},{4,132},{5,167},{6,194},{7,224},{8,13},... | collective-permute-start | bytes 110600 | tf_op jit(solution)/shard_map/ppermute | solution.py:378
  69.2 6.7 %collective-permute-done.12.odd_ref = bf16[144,128]{1,0:T(8,128)(2,1)S(1)} collective-permute-done((bf16[144,128]{1,0:T(8,128)(2,1)S(1)}, bf16[144,128]{1,0:T(8,128)(2,1)S(1)}, u32[]{:S(2)}, u32[]{:S(2)}) %collective-permute-start.12) | collective-permute-done | bytes 36896 | tf_op jit(solution)/shard_map/ppermute | solution.py:378
  75.9 1.0 %collective-permute-done.11.even_ref = bf16[144,128]{1,0:T(8,128)(2,1)S(1)} collective-permute-done((bf16[144,128]{1,0:T(8,128)(2,1)S(1)}, bf16[144,128]{1,0:T(8,128)(2,1)S(1)}, u32[]{:S(2)}, u32[]{:S(2)}) %collective-permute-start.11) | collective-permute-done | bytes 36896 | tf_op jit(solution)/shard_map/ppermute | solution.py:378
  77.0 1.2 %multiply_right.1.mid_ref = f32[4,1376,128]{2,1,0:T(8,128)S(1)} custom-call(s32[2]{0:T(128)S(1)} %pad_add_fusion.1.at_ref, bf16[4,1376,128]{2,1,0:T(8,128)(2,1)S(1)} %copy-done.4, bf16[144,128]{1,0:T(8,128)(2,1)S(1)} %collective-permute-done.11.even_ref, bf16[144,128]{1,0:T(8,128)(2,1)S(1)} %collective-permute-done.12.odd_ref), custom_call_target="tpu_custom_call" | custom-call | flops 20000000000 | bytes 6000000 | tf_op jit(solution)/shard_map/multiply_right/pallas_call | solution.py:216
  78.2 3.6 %apply_roots.1 = (bf16[4,1376,128]{2,1,0:T(8,128)(2,1)}, bf16[172,2,172]{2,1,0:T(2,128)(2,1)}, bf16[2,128,128]{2,1,0:T(8,128)(2,1)}) custom-call(s32[3]{0:T(128)S(1)} %pad_add_fusion.at_ref, s32[4,8]{1,0:T(4,128)S(1)} %copy-done.2, s32[4,4]{1,0:T(4,128)S(1)} %copy-done.3, f32[4,1376,128]{2,1,0:T(8,128)S(1)} %multiply_right.1.mid_ref, ...), custom_call_target="tpu_custom_call" | custom-call | flops 10000 | bytes 10000 | tf_op jit(solution)/shard_map/apply_roots/pallas_call | solution.py:284
  (57 shorter events, 4.5 us)
Async XLA Ops:
  0.7 1.6 %copy-start = (bf16[4,512,512]{2,1,0:T(8,128)(2,1)S(1)}, bf16[4,512,512]{2,1,0:T(8,128)(2,1)}, u32[]{:S(2)}) copy-start(bf16[4,512,512]{2,1,0:T(8,128)(2,1)} %g_ref.3) | copy-start | bytes 6291460
  2.3 3.9 %copy-start.1 = (bf16[4,512,512]{2,1,0:T(8,128)(2,1)S(1)}, bf16[4,512,512]{2,1,0:T(8,128)(2,1)}, u32[]{:S(2)}) copy-start(bf16[4,512,512]{2,1,0:T(8,128)(2,1)} %g_ref.3) | copy-start | bytes 6291460
  6.0 3.9 %collective-permute-start = (f32[2,2,2,352,128]{4,3,2,1,0:T(8,128)S(1)}, f32[2,2,2,352,128]{4,3,2,1,0:T(8,128)}, u32[]{:S(2)}, u32[]{:S(2)}) collective-permute-start(f32[2,2,2,352,128]{4,3,2,1,0:T(8,128)S(1)} %covariances.3), channel_id=1, source_target_pairs={{0,8},{8,0},{16,24},{24,16},{32,40},{40,32},{48,56},{56,48},{64,72... | collective-permute-start | bytes 4325384 | tf_op jit(solution)/shard_map/ppermute | solution.py:348
  11.5 7.5 %collective-permute-start.3 = (f16[2,352,128]{2,1,0:T(8,128)(2,1)S(1)}, f16[2,352,128]{2,1,0:T(8,128)(2,1)S(1)}, u32[]{:S(2)}, u32[]{:S(2)}) collective-permute-start(f16[2,352,128]{2,1,0:T(8,128)(2,1)S(1)} %fusion.7), channel_id=1, source_target_pairs={{0,32},{8,40},{16,48},{24,56},{32,0},{40,8},{48,16},{56,24},{64,96... | collective-permute-start | bytes 540680 | tf_op jit(solution)/shard_map/ppermute | solution.py:358
  13.5 10.5 %collective-permute-start.1 = (f16[2,352,128]{2,1,0:T(8,128)(2,1)S(1)}, f16[2,352,128]{2,1,0:T(8,128)(2,1)S(1)}, u32[]{:S(2)}, u32[]{:S(2)}) collective-permute-start(f16[2,352,128]{2,1,0:T(8,128)(2,1)S(1)} %get-tuple-element.15), channel_id=1, source_target_pairs={{0,16},{8,24},{16,0},{24,8},{32,48},{40,56},{48,32},{56,40},{64,80... | collective-permute-start | bytes 540680 | tf_op jit(solution)/shard_map/ppermute | solution.py:357
  14.3 9.8 %collective-permute-start.2 = (f16[2,352,128]{2,1,0:T(8,128)(2,1)S(1)}, f16[2,352,128]{2,1,0:T(8,128)(2,1)S(1)}, u32[]{:S(2)}, u32[]{:S(2)}) collective-permute-start(f16[2,352,128]{2,1,0:T(8,128)(2,1)S(1)} %get-tuple-element.16), channel_id=1, source_target_pairs={{0,48},{8,56},{16,32},{24,40},{32,16},{40,24},{48,0},{56,8},{64,11... | collective-permute-start | bytes 540680 | tf_op jit(solution)/shard_map/ppermute | solution.py:356
  24.2 10.7 %collective-permute-start.5 = (f16[208,128]{1,0:T(8,128)(2,1)S(1)}, f16[208,128]{1,0:T(8,128)(2,1)S(1)}, u32[]{:S(2)}, u32[]{:S(2)}) collective-permute-start(f16[208,128]{1,0:T(8,128)(2,1)S(1)} %fusion.14), channel_id=1, source_target_pairs={{0,128},{8,136},{16,144},{24,152},{32,160},{40,168},{48,176},{56,1... | collective-permute-start | bytes 159752 | tf_op jit(solution)/shard_map/ppermute | solution.py:367
  30.6 6.4 %collective-permute-start.4 = (f16[208,128]{1,0:T(8,128)(2,1)S(1)}, f16[208,128]{1,0:T(8,128)(2,1)S(1)}, u32[]{:S(2)}, u32[]{:S(2)}) collective-permute-start(f16[208,128]{1,0:T(8,128)(2,1)S(1)} %get-tuple-element.23), channel_id=1, source_target_pairs={{0,64},{8,72},{16,80},{24,88},{32,96},{40,104},{48,112},{56,120},{... | collective-permute-start | bytes 159752 | tf_op jit(solution)/shard_map/ppermute | solution.py:367
  32.2 5.5 %collective-permute-start.6 = (f16[208,128]{1,0:T(8,128)(2,1)S(1)}, f16[208,128]{1,0:T(8,128)(2,1)S(1)}, u32[]{:S(2)}, u32[]{:S(2)}) collective-permute-start(f16[208,128]{1,0:T(8,128)(2,1)S(1)} %get-tuple-element.24), channel_id=1, source_target_pairs={{0,192},{8,200},{16,208},{24,216},{32,224},{40,232},{48,240},{56,2... | collective-permute-start | bytes 159752 | tf_op jit(solution)/shard_map/ppermute | solution.py:367
  46.2 6.5 %collective-permute-start.9 = (bf16[176,128]{1,0:T(8,128)(2,1)S(1)}, bf16[176,128]{1,0:T(8,128)(2,1)S(1)}, u32[]{:S(2)}, u32[]{:S(2)}) collective-permute-start(bf16[176,128]{1,0:T(8,128)(2,1)S(1)} %inverse_roots.1), channel_id=1, source_target_pairs={{0,192},{8,200},{16,208},{24,216},{32,224},{40,232},{48,240},{56,2... | collective-permute-start | bytes 135176 | tf_op jit(solution)/shard_map/ppermute | solution.py:371
  50.2 8.2 %collective-permute-start.8 = (bf16[176,128]{1,0:T(8,128)(2,1)S(1)}, bf16[176,128]{1,0:T(8,128)(2,1)S(1)}, u32[]{:S(2)}, u32[]{:S(2)}) collective-permute-start(bf16[176,128]{1,0:T(8,128)(2,1)S(1)} %inverse_roots.1), channel_id=1, source_target_pairs={{0,128},{8,136},{16,144},{24,152},{32,160},{40,168},{48,176},{56,1... | collective-permute-start | bytes 135176 | tf_op jit(solution)/shard_map/ppermute | solution.py:371
  51.0 7.4 %collective-permute-start.7 = (bf16[176,128]{1,0:T(8,128)(2,1)S(1)}, bf16[176,128]{1,0:T(8,128)(2,1)S(1)}, u32[]{:S(2)}, u32[]{:S(2)}) collective-permute-start(bf16[176,128]{1,0:T(8,128)(2,1)S(1)} %inverse_roots.1), channel_id=1, source_target_pairs={{0,64},{8,72},{16,80},{24,88},{32,96},{40,104},{48,112},{56,120},{... | collective-permute-start | bytes 135176 | tf_op jit(solution)/shard_map/ppermute | solution.py:371
  52.7 24.3 %copy-start.4 = (bf16[4,1376,128]{2,1,0:T(8,128)(2,1)S(1)}, bf16[4,1376,128]{2,1,0:T(8,128)(2,1)}, u32[]{:S(2)}) copy-start(bf16[4,1376,128]{2,1,0:T(8,128)(2,1)} %w_ref.1) | copy-start | bytes 4227076
  58.4 10.5 %collective-permute-start.15 = (bf16[704,128]{1,0:T(8,128)(2,1)S(1)}, bf16[704,128]{1,0:T(8,128)(2,1)S(1)}, u32[]{:S(2)}, u32[]{:S(2)}) collective-permute-start(bf16[704,128]{1,0:T(8,128)(2,1)S(1)} %pad_maximum_fusion.1), channel_id=1, source_target_pairs={{0,48},{8,56},{16,32},{24,40},{32,16},{40,24},{48,0},{56,8},{64,11... | collective-permute-start | bytes 540680 | tf_op jit(solution)/shard_map/ppermute | solution.py:376
  59.1 9.9 %collective-permute-start.14 = (bf16[704,128]{1,0:T(8,128)(2,1)S(1)}, bf16[704,128]{1,0:T(8,128)(2,1)S(1)}, u32[]{:S(2)}, u32[]{:S(2)}) collective-permute-start(bf16[704,128]{1,0:T(8,128)(2,1)S(1)} %pad_maximum_fusion.1), channel_id=1, source_target_pairs={{0,32},{8,40},{16,48},{24,56},{32,0},{40,8},{48,16},{56,24},{64,96... | collective-permute-start | bytes 540680 | tf_op jit(solution)/shard_map/ppermute | solution.py:375
  60.5 8.5 %collective-permute-start.13 = (bf16[704,128]{1,0:T(8,128)(2,1)S(1)}, bf16[704,128]{1,0:T(8,128)(2,1)S(1)}, u32[]{:S(2)}, u32[]{:S(2)}) collective-permute-start(bf16[704,128]{1,0:T(8,128)(2,1)S(1)} %pad_maximum_fusion.1), channel_id=1, source_target_pairs={{0,16},{8,24},{16,0},{24,8},{32,48},{40,56},{48,32},{56,40},{64,80... | collective-permute-start | bytes 540680 | tf_op jit(solution)/shard_map/ppermute | solution.py:374
  62.0 1.4 %collective-permute-start.10 = (bf16[704,128]{1,0:T(8,128)(2,1)S(1)}, bf16[704,128]{1,0:T(8,128)(2,1)S(1)}, u32[]{:S(2)}, u32[]{:S(2)}) collective-permute-start(bf16[704,128]{1,0:T(8,128)(2,1)S(1)} %pad_maximum_fusion.1), channel_id=1, source_target_pairs={{0,8},{8,0},{16,24},{24,16},{32,40},{40,32},{48,56},{56,48},{64,72... | collective-permute-start | bytes 540680 | tf_op jit(solution)/shard_map/ppermute | solution.py:377
  63.4 12.5 %collective-permute-start.12 = (bf16[144,128]{1,0:T(8,128)(2,1)S(1)}, bf16[144,128]{1,0:T(8,128)(2,1)S(1)}, u32[]{:S(2)}, u32[]{:S(2)}) collective-permute-start(bf16[144,128]{1,0:T(8,128)(2,1)S(1)} %concatenate.30), channel_id=1, source_target_pairs={{0,3},{1,36},{2,65},{3,98},{4,130},{5,165},{6,192},{7,227},{8,11},... | collective-permute-start | bytes 110600 | tf_op jit(solution)/shard_map/ppermute | solution.py:378
  63.9 13.1 %collective-permute-start.11 = (bf16[144,128]{1,0:T(8,128)(2,1)S(1)}, bf16[144,128]{1,0:T(8,128)(2,1)S(1)}, u32[]{:S(2)}, u32[]{:S(2)}) collective-permute-start(bf16[144,128]{1,0:T(8,128)(2,1)S(1)} %concatenate.30), channel_id=1, source_target_pairs={{0,5},{1,38},{2,67},{3,97},{4,132},{5,167},{6,194},{7,224},{8,13},... | collective-permute-start | bytes 110600 | tf_op jit(solution)/shard_map/ppermute | solution.py:378
  69.0 9.2 %collective-permute-start.16 = (bf16[2112,128]{1,0:T(8,128)(2,1)S(1)}, bf16[2112,128]{1,0:T(8,128)(2,1)S(1)}, u32[]{:S(2)}, u32[]{:S(2)}) collective-permute-start(bf16[2112,128]{1,0:T(8,128)(2,1)S(1)} %pad_maximum_fusion), channel_id=1, source_target_pairs={{0,8},{8,0},{16,24},{24,16},{32,40},{40,32},{48,56},{56,48},{64,72... | collective-permute-start | bytes 1622024 | tf_op jit(solution)/shard_map/ppermute | solution.py:380
  69.2 9.0 %copy-start.2 = (s32[4,8]{1,0:T(4,128)S(1)}, s32[4,8]{1,0:T(4,128)}, u32[]{:S(2)}) copy-start(s32[4,8]{1,0:T(4,128)} %oa_ref.1) | copy-start | bytes 388
  69.2 9.0 %copy-start.3 = (s32[4,4]{1,0:T(4,128)S(1)}, s32[4,4]{1,0:T(4,128)}, u32[]{:S(2)}) copy-start(s32[4,4]{1,0:T(4,128)} %og_ref.1) | copy-start | bytes 196

commit v4 on v3

--- a/solution.py
+++ b/solution.py
@@ -19,12 +19,14 @@
 PAIR = RA + RG + RA
 DIAG = 136
 GATHERED = RA + RG // 2
+TAIL = 128
 TAILS = 144
 WIRE = jnp.float16
 WIRE_SCALE = 256.0
 
 damping_share = 0.01
 
+SMALL = pltpu.CompilerParams(vmem_limit_bytes=24 << 20)
 CHEAP = pl.CostEstimate(flops=10**4, bytes_accessed=10**4, transcendentals=0)
 PARAMS = pltpu.CompilerParams(vmem_limit_bytes=48 << 20)
 
@@ -222,7 +224,7 @@
             pltpu.VMEM((8, RG // 2, BG), jnp.float32),
             pltpu.VMEM((8, 1, BG), jnp.float32),
         ],
-        compiler_params=PARAMS,
+        compiler_params=SMALL,
         cost_estimate=pl.CostEstimate(
             flops=2 * 10**10, bytes_accessed=6 * 10**6, transcendentals=0
         ),
@@ -230,8 +232,36 @@
     )(at, weight_grad, even, odd)
 
 
+def unpack_kernel(*refs):
+    full_ref, tails_ref = refs[-2:]
+    slot = 0
+    for ref in refs[:-2]:
+        for start in range(0, ref.shape[0], GATHERED):
+            packed = ref[start : start + RA].astype(jnp.float32)
+            full_ref[slot] = unpack_wide(packed).astype(jnp.bfloat16)
+            tails_ref[slot] = ref[start + TAIL : start + GATHERED]
+            slot += 1
+
+
+def unpack_roots(*messages):
+    whole = pl.BlockSpec(memory_space=pltpu.VMEM)
+    return pl.pallas_call(
+        unpack_kernel,
+        in_specs=[whole] * len(messages),
+        out_specs=[whole] * 2,
+        out_shape=[
+            jax.ShapeDtypeStruct((16, 176, 256), jnp.bfloat16),
+            jax.ShapeDtypeStruct((16, GATHERED - TAIL, BG), jnp.bfloat16),
+        ],
+        compiler_params=SMALL,
+        cost_estimate=CHEAP,
+        name="unpack_roots",
+    )(*messages)
+
+
 def apply_kernel(
-    at_ref, oa_ref, og_ref, mid_ref, own_ref, first_ref, rest_ref, out_ref, sa_ref, sg_ref, a_ref
+    at_ref, oa_ref, og_ref, mid_ref, full0_ref, full1_ref, tails0_ref, tails1_ref,
+    out_ref, sa_ref, sg_ref,
 ):
     z, y, c = (at_ref[i] for i in range(3))
     position = 4 * z + 2 * y + c
@@ -242,29 +272,31 @@
         turn = (((z ^ odd) - z_of) & 7) >> 1
         return c_of ^ c, 8 * odd + 4 * (y_of ^ y) + turn
 
-    for slot in range(16):
-        a_ref[0, slot] = own_ref[GATHERED * slot : GATHERED * (slot + 1)]
-        ref, start = (first_ref, slot) if slot < 4 else (rest_ref, slot - 4)
-        a_ref[1, slot] = ref[GATHERED * start : GATHERED * (start + 1)]
-    for layer in range(LAYERS):
-        for quad in range(2):
-            results = []
-            for k in range(4 * quad, 4 * quad + 4):
-                i, slot = place(k, layer % 2, layer // 2)
-                left = unpack_wide(a_ref[i, slot, 0:RA].astype(jnp.float32))
-                left = left[0:BA, 0:BA].astype(jnp.bfloat16)
-                x = mid_ref[layer, BA * k : BA * (k + 1)].astype(jnp.bfloat16)
-                results.append(jnp.dot(left, x, preferred_element_type=jnp.float32))
-            out_ref[layer, 4 * BA * quad : 4 * BA * (quad + 1)] = jnp.concatenate(
-                results, axis=0
-            ).astype(jnp.bfloat16)
+    for beside, full_ref in enumerate((full0_ref, full1_ref)):
+        for odd in range(2):
+            layer = 2 * (c ^ beside) + odd
+            for quad in range(2):
+                results = []
+                for k in range(4 * quad, 4 * quad + 4):
+                    _, slot = place(k, odd, c ^ beside)
+                    left = full_ref[slot, 0:BA, 0:BA]
+                    x = mid_ref[layer, BA * k : BA * (k + 1)].astype(jnp.bfloat16)
+                    results.append(jnp.dot(left, x, preferred_element_type=jnp.float32))
+                out_ref[layer, 4 * BA * quad : 4 * BA * (quad + 1)] = jnp.concatenate(
+                    results, axis=0
+                ).astype(jnp.bfloat16)
+
+    def chosen(beside, slot, own_ref, other_ref):
+        own, other = own_ref[slot].astype(jnp.float32), other_ref[slot].astype(jnp.float32)
+        return jnp.where(beside == 0, own, other)
+
     stored = []
     for r in range(2):
         block = owned_a[r]
         held = jnp.maximum(block, 0)
         layer = held >> 3
         i, slot = place(held & 7, layer & 1, layer >> 1)
-        root = unpack_wide(a_ref[i, slot, 0:RA].astype(jnp.float32))[0:BA, 0:BA]
+        root = chosen(i, slot, full0_ref, full1_ref)[0:BA, 0:BA]
         stored.append(jnp.where(block >= 0, root, 0.0))
         block = owned_g[r]
         held = jnp.maximum(block, 0)
@@ -272,8 +304,8 @@
         halves = []
         for half in range(2):
             i, slot = place(layer + 4 * half, k >> 1, k & 1)
-            halves.append(a_ref[i, slot, RA - 16 : GATHERED].astype(jnp.float32))
-        spare = halves[0][DIAG - RA + 16 : DIAG - RA + 17]
+            halves.append(chosen(i, slot, tails0_ref, tails1_ref))
+        spare = halves[0][DIAG - TAIL : DIAG - TAIL + 1]
         root = unpack_halves(halves[0][16:48], halves[1][16:48], spare)
         sg_ref[r] = jnp.where(block >= 0, root, 0.0).astype(jnp.bfloat16)
     sa_ref[...] = jnp.stack(stored, axis=1).astype(jnp.bfloat16)
@@ -283,15 +315,14 @@
     whole = pl.BlockSpec(memory_space=pltpu.VMEM)
     return pl.pallas_call(
         apply_kernel,
-        in_specs=[pl.BlockSpec(memory_space=pltpu.SMEM)] * 3 + [whole] * 4,
+        in_specs=[pl.BlockSpec(memory_space=pltpu.SMEM)] * 3 + [whole] * 5,
         out_specs=[whole] * 3,
         out_shape=[
             jax.ShapeDtypeStruct(mid.shape, jnp.bfloat16),
             jax.ShapeDtypeStruct((BA, 2, BA), jnp.bfloat16),
             jax.ShapeDtypeStruct((2, BG, BG), jnp.bfloat16),
         ],
-        scratch_shapes=[pltpu.VMEM((2, 16, GATHERED, BG), jnp.bfloat16)],
-        compiler_params=PARAMS,
+        compiler_params=SMALL,
         cost_estimate=CHEAP,
         name="apply_roots",
     )(at, owner_a, owner_g, mid, *gathered)
@@ -380,9 +411,11 @@
     rest = lax.ppermute(gathered[4 * GATHERED :], "dp", OVER_CORE)
 
     at = jnp.stack([z, y, core])
+    full_own, tails_own = unpack_roots(gathered)
+    full_beside, tails_beside = unpack_roots(first, rest)
     mid = multiply_right(jnp.stack([z, column]), weight_grad, *tails)
     precond_grad, store_a, store_g = apply_roots(
-        at, owner_a, gradient_block_owner, mid, gathered, first, rest
+        at, owner_a, gradient_block_owner, mid, full_own, full_beside, tails_own, tails_beside
     )
     return precond_grad, jnp.swapaxes(store_a, 0, 1)[None, None], store_g[None, None]
 

time: 82 us -> 82.2 us (level)
    pallas_call x0 -> x2, Pallas kernels: none -> 1.36 us  [unpack_roots(): pl.pallas_call(unpack_kernel, in_specs=[whole] * len(messages), out_specs...]
  transfers between devices with their start and end apart: 17 -> 17, of which waited for: 8 -> 8; matrix products, arithmetic and copies ran while one was open for 1% -> 1% of each run, Pallas kernels for 6% -> 7%
where the time goes in v4:
time: 82.2 us; the launch traced here: 82 us
  starting transfers between devices  29.9 us (36%)
  waiting for transfers between devices  25.6 us (31%)
  Pallas kernels  21.4 us (26%)
  other arithmetic  2.12 us (3%)
  local copies, waits for them, and re-layouts  1.97 us (2%)
  between operations  0.97 us (1%)
    ppermute x3, starting transfers between devices, shards(): lax.ppermute(narrow(message(t)), 'dp', along_z(2 * t))  10.6 us
    pallas_call x1, Pallas kernels, inverse_roots(): pl.pallas_call(roots_kernel, in_specs=[pl.BlockSpec(memory_space=pltpu.SM...  8.35 us
    pallas_call x2, Pallas kernels, covariances(): pl.pallas_call(functools.partial(cov_kernel, scale), grid_spec=pltpu.Pref...  7.36 us
    ppermute x2, waiting for transfers between devices, shards(): lax.ppermute(tails, ('dp', 'grp'), pairs)  7.02 us
    ppermute x3, starting transfers between devices, shards(): lax.ppermute(packed, 'dp', along_z(2 * t))  6.48 us
    ppermute x3, waiting for transfers between devices, shards(): lax.ppermute(packed, 'dp', along_z(2 * t))  5.73 us
    ppermute x2, starting transfers between devices, shards(): lax.ppermute(tails, ('dp', 'grp'), pairs)  5.53 us
    ppermute x1, waiting for transfers between devices, shards(): got_y = lax.ppermute(narrow(other[0]), 'dp', OVER_Y)  5.03 us
  transfers between devices with their start and end apart: 17, of which 8 were waited for; matrix products, arithmetic and copies ran while one was open for 1% of the time, Pallas kernels for 7%

profile of v4, /device:TPU:30, one launch (start us, length us, event | category | flops | bytes accessed | tf_op | source)
XLA Modules:
  0.0 82.0 jit_solution(3115381306370294858)
XLA Ops:
  0.7 1.6 %copy-done = bf16[4,512,512]{2,1,0:T(8,128)(2,1)S(1)} copy-done((bf16[4,512,512]{2,1,0:T(8,128)(2,1)S(1)}, bf16[4,512,512]{2,1,0:T(8,128)(2,1)}, u32[]{:S(2)}) %copy-start) | copy-done | bytes 2097176
  2.3 3.7 %covariances.3 = f32[2,2,2,352,128]{4,3,2,1,0:T(8,128)S(1)} custom-call(s32[2]{0:T(128)S(1)} %pad_add_fusion.3.at_ref, bf16[4,1376,512]{2,1,0:T(8,128)(2,1)} %bitcast.34, bf16[4,512,512]{2,1,0:T(8,128)(2,1)S(1)} %copy-done), custom_call_target="tpu_custom_call" | custom-call | flops 10000 | bytes 10000 | tf_op jit(solution)/shard_map/covariances/pallas_call | solution.py:107
  6.2 3.6 %covariances.2 = f32[2,2,2,352,128]{4,3,2,1,0:T(8,128)S(1)} custom-call(s32[2]{0:T(128)S(1)} %pad_add_fusion.2.at_ref, bf16[4,1376,512]{2,1,0:T(8,128)(2,1)} %bitcast.35, bf16[4,512,512]{2,1,0:T(8,128)(2,1)S(1)} %copy-done.1), custom_call_target="tpu_custom_call" | custom-call | flops 10000 | bytes 10000 | tf_op jit(solution)/shard_map/covariances/pallas_call | solution.py:107
  9.9 1.5 %dynamic-slice_add_fusion = (f32[1,2,2,352,128]{4,3,2,1,0:T(8,128)S(1)}, f32[1,2,2,352,128]{4,3,2,1,0:T(8,128)S(1)}) fusion(f32[2,2,2,352,128]{4,3,2,1,0:T(8,128)} %collective-permute-done, s32[]{:T(128)S(6)} %select_n.20, f32[2,2,2,352,128]{4,3,2,1,0:T(8,128)S(1)} %covariances.2, s32[]{:T(128)S(6)} %select_n.19), kind=kLoop, calls=%fused_computation | loop fusion | flops 360448 | bytes 4325384 | tf_op jit(solution)/shard_map/add | solution.py:384
  11.5 2.0 %collective-permute-start.3 = (f16[2,352,128]{2,1,0:T(8,128)(2,1)S(1)}, f16[2,352,128]{2,1,0:T(8,128)(2,1)S(1)}, u32[]{:S(2)}, u32[]{:S(2)}) collective-permute-start(f16[2,352,128]{2,1,0:T(8,128)(2,1)S(1)} %fusion.7), channel_id=1, source_target_pairs={{0,32},{8,40},{16,48},{24,56},{32,0},{40,8},{48,16},{56,24},{64,96... | collective-permute-start | bytes 540680 | tf_op jit(solution)/shard_map/ppermute | solution.py:389
  14.3 0.8 %collective-permute-start.2 = (f16[2,352,128]{2,1,0:T(8,128)(2,1)S(1)}, f16[2,352,128]{2,1,0:T(8,128)(2,1)S(1)}, u32[]{:S(2)}, u32[]{:S(2)}) collective-permute-start(f16[2,352,128]{2,1,0:T(8,128)(2,1)S(1)} %get-tuple-element.24), channel_id=1, source_target_pairs={{0,48},{8,56},{16,32},{24,40},{32,16},{40,24},{48,0},{56,8},{64,11... | collective-permute-start | bytes 540680 | tf_op jit(solution)/shard_map/ppermute | solution.py:387
  15.1 3.9 %collective-permute-done.3 = f16[2,352,128]{2,1,0:T(8,128)(2,1)S(1)} collective-permute-done((f16[2,352,128]{2,1,0:T(8,128)(2,1)S(1)}, f16[2,352,128]{2,1,0:T(8,128)(2,1)S(1)}, u32[]{:S(2)}, u32[]{:S(2)}) %collective-permute-start.3) | collective-permute-done | bytes 180256 | tf_op jit(solution)/shard_map/ppermute | solution.py:389
  19.0 5.0 %collective-permute-done.1 = f16[2,352,128]{2,1,0:T(8,128)(2,1)S(1)} collective-permute-done((f16[2,352,128]{2,1,0:T(8,128)(2,1)S(1)}, f16[2,352,128]{2,1,0:T(8,128)(2,1)S(1)}, u32[]{:S(2)}, u32[]{:S(2)}) %collective-permute-start.1) | collective-permute-done | bytes 180256 | tf_op jit(solution)/shard_map/ppermute | solution.py:388
  24.2 6.4 %collective-permute-start.5 = (f16[208,128]{1,0:T(8,128)(2,1)S(1)}, f16[208,128]{1,0:T(8,128)(2,1)S(1)}, u32[]{:S(2)}, u32[]{:S(2)}) collective-permute-start(f16[208,128]{1,0:T(8,128)(2,1)S(1)} %fusion.14), channel_id=1, source_target_pairs={{0,128},{8,136},{16,144},{24,152},{32,160},{40,168},{48,176},{56,1... | collective-permute-start | bytes 159752 | tf_op jit(solution)/shard_map/ppermute | solution.py:398
  30.6 1.5 %collective-permute-start.4 = (f16[208,128]{1,0:T(8,128)(2,1)S(1)}, f16[208,128]{1,0:T(8,128)(2,1)S(1)}, u32[]{:S(2)}, u32[]{:S(2)}) collective-permute-start(f16[208,128]{1,0:T(8,128)(2,1)S(1)} %get-tuple-element.31), channel_id=1, source_target_pairs={{0,64},{8,72},{16,80},{24,88},{32,96},{40,104},{48,112},{56,120},{... | collective-permute-start | bytes 159752 | tf_op jit(solution)/shard_map/ppermute | solution.py:398
  32.2 2.7 %collective-permute-start.6 = (f16[208,128]{1,0:T(8,128)(2,1)S(1)}, f16[208,128]{1,0:T(8,128)(2,1)S(1)}, u32[]{:S(2)}, u32[]{:S(2)}) collective-permute-start(f16[208,128]{1,0:T(8,128)(2,1)S(1)} %get-tuple-element.32), channel_id=1, source_target_pairs={{0,192},{8,200},{16,208},{24,216},{32,224},{40,232},{48,240},{56,2... | collective-permute-start | bytes 159752 | tf_op jit(solution)/shard_map/ppermute | solution.py:398
  34.9 2.1 %collective-permute-done.4 = f16[208,128]{1,0:T(8,128)(2,1)S(1)} collective-permute-done((f16[208,128]{1,0:T(8,128)(2,1)S(1)}, f16[208,128]{1,0:T(8,128)(2,1)S(1)}, u32[]{:S(2)}, u32[]{:S(2)}) %collective-permute-start.4) | collective-permute-done | bytes 53280 | tf_op jit(solution)/shard_map/ppermute | solution.py:398
  37.8 8.3 %inverse_roots.1 = bf16[176,128]{1,0:T(8,128)(2,1)S(1)} custom-call(s32[1]{0:T(128)} %bitcast.z_ref, f32[208,128]{1,0:T(8,128)S(1)} %fusion.12.total_ref), custom_call_target="tpu_custom_call" | custom-call | flops 10000 | bytes 10000 | tf_op jit(solution)/shard_map/inverse_roots/pallas_call | solution.py:178
  46.2 4.0 %collective-permute-start.9 = (bf16[176,128]{1,0:T(8,128)(2,1)S(1)}, bf16[176,128]{1,0:T(8,128)(2,1)S(1)}, u32[]{:S(2)}, u32[]{:S(2)}) collective-permute-start(bf16[176,128]{1,0:T(8,128)(2,1)S(1)} %inverse_roots.1), channel_id=1, source_target_pairs={{0,192},{8,200},{16,208},{24,216},{32,224},{40,232},{48,240},{56,2... | collective-permute-start | bytes 135176 | tf_op jit(solution)/shard_map/ppermute | solution.py:402
  51.0 1.7 %collective-permute-start.7 = (bf16[176,128]{1,0:T(8,128)(2,1)S(1)}, bf16[176,128]{1,0:T(8,128)(2,1)S(1)}, u32[]{:S(2)}, u32[]{:S(2)}) collective-permute-start(bf16[176,128]{1,0:T(8,128)(2,1)S(1)} %inverse_roots.1), channel_id=1, source_target_pairs={{0,64},{8,72},{16,80},{24,88},{32,96},{40,104},{48,112},{56,120},{... | collective-permute-start | bytes 135176 | tf_op jit(solution)/shard_map/ppermute | solution.py:402
  52.7 5.7 %collective-permute-done.8 = bf16[176,128]{1,0:T(8,128)(2,1)S(1)} collective-permute-done((bf16[176,128]{1,0:T(8,128)(2,1)S(1)}, bf16[176,128]{1,0:T(8,128)(2,1)S(1)}, u32[]{:S(2)}, u32[]{:S(2)}) %collective-permute-start.8) | collective-permute-done | bytes 45088 | tf_op jit(solution)/shard_map/ppermute | solution.py:402
  59.1 1.4 %collective-permute-start.14 = (bf16[704,128]{1,0:T(8,128)(2,1)S(1)}, bf16[704,128]{1,0:T(8,128)(2,1)S(1)}, u32[]{:S(2)}, u32[]{:S(2)}) collective-permute-start(bf16[704,128]{1,0:T(8,128)(2,1)S(1)} %pad_maximum_fusion.1), channel_id=1, source_target_pairs={{0,32},{8,40},{16,48},{24,56},{32,0},{40,8},{48,16},{56,24},{64,96... | collective-permute-start | bytes 540680 | tf_op jit(solution)/shard_map/ppermute | solution.py:406
  60.5 1.5 %collective-permute-start.13 = (bf16[704,128]{1,0:T(8,128)(2,1)S(1)}, bf16[704,128]{1,0:T(8,128)(2,1)S(1)}, u32[]{:S(2)}, u32[]{:S(2)}) collective-permute-start(bf16[704,128]{1,0:T(8,128)(2,1)S(1)} %pad_maximum_fusion.1), channel_id=1, source_target_pairs={{0,16},{8,24},{16,0},{24,8},{32,48},{40,56},{48,32},{56,40},{64,80... | collective-permute-start | bytes 540680 | tf_op jit(solution)/shard_map/ppermute | solution.py:405
  62.3 1.1 %collective-permute-done.10.refs_0_ = bf16[704,128]{1,0:T(8,128)(2,1)S(1)} collective-permute-done((bf16[704,128]{1,0:T(8,128)(2,1)S(1)}, bf16[704,128]{1,0:T(8,128)(2,1)S(1)}, u32[]{:S(2)}, u32[]{:S(2)}) %collective-permute-start.10) | collective-permute-done | bytes 180256 | tf_op jit(solution)/shard_map/ppermute | solution.py:408
  63.9 5.1 %collective-permute-start.11 = (bf16[144,128]{1,0:T(8,128)(2,1)S(1)}, bf16[144,128]{1,0:T(8,128)(2,1)S(1)}, u32[]{:S(2)}, u32[]{:S(2)}) collective-permute-start(bf16[144,128]{1,0:T(8,128)(2,1)S(1)} %concatenate.30), channel_id=1, source_target_pairs={{0,5},{1,38},{2,67},{3,97},{4,132},{5,167},{6,194},{7,224},{8,13},... | collective-permute-start | bytes 110600 | tf_op jit(solution)/shard_map/ppermute | solution.py:409
  69.9 6.0 %collective-permute-done.12.odd_ref = bf16[144,128]{1,0:T(8,128)(2,1)S(1)} collective-permute-done((bf16[144,128]{1,0:T(8,128)(2,1)S(1)}, bf16[144,128]{1,0:T(8,128)(2,1)S(1)}, u32[]{:S(2)}, u32[]{:S(2)}) %collective-permute-start.12) | collective-permute-done | bytes 36896 | tf_op jit(solution)/shard_map/ppermute | solution.py:409
  75.9 1.0 %collective-permute-done.11.even_ref = bf16[144,128]{1,0:T(8,128)(2,1)S(1)} collective-permute-done((bf16[144,128]{1,0:T(8,128)(2,1)S(1)}, bf16[144,128]{1,0:T(8,128)(2,1)S(1)}, u32[]{:S(2)}, u32[]{:S(2)}) %collective-permute-start.11) | collective-permute-done | bytes 36896 | tf_op jit(solution)/shard_map/ppermute | solution.py:409
  77.0 1.2 %multiply_right.1.mid_ref = f32[4,1376,128]{2,1,0:T(8,128)S(1)} custom-call(s32[2]{0:T(128)S(1)} %pad_add_fusion.1.at_ref, bf16[4,1376,128]{2,1,0:T(8,128)(2,1)S(1)} %copy-done.4, bf16[144,128]{1,0:T(8,128)(2,1)S(1)} %collective-permute-done.11.even_ref, bf16[144,128]{1,0:T(8,128)(2,1)S(1)} %collective-permute-done.12.odd_ref), custom_call_target="tpu_custom_call" | custom-call | flops 20000000000 | bytes 6000000 | tf_op jit(solution)/shard_map/multiply_right/pallas_call | solution.py:218
  78.9 3.1 %apply_roots.1 = (bf16[4,1376,128]{2,1,0:T(8,128)(2,1)}, bf16[172,2,172]{2,1,0:T(2,128)(2,1)}, bf16[2,128,128]{2,1,0:T(8,128)(2,1)}) custom-call(s32[3]{0:T(128)S(1)} %pad_add_fusion.at_ref, s32[4,8]{1,0:T(4,128)S(1)} %copy-done.2, s32[4,4]{1,0:T(4,128)S(1)} %copy-done.3, f32[4,1376,128]{2,1,0:T(8,128)S(1)} %multiply_right.1.mid_ref, ...), custom_call_target="tpu_custom_call" | custom-call | flops 10000 | bytes 10000 | tf_op jit(solution)/shard_map/apply_roots/pallas_call | solution.py:316
  (59 shorter events, 5.8 us)
Async XLA Ops:
  0.7 1.6 %copy-start = (bf16[4,512,512]{2,1,0:T(8,128)(2,1)S(1)}, bf16[4,512,512]{2,1,0:T(8,128)(2,1)}, u32[]{:S(2)}) copy-start(bf16[4,512,512]{2,1,0:T(8,128)(2,1)} %g_ref.3) | copy-start | bytes 6291460
  2.3 3.9 %copy-start.1 = (bf16[4,512,512]{2,1,0:T(8,128)(2,1)S(1)}, bf16[4,512,512]{2,1,0:T(8,128)(2,1)}, u32[]{:S(2)}) copy-start(bf16[4,512,512]{2,1,0:T(8,128)(2,1)} %g_ref.3) | copy-start | bytes 6291460
  6.0 3.9 %collective-permute-start = (f32[2,2,2,352,128]{4,3,2,1,0:T(8,128)S(1)}, f32[2,2,2,352,128]{4,3,2,1,0:T(8,128)}, u32[]{:S(2)}, u32[]{:S(2)}) collective-permute-start(f32[2,2,2,352,128]{4,3,2,1,0:T(8,128)S(1)} %covariances.3), channel_id=1, source_target_pairs={{0,8},{8,0},{16,24},{24,16},{32,40},{40,32},{48,56},{56,48},{64,72... | collective-permute-start | bytes 4325384 | tf_op jit(solution)/shard_map/ppermute | solution.py:379
  11.5 7.5 %collective-permute-start.3 = (f16[2,352,128]{2,1,0:T(8,128)(2,1)S(1)}, f16[2,352,128]{2,1,0:T(8,128)(2,1)S(1)}, u32[]{:S(2)}, u32[]{:S(2)}) collective-permute-start(f16[2,352,128]{2,1,0:T(8,128)(2,1)S(1)} %fusion.7), channel_id=1, source_target_pairs={{0,32},{8,40},{16,48},{24,56},{32,0},{40,8},{48,16},{56,24},{64,96... | collective-permute-start | bytes 540680 | tf_op jit(solution)/shard_map/ppermute | solution.py:389
  13.5 10.5 %collective-permute-start.1 = (f16[2,352,128]{2,1,0:T(8,128)(2,1)S(1)}, f16[2,352,128]{2,1,0:T(8,128)(2,1)S(1)}, u32[]{:S(2)}, u32[]{:S(2)}) collective-permute-start(f16[2,352,128]{2,1,0:T(8,128)(2,1)S(1)} %get-tuple-element.23), channel_id=1, source_target_pairs={{0,16},{8,24},{16,0},{24,8},{32,48},{40,56},{48,32},{56,40},{64,80... | collective-permute-start | bytes 540680 | tf_op jit(solution)/shard_map/ppermute | solution.py:388
  14.3 9.8 %collective-permute-start.2 = (f16[2,352,128]{2,1,0:T(8,128)(2,1)S(1)}, f16[2,352,128]{2,1,0:T(8,128)(2,1)S(1)}, u32[]{:S(2)}, u32[]{:S(2)}) collective-permute-start(f16[2,352,128]{2,1,0:T(8,128)(2,1)S(1)} %get-tuple-element.24), channel_id=1, source_target_pairs={{0,48},{8,56},{16,32},{24,40},{32,16},{40,24},{48,0},{56,8},{64,11... | collective-permute-start | bytes 540680 | tf_op jit(solution)/shard_map/ppermute | solution.py:387
  24.2 10.7 %collective-permute-start.5 = (f16[208,128]{1,0:T(8,128)(2,1)S(1)}, f16[208,128]{1,0:T(8,128)(2,1)S(1)}, u32[]{:S(2)}, u32[]{:S(2)}) collective-permute-start(f16[208,128]{1,0:T(8,128)(2,1)S(1)} %fusion.14), channel_id=1, source_target_pairs={{0,128},{8,136},{16,144},{24,152},{32,160},{40,168},{48,176},{56,1... | collective-permute-start | bytes 159752 | tf_op jit(solution)/shard_map/ppermute | solution.py:398
  30.6 6.4 %collective-permute-start.4 = (f16[208,128]{1,0:T(8,128)(2,1)S(1)}, f16[208,128]{1,0:T(8,128)(2,1)S(1)}, u32[]{:S(2)}, u32[]{:S(2)}) collective-permute-start(f16[208,128]{1,0:T(8,128)(2,1)S(1)} %get-tuple-element.31), channel_id=1, source_target_pairs={{0,64},{8,72},{16,80},{24,88},{32,96},{40,104},{48,112},{56,120},{... | collective-permute-start | bytes 159752 | tf_op jit(solution)/shard_map/ppermute | solution.py:398
  32.2 5.5 %collective-permute-start.6 = (f16[208,128]{1,0:T(8,128)(2,1)S(1)}, f16[208,128]{1,0:T(8,128)(2,1)S(1)}, u32[]{:S(2)}, u32[]{:S(2)}) collective-permute-start(f16[208,128]{1,0:T(8,128)(2,1)S(1)} %get-tuple-element.32), channel_id=1, source_target_pairs={{0,192},{8,200},{16,208},{24,216},{32,224},{40,232},{48,240},{56,2... | collective-permute-start | bytes 159752 | tf_op jit(solution)/shard_map/ppermute | solution.py:398
  46.2 6.5 %collective-permute-start.9 = (bf16[176,128]{1,0:T(8,128)(2,1)S(1)}, bf16[176,128]{1,0:T(8,128)(2,1)S(1)}, u32[]{:S(2)}, u32[]{:S(2)}) collective-permute-start(bf16[176,128]{1,0:T(8,128)(2,1)S(1)} %inverse_roots.1), channel_id=1, source_target_pairs={{0,192},{8,200},{16,208},{24,216},{32,224},{40,232},{48,240},{56,2... | collective-permute-start | bytes 135176 | tf_op jit(solution)/shard_map/ppermute | solution.py:402
  50.2 8.2 %collective-permute-start.8 = (bf16[176,128]{1,0:T(8,128)(2,1)S(1)}, bf16[176,128]{1,0:T(8,128)(2,1)S(1)}, u32[]{:S(2)}, u32[]{:S(2)}) collective-permute-start(bf16[176,128]{1,0:T(8,128)(2,1)S(1)} %inverse_roots.1), channel_id=1, source_target_pairs={{0,128},{8,136},{16,144},{24,152},{32,160},{40,168},{48,176},{56,1... | collective-permute-start | bytes 135176 | tf_op jit(solution)/shard_map/ppermute | solution.py:402
  51.0 7.4 %collective-permute-start.7 = (bf16[176,128]{1,0:T(8,128)(2,1)S(1)}, bf16[176,128]{1,0:T(8,128)(2,1)S(1)}, u32[]{:S(2)}, u32[]{:S(2)}) collective-permute-start(bf16[176,128]{1,0:T(8,128)(2,1)S(1)} %inverse_roots.1), channel_id=1, source_target_pairs={{0,64},{8,72},{16,80},{24,88},{32,96},{40,104},{48,112},{56,120},{... | collective-permute-start | bytes 135176 | tf_op jit(solution)/shard_map/ppermute | solution.py:402
  58.4 10.6 %collective-permute-start.15 = (bf16[704,128]{1,0:T(8,128)(2,1)S(1)}, bf16[704,128]{1,0:T(8,128)(2,1)S(1)}, u32[]{:S(2)}, u32[]{:S(2)}) collective-permute-start(bf16[704,128]{1,0:T(8,128)(2,1)S(1)} %pad_maximum_fusion.1), channel_id=1, source_target_pairs={{0,48},{8,56},{16,32},{24,40},{32,16},{40,24},{48,0},{56,8},{64,11... | collective-permute-start | bytes 540680 | tf_op jit(solution)/shard_map/ppermute | solution.py:407
  59.1 9.9 %collective-permute-start.14 = (bf16[704,128]{1,0:T(8,128)(2,1)S(1)}, bf16[704,128]{1,0:T(8,128)(2,1)S(1)}, u32[]{:S(2)}, u32[]{:S(2)}) collective-permute-start(bf16[704,128]{1,0:T(8,128)(2,1)S(1)} %pad_maximum_fusion.1), channel_id=1, source_target_pairs={{0,32},{8,40},{16,48},{24,56},{32,0},{40,8},{48,16},{56,24},{64,96... | collective-permute-start | bytes 540680 | tf_op jit(solution)/shard_map/ppermute | solution.py:406
  60.5 8.5 %collective-permute-start.13 = (bf16[704,128]{1,0:T(8,128)(2,1)S(1)}, bf16[704,128]{1,0:T(8,128)(2,1)S(1)}, u32[]{:S(2)}, u32[]{:S(2)}) collective-permute-start(bf16[704,128]{1,0:T(8,128)(2,1)S(1)} %pad_maximum_fusion.1), channel_id=1, source_target_pairs={{0,16},{8,24},{16,0},{24,8},{32,48},{40,56},{48,32},{56,40},{64,80... | collective-permute-start | bytes 540680 | tf_op jit(solution)/shard_map/ppermute | solution.py:405
  62.0 1.4 %collective-permute-start.10 = (bf16[704,128]{1,0:T(8,128)(2,1)S(1)}, bf16[704,128]{1,0:T(8,128)(2,1)S(1)}, u32[]{:S(2)}, u32[]{:S(2)}) collective-permute-start(bf16[704,128]{1,0:T(8,128)(2,1)S(1)} %pad_maximum_fusion.1), channel_id=1, source_target_pairs={{0,8},{8,0},{16,24},{24,16},{32,40},{40,32},{48,56},{56,48},{64,72... | collective-permute-start | bytes 540680 | tf_op jit(solution)/shard_map/ppermute | solution.py:408
  62.3 14.6 %copy-start.4 = (bf16[4,1376,128]{2,1,0:T(8,128)(2,1)S(1)}, bf16[4,1376,128]{2,1,0:T(8,128)(2,1)}, u32[]{:S(2)}) copy-start(bf16[4,1376,128]{2,1,0:T(8,128)(2,1)} %w_ref.1) | copy-start | bytes 4227076
  63.4 12.5 %collective-permute-start.12 = (bf16[144,128]{1,0:T(8,128)(2,1)S(1)}, bf16[144,128]{1,0:T(8,128)(2,1)S(1)}, u32[]{:S(2)}, u32[]{:S(2)}) collective-permute-start(bf16[144,128]{1,0:T(8,128)(2,1)S(1)} %concatenate.30), channel_id=1, source_target_pairs={{0,3},{1,36},{2,65},{3,98},{4,130},{5,165},{6,192},{7,227},{8,11},... | collective-permute-start | bytes 110600 | tf_op jit(solution)/shard_map/ppermute | solution.py:409
  63.9 13.1 %collective-permute-start.11 = (bf16[144,128]{1,0:T(8,128)(2,1)S(1)}, bf16[144,128]{1,0:T(8,128)(2,1)S(1)}, u32[]{:S(2)}, u32[]{:S(2)}) collective-permute-start(bf16[144,128]{1,0:T(8,128)(2,1)S(1)} %concatenate.30), channel_id=1, source_target_pairs={{0,5},{1,38},{2,67},{3,97},{4,132},{5,167},{6,194},{7,224},{8,13},... | collective-permute-start | bytes 110600 | tf_op jit(solution)/shard_map/ppermute | solution.py:409
  69.1 9.1 %collective-permute-start.16 = (bf16[2112,128]{1,0:T(8,128)(2,1)S(1)}, bf16[2112,128]{1,0:T(8,128)(2,1)S(1)}, u32[]{:S(2)}, u32[]{:S(2)}) collective-permute-start(bf16[2112,128]{1,0:T(8,128)(2,1)S(1)} %pad_maximum_fusion), channel_id=1, source_target_pairs={{0,8},{8,0},{16,24},{24,16},{32,40},{40,32},{48,56},{56,48},{64,72... | collective-permute-start | bytes 1622024 | tf_op jit(solution)/shard_map/ppermute | solution.py:411
  69.9 9.0 %copy-start.2 = (s32[4,8]{1,0:T(4,128)S(1)}, s32[4,8]{1,0:T(4,128)}, u32[]{:S(2)}) copy-start(s32[4,8]{1,0:T(4,128)} %oa_ref.1) | copy-start | bytes 388
  69.9 9.0 %copy-start.3 = (s32[4,4]{1,0:T(4,128)S(1)}, s32[4,4]{1,0:T(4,128)}, u32[]{:S(2)}) copy-start(s32[4,4]{1,0:T(4,128)} %og_ref.1) | copy-start | bytes 196

commit v5 on v4

--- a/solution.py
+++ b/solution.py
@@ -264,59 +264,81 @@
     out_ref, sa_ref, sg_ref,
 ):
     z, y, c = (at_ref[i] for i in range(3))
-    position = 4 * z + 2 * y + c
-    owned_a, owned_g = owned_blocks(oa_ref, 8, position), owned_blocks(og_ref, 4, position)
 
     def place(z_of, y_of, c_of):
         odd = (z ^ z_of) & 1
         turn = (((z ^ odd) - z_of) & 7) >> 1
         return c_of ^ c, 8 * odd + 4 * (y_of ^ y) + turn
 
-    for beside, full_ref in enumerate((full0_ref, full1_ref)):
-        for odd in range(2):
-            layer = 2 * (c ^ beside) + odd
-            for quad in range(2):
-                results = []
-                for k in range(4 * quad, 4 * quad + 4):
-                    _, slot = place(k, odd, c ^ beside)
-                    left = full_ref[slot, 0:BA, 0:BA]
-                    x = mid_ref[layer, BA * k : BA * (k + 1)].astype(jnp.bfloat16)
-                    results.append(jnp.dot(left, x, preferred_element_type=jnp.float32))
-                out_ref[layer, 4 * BA * quad : 4 * BA * (quad + 1)] = jnp.concatenate(
-                    results, axis=0
-                ).astype(jnp.bfloat16)
+    step = pl.program_id(0)
+    odd = step & 1
+
+    def multiply(beside, full_ref):
+        layer = 2 * (c ^ beside) + odd
+        for quad in range(2):
+            results = []
+            for k in range(4 * quad, 4 * quad + 4):
+                _, slot = place(k, odd, c ^ beside)
+                left = full_ref[slot, 0:BA, 0:BA]
+                x = mid_ref[layer, BA * k : BA * (k + 1)].astype(jnp.bfloat16)
+                results.append(jnp.dot(left, x, preferred_element_type=jnp.float32))
+            out_ref[0, 4 * BA * quad : 4 * BA * (quad + 1)] = jnp.concatenate(
+                results, axis=0
+            ).astype(jnp.bfloat16)
+
+    @pl.when(step < 2)
+    def _():
+        multiply(0, full0_ref)
+
+    @pl.when(step >= 2)
+    def _():
+        multiply(1, full1_ref)
 
     def chosen(beside, slot, own_ref, other_ref):
         own, other = own_ref[slot].astype(jnp.float32), other_ref[slot].astype(jnp.float32)
         return jnp.where(beside == 0, own, other)
 
-    stored = []
-    for r in range(2):
-        block = owned_a[r]
-        held = jnp.maximum(block, 0)
-        layer = held >> 3
-        i, slot = place(held & 7, layer & 1, layer >> 1)
-        root = chosen(i, slot, full0_ref, full1_ref)[0:BA, 0:BA]
-        stored.append(jnp.where(block >= 0, root, 0.0))
-        block = owned_g[r]
-        held = jnp.maximum(block, 0)
-        layer, k = held >> 2, held & 3
-        halves = []
-        for half in range(2):
-            i, slot = place(layer + 4 * half, k >> 1, k & 1)
-            halves.append(chosen(i, slot, tails0_ref, tails1_ref))
-        spare = halves[0][DIAG - TAIL : DIAG - TAIL + 1]
-        root = unpack_halves(halves[0][16:48], halves[1][16:48], spare)
-        sg_ref[r] = jnp.where(block >= 0, root, 0.0).astype(jnp.bfloat16)
-    sa_ref[...] = jnp.stack(stored, axis=1).astype(jnp.bfloat16)
+    @pl.when(step == 0)
+    def _():
+        position = 4 * z + 2 * y + c
+        owned_a, owned_g = owned_blocks(oa_ref, 8, position), owned_blocks(og_ref, 4, position)
+        stored = []
+        for r in range(2):
+            block = owned_a[r]
+            held = jnp.maximum(block, 0)
+            layer = held >> 3
+            i, slot = place(held & 7, layer & 1, layer >> 1)
+            root = chosen(i, slot, full0_ref, full1_ref)[0:BA, 0:BA]
+            stored.append(jnp.where(block >= 0, root, 0.0))
+            block = owned_g[r]
+            held = jnp.maximum(block, 0)
+            layer, k = held >> 2, held & 3
+            halves = []
+            for half in range(2):
+                i, slot = place(layer + 4 * half, k >> 1, k & 1)
+                halves.append(chosen(i, slot, tails0_ref, tails1_ref))
+            spare = halves[0][DIAG - TAIL : DIAG - TAIL + 1]
+            root = unpack_halves(halves[0][16:48], halves[1][16:48], spare)
+            sg_ref[r] = jnp.where(block >= 0, root, 0.0).astype(jnp.bfloat16)
+        sa_ref[...] = jnp.stack(stored, axis=1).astype(jnp.bfloat16)
 
 
 def apply_roots(at, owner_a, owner_g, mid, *gathered):
     whole = pl.BlockSpec(memory_space=pltpu.VMEM)
+    scalars = pl.BlockSpec(memory_space=pltpu.SMEM)
+    layer_block = (1,) + mid.shape[1:]
     return pl.pallas_call(
         apply_kernel,
-        in_specs=[pl.BlockSpec(memory_space=pltpu.SMEM)] * 3 + [whole] * 5,
-        out_specs=[whole] * 3,
+        grid_spec=pltpu.PrefetchScalarGridSpec(
+            num_scalar_prefetch=1,
+            grid=(LAYERS,),
+            in_specs=[scalars] * 2 + [whole] * 5,
+            out_specs=[
+                pl.BlockSpec(layer_block, lambda i, s: (2 * (s[2] ^ (i >> 1)) + (i & 1), 0, 0)),
+                pl.BlockSpec((BA, 2, BA), lambda i, s: (0, 0, 0)),
+                pl.BlockSpec((2, BG, BG), lambda i, s: (0, 0, 0)),
+            ],
+        ),
         out_shape=[
             jax.ShapeDtypeStruct(mid.shape, jnp.bfloat16),
             jax.ShapeDtypeStruct((BA, 2, BA), jnp.bfloat16),

time: 82.2 us -> 83.7 us (1.018)
  Pallas kernels: 21.4 us -> 22.9 us
    pallas_call x1, Pallas kernels: 3.12 us -> 4.61 us  [apply_roots(): pl.pallas_call(apply_kernel, grid_spec=pltpu.PrefetchScalarGridSpec(num_s...]
where the time goes in v5:
time: 83.7 us; the launch traced here: 83.5 us
  starting transfers between devices  29.9 us (36%)
  waiting for transfers between devices  25.6 us (31%)
  Pallas kernels  22.9 us (27%)
  other arithmetic  2.12 us (3%)
  local copies, waits for them, and re-layouts  1.97 us (2%)
  between operations  0.97 us (1%)
    ppermute x3, starting transfers between devices, shards(): lax.ppermute(narrow(message(t)), 'dp', along_z(2 * t))  10.6 us
    pallas_call x1, Pallas kernels, inverse_roots(): pl.pallas_call(roots_kernel, in_specs=[pl.BlockSpec(memory_space=pltpu.SM...  8.35 us
    pallas_call x2, Pallas kernels, covariances(): pl.pallas_call(functools.partial(cov_kernel, scale), grid_spec=pltpu.Pref...  7.36 us
    ppermute x2, waiting for transfers between devices, shards(): lax.ppermute(tails, ('dp', 'grp'), pairs)  7.02 us
    ppermute x3, starting transfers between devices, shards(): lax.ppermute(packed, 'dp', along_z(2 * t))  6.48 us
    ppermute x3, waiting for transfers between devices, shards(): lax.ppermute(packed, 'dp', along_z(2 * t))  5.73 us
    ppermute x2, starting transfers between devices, shards(): lax.ppermute(tails, ('dp', 'grp'), pairs)  5.53 us
    ppermute x1, waiting for transfers between devices, shards(): got_y = lax.ppermute(narrow(other[0]), 'dp', OVER_Y)  5.03 us
  transfers between devices with their start and end apart: 17, of which 8 were waited for; matrix products, arithmetic and copies ran while one was open for 1% of the time, Pallas kernels for 7%

profile of v5, /device:TPU:30, one launch (start us, length us, event | category | flops | bytes accessed | tf_op | source)
XLA Modules:
  0.0 83.5 jit_solution(9390649697249486388)
XLA Ops:
  0.7 1.6 %copy-done = bf16[4,512,512]{2,1,0:T(8,128)(2,1)S(1)} copy-done((bf16[4,512,512]{2,1,0:T(8,128)(2,1)S(1)}, bf16[4,512,512]{2,1,0:T(8,128)(2,1)}, u32[]{:S(2)}) %copy-start) | copy-done | bytes 2097176
  2.3 3.7 %covariances.3 = f32[2,2,2,352,128]{4,3,2,1,0:T(8,128)S(1)} custom-call(s32[2]{0:T(128)S(1)} %pad_add_fusion.3.at_ref, bf16[4,1376,512]{2,1,0:T(8,128)(2,1)} %bitcast.34, bf16[4,512,512]{2,1,0:T(8,128)(2,1)S(1)} %copy-done), custom_call_target="tpu_custom_call" | custom-call | flops 10000 | bytes 10000 | tf_op jit(solution)/shard_map/covariances/pallas_call | solution.py:107
  6.2 3.6 %covariances.2 = f32[2,2,2,352,128]{4,3,2,1,0:T(8,128)S(1)} custom-call(s32[2]{0:T(128)S(1)} %pad_add_fusion.2.at_ref, bf16[4,1376,512]{2,1,0:T(8,128)(2,1)} %bitcast.35, bf16[4,512,512]{2,1,0:T(8,128)(2,1)S(1)} %copy-done.1), custom_call_target="tpu_custom_call" | custom-call | flops 10000 | bytes 10000 | tf_op jit(solution)/shard_map/covariances/pallas_call | solution.py:107
  9.9 1.5 %dynamic-slice_add_fusion = (f32[1,2,2,352,128]{4,3,2,1,0:T(8,128)S(1)}, f32[1,2,2,352,128]{4,3,2,1,0:T(8,128)S(1)}) fusion(f32[2,2,2,352,128]{4,3,2,1,0:T(8,128)} %collective-permute-done, s32[]{:T(128)S(6)} %select_n.20, f32[2,2,2,352,128]{4,3,2,1,0:T(8,128)S(1)} %covariances.2, s32[]{:T(128)S(6)} %select_n.19), kind=kLoop, calls=%fused_computation | loop fusion | flops 360448 | bytes 4325384 | tf_op jit(solution)/shard_map/add | solution.py:406
  11.5 2.0 %collective-permute-start.3 = (f16[2,352,128]{2,1,0:T(8,128)(2,1)S(1)}, f16[2,352,128]{2,1,0:T(8,128)(2,1)S(1)}, u32[]{:S(2)}, u32[]{:S(2)}) collective-permute-start(f16[2,352,128]{2,1,0:T(8,128)(2,1)S(1)} %fusion.7), channel_id=1, source_target_pairs={{0,32},{8,40},{16,48},{24,56},{32,0},{40,8},{48,16},{56,24},{64,96... | collective-permute-start | bytes 540680 | tf_op jit(solution)/shard_map/ppermute | solution.py:411
  14.3 0.8 collective-permute-start.2
  15.1 3.9 %collective-permute-done.3 = f16[2,352,128]{2,1,0:T(8,128)(2,1)S(1)} collective-permute-done((f16[2,352,128]{2,1,0:T(8,128)(2,1)S(1)}, f16[2,352,128]{2,1,0:T(8,128)(2,1)S(1)}, u32[]{:S(2)}, u32[]{:S(2)}) %collective-permute-start.3) | collective-permute-done | bytes 180256 | tf_op jit(solution)/shard_map/ppermute | solution.py:411
  19.0 5.0 %collective-permute-done.1 = f16[2,352,128]{2,1,0:T(8,128)(2,1)S(1)} collective-permute-done((f16[2,352,128]{2,1,0:T(8,128)(2,1)S(1)}, f16[2,352,128]{2,1,0:T(8,128)(2,1)S(1)}, u32[]{:S(2)}, u32[]{:S(2)}) %collective-permute-start.1) | collective-permute-done | bytes 180256 | tf_op jit(solution)/shard_map/ppermute | solution.py:410
  24.2 6.4 %collective-permute-start.5 = (f16[208,128]{1,0:T(8,128)(2,1)S(1)}, f16[208,128]{1,0:T(8,128)(2,1)S(1)}, u32[]{:S(2)}, u32[]{:S(2)}) collective-permute-start(f16[208,128]{1,0:T(8,128)(2,1)S(1)} %fusion.14), channel_id=1, source_target_pairs={{0,128},{8,136},{16,144},{24,152},{32,160},{40,168},{48,176},{56,1... | collective-permute-start | bytes 159752 | tf_op jit(solution)/shard_map/ppermute | solution.py:420
  30.6 1.5 %collective-permute-start.4 = (f16[208,128]{1,0:T(8,128)(2,1)S(1)}, f16[208,128]{1,0:T(8,128)(2,1)S(1)}, u32[]{:S(2)}, u32[]{:S(2)}) collective-permute-start(f16[208,128]{1,0:T(8,128)(2,1)S(1)} %get-tuple-element.31), channel_id=1, source_target_pairs={{0,64},{8,72},{16,80},{24,88},{32,96},{40,104},{48,112},{56,120},{... | collective-permute-start | bytes 159752 | tf_op jit(solution)/shard_map/ppermute | solution.py:420
  32.2 2.7 %collective-permute-start.6 = (f16[208,128]{1,0:T(8,128)(2,1)S(1)}, f16[208,128]{1,0:T(8,128)(2,1)S(1)}, u32[]{:S(2)}, u32[]{:S(2)}) collective-permute-start(f16[208,128]{1,0:T(8,128)(2,1)S(1)} %get-tuple-element.32), channel_id=1, source_target_pairs={{0,192},{8,200},{16,208},{24,216},{32,224},{40,232},{48,240},{56,2... | collective-permute-start | bytes 159752 | tf_op jit(solution)/shard_map/ppermute | solution.py:420
  34.9 2.1 %collective-permute-done.4 = f16[208,128]{1,0:T(8,128)(2,1)S(1)} collective-permute-done((f16[208,128]{1,0:T(8,128)(2,1)S(1)}, f16[208,128]{1,0:T(8,128)(2,1)S(1)}, u32[]{:S(2)}, u32[]{:S(2)}) %collective-permute-start.4) | collective-permute-done | bytes 53280 | tf_op jit(solution)/shard_map/ppermute | solution.py:420
  37.8 8.3 %inverse_roots.1 = bf16[176,128]{1,0:T(8,128)(2,1)S(1)} custom-call(s32[1]{0:T(128)} %bitcast.z_ref, f32[208,128]{1,0:T(8,128)S(1)} %fusion.12.total_ref), custom_call_target="tpu_custom_call" | custom-call | flops 10000 | bytes 10000 | tf_op jit(solution)/shard_map/inverse_roots/pallas_call | solution.py:178
  46.2 4.0 %collective-permute-start.9 = (bf16[176,128]{1,0:T(8,128)(2,1)S(1)}, bf16[176,128]{1,0:T(8,128)(2,1)S(1)}, u32[]{:S(2)}, u32[]{:S(2)}) collective-permute-start(bf16[176,128]{1,0:T(8,128)(2,1)S(1)} %inverse_roots.1), channel_id=1, source_target_pairs={{0,192},{8,200},{16,208},{24,216},{32,224},{40,232},{48,240},{56,2... | collective-permute-start | bytes 135176 | tf_op jit(solution)/shard_map/ppermute | solution.py:424
  51.0 1.7 %collective-permute-start.7 = (bf16[176,128]{1,0:T(8,128)(2,1)S(1)}, bf16[176,128]{1,0:T(8,128)(2,1)S(1)}, u32[]{:S(2)}, u32[]{:S(2)}) collective-permute-start(bf16[176,128]{1,0:T(8,128)(2,1)S(1)} %inverse_roots.1), channel_id=1, source_target_pairs={{0,64},{8,72},{16,80},{24,88},{32,96},{40,104},{48,112},{56,120},{... | collective-permute-start | bytes 135176 | tf_op jit(solution)/shard_map/ppermute | solution.py:424
  52.7 5.7 %collective-permute-done.8 = bf16[176,128]{1,0:T(8,128)(2,1)S(1)} collective-permute-done((bf16[176,128]{1,0:T(8,128)(2,1)S(1)}, bf16[176,128]{1,0:T(8,128)(2,1)S(1)}, u32[]{:S(2)}, u32[]{:S(2)}) %collective-permute-start.8) | collective-permute-done | bytes 45088 | tf_op jit(solution)/shard_map/ppermute | solution.py:424
  59.1 1.4 %collective-permute-start.14 = (bf16[704,128]{1,0:T(8,128)(2,1)S(1)}, bf16[704,128]{1,0:T(8,128)(2,1)S(1)}, u32[]{:S(2)}, u32[]{:S(2)}) collective-permute-start(bf16[704,128]{1,0:T(8,128)(2,1)S(1)} %pad_maximum_fusion.1), channel_id=1, source_target_pairs={{0,32},{8,40},{16,48},{24,56},{32,0},{40,8},{48,16},{56,24},{64,96... | collective-permute-start | bytes 540680 | tf_op jit(solution)/shard_map/ppermute | solution.py:428
  60.5 1.5 %collective-permute-start.13 = (bf16[704,128]{1,0:T(8,128)(2,1)S(1)}, bf16[704,128]{1,0:T(8,128)(2,1)S(1)}, u32[]{:S(2)}, u32[]{:S(2)}) collective-permute-start(bf16[704,128]{1,0:T(8,128)(2,1)S(1)} %pad_maximum_fusion.1), channel_id=1, source_target_pairs={{0,16},{8,24},{16,0},{24,8},{32,48},{40,56},{48,32},{56,40},{64,80... | collective-permute-start | bytes 540680 | tf_op jit(solution)/shard_map/ppermute | solution.py:427
  62.3 1.1 %collective-permute-done.10.refs_0_ = bf16[704,128]{1,0:T(8,128)(2,1)S(1)} collective-permute-done((bf16[704,128]{1,0:T(8,128)(2,1)S(1)}, bf16[704,128]{1,0:T(8,128)(2,1)S(1)}, u32[]{:S(2)}, u32[]{:S(2)}) %collective-permute-start.10) | collective-permute-done | bytes 180256 | tf_op jit(solution)/shard_map/ppermute | solution.py:430
  63.9 5.1 %collective-permute-start.11 = (bf16[144,128]{1,0:T(8,128)(2,1)S(1)}, bf16[144,128]{1,0:T(8,128)(2,1)S(1)}, u32[]{:S(2)}, u32[]{:S(2)}) collective-permute-start(bf16[144,128]{1,0:T(8,128)(2,1)S(1)} %concatenate.30), channel_id=1, source_target_pairs={{0,5},{1,38},{2,67},{3,97},{4,132},{5,167},{6,194},{7,224},{8,13},... | collective-permute-start | bytes 110600 | tf_op jit(solution)/shard_map/ppermute | solution.py:431
  69.9 6.0 %collective-permute-done.12.odd_ref = bf16[144,128]{1,0:T(8,128)(2,1)S(1)} collective-permute-done((bf16[144,128]{1,0:T(8,128)(2,1)S(1)}, bf16[144,128]{1,0:T(8,128)(2,1)S(1)}, u32[]{:S(2)}, u32[]{:S(2)}) %collective-permute-start.12) | collective-permute-done | bytes 36896 | tf_op jit(solution)/shard_map/ppermute | solution.py:431
  75.9 1.0 %collective-permute-done.11.even_ref = bf16[144,128]{1,0:T(8,128)(2,1)S(1)} collective-permute-done((bf16[144,128]{1,0:T(8,128)(2,1)S(1)}, bf16[144,128]{1,0:T(8,128)(2,1)S(1)}, u32[]{:S(2)}, u32[]{:S(2)}) %collective-permute-start.11) | collective-permute-done | bytes 36896 | tf_op jit(solution)/shard_map/ppermute | solution.py:431
  77.0 1.2 %multiply_right.1.mid_ref = f32[4,1376,128]{2,1,0:T(8,128)S(1)} custom-call(s32[2]{0:T(128)S(1)} %pad_add_fusion.1.at_ref, bf16[4,1376,128]{2,1,0:T(8,128)(2,1)S(1)} %copy-done.4, bf16[144,128]{1,0:T(8,128)(2,1)S(1)} %collective-permute-done.11.even_ref, bf16[144,128]{1,0:T(8,128)(2,1)S(1)} %collective-permute-done.12.odd_ref), custom_call_target="tpu_custom_call" | custom-call | flops 20000000000 | bytes 6000000 | tf_op jit(solution)/shard_map/multiply_right/pallas_call | solution.py:218
  78.9 4.6 %apply_roots.1 = (bf16[4,1376,128]{2,1,0:T(8,128)(2,1)}, bf16[172,2,172]{2,1,0:T(2,128)(2,1)}, bf16[2,128,128]{2,1,0:T(8,128)(2,1)}) custom-call(s32[3]{0:T(128)S(1)} %pad_add_fusion.at_ref, s32[4,8]{1,0:T(4,128)S(1)} %copy-done.2, s32[4,4]{1,0:T(4,128)S(1)} %copy-done.3, f32[4,1376,128]{2,1,0:T(8,128)S(1)} %multiply_right.1.mid_ref, ...), custom_call_target="tpu_custom_call" | custom-call | flops 10000 | bytes 10000 | tf_op jit(solution)/shard_map/apply_roots/pallas_call | solution.py:330
  (59 shorter events, 5.8 us)
Async XLA Ops:
  0.7 1.6 %copy-start = (bf16[4,512,512]{2,1,0:T(8,128)(2,1)S(1)}, bf16[4,512,512]{2,1,0:T(8,128)(2,1)}, u32[]{:S(2)}) copy-start(bf16[4,512,512]{2,1,0:T(8,128)(2,1)} %g_ref.3) | copy-start | bytes 6291460
  2.3 3.9 %copy-start.1 = (bf16[4,512,512]{2,1,0:T(8,128)(2,1)S(1)}, bf16[4,512,512]{2,1,0:T(8,128)(2,1)}, u32[]{:S(2)}) copy-start(bf16[4,512,512]{2,1,0:T(8,128)(2,1)} %g_ref.3) | copy-start | bytes 6291460
  6.0 3.9 %collective-permute-start = (f32[2,2,2,352,128]{4,3,2,1,0:T(8,128)S(1)}, f32[2,2,2,352,128]{4,3,2,1,0:T(8,128)}, u32[]{:S(2)}, u32[]{:S(2)}) collective-permute-start(f32[2,2,2,352,128]{4,3,2,1,0:T(8,128)S(1)} %covariances.3), channel_id=1, source_target_pairs={{0,8},{8,0},{16,24},{24,16},{32,40},{40,32},{48,56},{56,48},{64,72... | collective-permute-start | bytes 4325384 | tf_op jit(solution)/shard_map/ppermute | solution.py:401
  11.5 7.5 %collective-permute-start.3 = (f16[2,352,128]{2,1,0:T(8,128)(2,1)S(1)}, f16[2,352,128]{2,1,0:T(8,128)(2,1)S(1)}, u32[]{:S(2)}, u32[]{:S(2)}) collective-permute-start(f16[2,352,128]{2,1,0:T(8,128)(2,1)S(1)} %fusion.7), channel_id=1, source_target_pairs={{0,32},{8,40},{16,48},{24,56},{32,0},{40,8},{48,16},{56,24},{64,96... | collective-permute-start | bytes 540680 | tf_op jit(solution)/shard_map/ppermute | solution.py:411
  13.5 10.5 %collective-permute-start.1 = (f16[2,352,128]{2,1,0:T(8,128)(2,1)S(1)}, f16[2,352,128]{2,1,0:T(8,128)(2,1)S(1)}, u32[]{:S(2)}, u32[]{:S(2)}) collective-permute-start(f16[2,352,128]{2,1,0:T(8,128)(2,1)S(1)} %get-tuple-element.23), channel_id=1, source_target_pairs={{0,16},{8,24},{16,0},{24,8},{32,48},{40,56},{48,32},{56,40},{64,80... | collective-permute-start | bytes 540680 | tf_op jit(solution)/shard_map/ppermute | solution.py:410
  14.3 9.8 %collective-permute-start.2 = (f16[2,352,128]{2,1,0:T(8,128)(2,1)S(1)}, f16[2,352,128]{2,1,0:T(8,128)(2,1)S(1)}, u32[]{:S(2)}, u32[]{:S(2)}) collective-permute-start(f16[2,352,128]{2,1,0:T(8,128)(2,1)S(1)} %get-tuple-element.24), channel_id=1, source_target_pairs={{0,48},{8,56},{16,32},{24,40},{32,16},{40,24},{48,0},{56,8},{64,11... | collective-permute-start | bytes 540680 | tf_op jit(solution)/shard_map/ppermute | solution.py:409
  24.2 10.7 %collective-permute-start.5 = (f16[208,128]{1,0:T(8,128)(2,1)S(1)}, f16[208,128]{1,0:T(8,128)(2,1)S(1)}, u32[]{:S(2)}, u32[]{:S(2)}) collective-permute-start(f16[208,128]{1,0:T(8,128)(2,1)S(1)} %fusion.14), channel_id=1, source_target_pairs={{0,128},{8,136},{16,144},{24,152},{32,160},{40,168},{48,176},{56,1... | collective-permute-start | bytes 159752 | tf_op jit(solution)/shard_map/ppermute | solution.py:420
  30.6 6.4 %collective-permute-start.4 = (f16[208,128]{1,0:T(8,128)(2,1)S(1)}, f16[208,128]{1,0:T(8,128)(2,1)S(1)}, u32[]{:S(2)}, u32[]{:S(2)}) collective-permute-start(f16[208,128]{1,0:T(8,128)(2,1)S(1)} %get-tuple-element.31), channel_id=1, source_target_pairs={{0,64},{8,72},{16,80},{24,88},{32,96},{40,104},{48,112},{56,120},{... | collective-permute-start | bytes 159752 | tf_op jit(solution)/shard_map/ppermute | solution.py:420
  32.2 5.5 %collective-permute-start.6 = (f16[208,128]{1,0:T(8,128)(2,1)S(1)}, f16[208,128]{1,0:T(8,128)(2,1)S(1)}, u32[]{:S(2)}, u32[]{:S(2)}) collective-permute-start(f16[208,128]{1,0:T(8,128)(2,1)S(1)} %get-tuple-element.32), channel_id=1, source_target_pairs={{0,192},{8,200},{16,208},{24,216},{32,224},{40,232},{48,240},{56,2... | collective-permute-start | bytes 159752 | tf_op jit(solution)/shard_map/ppermute | solution.py:420
  46.2 6.5 %collective-permute-start.9 = (bf16[176,128]{1,0:T(8,128)(2,1)S(1)}, bf16[176,128]{1,0:T(8,128)(2,1)S(1)}, u32[]{:S(2)}, u32[]{:S(2)}) collective-permute-start(bf16[176,128]{1,0:T(8,128)(2,1)S(1)} %inverse_roots.1), channel_id=1, source_target_pairs={{0,192},{8,200},{16,208},{24,216},{32,224},{40,232},{48,240},{56,2... | collective-permute-start | bytes 135176 | tf_op jit(solution)/shard_map/ppermute | solution.py:424
  50.2 8.2 %collective-permute-start.8 = (bf16[176,128]{1,0:T(8,128)(2,1)S(1)}, bf16[176,128]{1,0:T(8,128)(2,1)S(1)}, u32[]{:S(2)}, u32[]{:S(2)}) collective-permute-start(bf16[176,128]{1,0:T(8,128)(2,1)S(1)} %inverse_roots.1), channel_id=1, source_target_pairs={{0,128},{8,136},{16,144},{24,152},{32,160},{40,168},{48,176},{56,1... | collective-permute-start | bytes 135176 | tf_op jit(solution)/shard_map/ppermute | solution.py:424
  51.0 7.4 %collective-permute-start.7 = (bf16[176,128]{1,0:T(8,128)(2,1)S(1)}, bf16[176,128]{1,0:T(8,128)(2,1)S(1)}, u32[]{:S(2)}, u32[]{:S(2)}) collective-permute-start(bf16[176,128]{1,0:T(8,128)(2,1)S(1)} %inverse_roots.1), channel_id=1, source_target_pairs={{0,64},{8,72},{16,80},{24,88},{32,96},{40,104},{48,112},{56,120},{... | collective-permute-start | bytes 135176 | tf_op jit(solution)/shard_map/ppermute | solution.py:424
  58.4 10.6 %collective-permute-start.15 = (bf16[704,128]{1,0:T(8,128)(2,1)S(1)}, bf16[704,128]{1,0:T(8,128)(2,1)S(1)}, u32[]{:S(2)}, u32[]{:S(2)}) collective-permute-start(bf16[704,128]{1,0:T(8,128)(2,1)S(1)} %pad_maximum_fusion.1), channel_id=1, source_target_pairs={{0,48},{8,56},{16,32},{24,40},{32,16},{40,24},{48,0},{56,8},{64,11... | collective-permute-start | bytes 540680 | tf_op jit(solution)/shard_map/ppermute | solution.py:429
  59.1 9.9 %collective-permute-start.14 = (bf16[704,128]{1,0:T(8,128)(2,1)S(1)}, bf16[704,128]{1,0:T(8,128)(2,1)S(1)}, u32[]{:S(2)}, u32[]{:S(2)}) collective-permute-start(bf16[704,128]{1,0:T(8,128)(2,1)S(1)} %pad_maximum_fusion.1), channel_id=1, source_target_pairs={{0,32},{8,40},{16,48},{24,56},{32,0},{40,8},{48,16},{56,24},{64,96... | collective-permute-start | bytes 540680 | tf_op jit(solution)/shard_map/ppermute | solution.py:428
  60.5 8.5 %collective-permute-start.13 = (bf16[704,128]{1,0:T(8,128)(2,1)S(1)}, bf16[704,128]{1,0:T(8,128)(2,1)S(1)}, u32[]{:S(2)}, u32[]{:S(2)}) collective-permute-start(bf16[704,128]{1,0:T(8,128)(2,1)S(1)} %pad_maximum_fusion.1), channel_id=1, source_target_pairs={{0,16},{8,24},{16,0},{24,8},{32,48},{40,56},{48,32},{56,40},{64,80... | collective-permute-start | bytes 540680 | tf_op jit(solution)/shard_map/ppermute | solution.py:427
  62.0 1.4 %collective-permute-start.10 = (bf16[704,128]{1,0:T(8,128)(2,1)S(1)}, bf16[704,128]{1,0:T(8,128)(2,1)S(1)}, u32[]{:S(2)}, u32[]{:S(2)}) collective-permute-start(bf16[704,128]{1,0:T(8,128)(2,1)S(1)} %pad_maximum_fusion.1), channel_id=1, source_target_pairs={{0,8},{8,0},{16,24},{24,16},{32,40},{40,32},{48,56},{56,48},{64,72... | collective-permute-start | bytes 540680 | tf_op jit(solution)/shard_map/ppermute | solution.py:430
  62.3 14.6 %copy-start.4 = (bf16[4,1376,128]{2,1,0:T(8,128)(2,1)S(1)}, bf16[4,1376,128]{2,1,0:T(8,128)(2,1)}, u32[]{:S(2)}) copy-start(bf16[4,1376,128]{2,1,0:T(8,128)(2,1)} %w_ref.1) | copy-start | bytes 4227076
  63.4 12.5 %collective-permute-start.12 = (bf16[144,128]{1,0:T(8,128)(2,1)S(1)}, bf16[144,128]{1,0:T(8,128)(2,1)S(1)}, u32[]{:S(2)}, u32[]{:S(2)}) collective-permute-start(bf16[144,128]{1,0:T(8,128)(2,1)S(1)} %concatenate.30), channel_id=1, source_target_pairs={{0,3},{1,36},{2,65},{3,98},{4,130},{5,165},{6,192},{7,227},{8,11},... | collective-permute-start | bytes 110600 | tf_op jit(solution)/shard_map/ppermute | solution.py:431
  63.9 13.1 %collective-permute-start.11 = (bf16[144,128]{1,0:T(8,128)(2,1)S(1)}, bf16[144,128]{1,0:T(8,128)(2,1)S(1)}, u32[]{:S(2)}, u32[]{:S(2)}) collective-permute-start(bf16[144,128]{1,0:T(8,128)(2,1)S(1)} %concatenate.30), channel_id=1, source_target_pairs={{0,5},{1,38},{2,67},{3,97},{4,132},{5,167},{6,194},{7,224},{8,13},... | collective-permute-start | bytes 110600 | tf_op jit(solution)/shard_map/ppermute | solution.py:431
  69.1 9.1 %collective-permute-start.16 = (bf16[2112,128]{1,0:T(8,128)(2,1)S(1)}, bf16[2112,128]{1,0:T(8,128)(2,1)S(1)}, u32[]{:S(2)}, u32[]{:S(2)}) collective-permute-start(bf16[2112,128]{1,0:T(8,128)(2,1)S(1)} %pad_maximum_fusion), channel_id=1, source_target_pairs={{0,8},{8,0},{16,24},{24,16},{32,40},{40,32},{48,56},{56,48},{64,72... | collective-permute-start | bytes 1622024 | tf_op jit(solution)/shard_map/ppermute | solution.py:433
  69.9 9.0 %copy-start.2 = (s32[4,8]{1,0:T(4,128)S(1)}, s32[4,8]{1,0:T(4,128)}, u32[]{:S(2)}) copy-start(s32[4,8]{1,0:T(4,128)} %oa_ref.1) | copy-start | bytes 388
  69.9 9.0 %copy-start.3 = (s32[4,4]{1,0:T(4,128)S(1)}, s32[4,4]{1,0:T(4,128)}, u32[]{:S(2)}) copy-start(s32[4,4]{1,0:T(4,128)} %og_ref.1) | copy-start | bytes 196

commit v6 on v3

--- a/solution.py
+++ b/solution.py
@@ -133,7 +133,7 @@
     return (one(0, 1) + one(1, 0)) + one(0, 0)
 
 
-def roots_kernel(z_ref, total_ref, packed_ref, wide, square):
+def roots_kernel(total_ref, packed_ref, wide, square):
     total = total_ref[...]
     spare = pltpu.roll(total[DIAG : DIAG + 1], HALF, 1)
     blocks = [unpack_wide(total[0:RA])[0:BA, 0:BA], unpack_square(total[RA:MSG], spare)]
@@ -167,22 +167,22 @@
     packed_ref[0:HALF] = folded.astype(jnp.bfloat16)
     packed_ref[HALF:112] = low.astype(jnp.bfloat16)
     packed_ref[112:RA] = corner.astype(jnp.bfloat16)
-    start = pl.multiple_of((z_ref[0] >> 2) * (RG // 2), RG // 2)
+    start = pl.multiple_of((lax.axis_index("dp") >> 4) * (RG // 2), RG // 2)
     packed_ref[RA:GATHERED] = square[pl.ds(start, RG // 2)].astype(jnp.bfloat16)
 
 
-def inverse_roots(total, z):
+def inverse_roots(total):
     whole = pl.BlockSpec(memory_space=pltpu.VMEM)
     return pl.pallas_call(
         roots_kernel,
-        in_specs=[pl.BlockSpec(memory_space=pltpu.SMEM), whole],
+        in_specs=[whole],
         out_specs=whole,
         out_shape=jax.ShapeDtypeStruct((GATHERED, BG), jnp.bfloat16),
         scratch_shapes=[pltpu.VMEM((176, 256), jnp.float32), pltpu.VMEM((RG, BG), jnp.float32)],
         compiler_params=PARAMS,
         cost_estimate=CHEAP,
         name="inverse_roots",
-    )(z.reshape(1), total)
+    )(total)
 
 
 def unpack_halves(first, second, spare):
@@ -198,8 +198,8 @@
     return first, second
 
 
-def right_kernel(at_ref, w_ref, even_ref, odd_ref, mid_ref, right, spares):
-    start = source_of(at_ref[0], at_ref[1])
+def right_kernel(w_ref, even_ref, odd_ref, mid_ref, right, spares):
+    start = source_of(lax.axis_index("dp") >> 2, lax.axis_index("grp"))
     for odd, ref in enumerate((even_ref, odd_ref)):
         for turn in range(4):
             source = ((start ^ odd) - 2 * turn) & 7
@@ -211,11 +211,11 @@
         mid_ref[layer] = product.astype(jnp.bfloat16).astype(jnp.float32)
 
 
-def multiply_right(at, weight_grad, even, odd):
+def multiply_right(weight_grad, even, odd):
     whole = pl.BlockSpec(memory_space=pltpu.VMEM)
     return pl.pallas_call(
         right_kernel,
-        in_specs=[pl.BlockSpec(memory_space=pltpu.SMEM)] + [whole] * 3,
+        in_specs=[whole] * 3,
         out_specs=whole,
         out_shape=jax.ShapeDtypeStruct(weight_grad.shape, jnp.float32),
         scratch_shapes=[
@@ -227,14 +227,14 @@
             flops=2 * 10**10, bytes_accessed=6 * 10**6, transcendentals=0
         ),
         name="multiply_right",
-    )(at, weight_grad, even, odd)
+    )(weight_grad, even, odd)
 
 
 def apply_kernel(
-    at_ref, oa_ref, og_ref, mid_ref, own_ref, first_ref, rest_ref, out_ref, sa_ref, sg_ref, a_ref
+    oa_ref, og_ref, mid_ref, own_ref, first_ref, rest_ref, out_ref, sa_ref, sg_ref, a_ref
 ):
-    z, y, c = (at_ref[i] for i in range(3))
-    position = 4 * z + 2 * y + c
+    position = lax.axis_index("dp")
+    z, y, c = position >> 2, (position >> 1) & 1, position & 1
     owned_a, owned_g = owned_blocks(oa_ref, 8, position), owned_blocks(og_ref, 4, position)
 
     def place(z_of, y_of, c_of):
@@ -279,11 +279,11 @@
     sa_ref[...] = jnp.stack(stored, axis=1).astype(jnp.bfloat16)
 
 
-def apply_roots(at, owner_a, owner_g, mid, *gathered):
+def apply_roots(owner_a, owner_g, mid, *gathered):
     whole = pl.BlockSpec(memory_space=pltpu.VMEM)
     return pl.pallas_call(
         apply_kernel,
-        in_specs=[pl.BlockSpec(memory_space=pltpu.SMEM)] * 3 + [whole] * 4,
+        in_specs=[pl.BlockSpec(memory_space=pltpu.SMEM)] * 2 + [whole] * 4,
         out_specs=[whole] * 3,
         out_shape=[
             jax.ShapeDtypeStruct(mid.shape, jnp.bfloat16),
@@ -294,7 +294,7 @@
         compiler_params=PARAMS,
         cost_estimate=CHEAP,
         name="apply_roots",
-    )(at, owner_a, owner_g, mid, *gathered)
+    )(owner_a, owner_g, mid, *gathered)
 
 
 def along_z(shift):
@@ -339,7 +339,6 @@
 
 def shards(hidden_acts, out_grads, weight_grad, owner_a, gradient_block_owner):
     position = lax.axis_index("dp")
-    column = lax.axis_index("grp")
     z, y, core = position // 4, lax.rem(position // 2, 2), lax.rem(position, 2)
     scale = 1.0 / (hidden_acts.shape[1] * lax.axis_size("dp"))
     turned = jnp.swapaxes(hidden_acts, 1, 2)
@@ -366,7 +365,7 @@
 
     arrived = [lax.ppermute(narrow(message(t)), "dp", along_z(2 * t)) for t in range(1, 4)]
     total = message(0) + sum(widen(x) for x in arrived)
-    packed = inverse_roots(total, z)
+    packed = inverse_roots(total)
 
     held = [packed] + [lax.ppermute(packed, "dp", along_z(2 * t)) for t in range(1, 4)]
     tails = tails_of(held)
@@ -379,10 +378,9 @@
     gathered = jnp.concatenate([held, got_y, got_z, got_both])
     rest = lax.ppermute(gathered[4 * GATHERED :], "dp", OVER_CORE)
 
-    at = jnp.stack([z, y, core])
-    mid = multiply_right(jnp.stack([z, column]), weight_grad, *tails)
+    mid = multiply_right(weight_grad, *tails)
     precond_grad, store_a, store_g = apply_roots(
-        at, owner_a, gradient_block_owner, mid, gathered, first, rest
+        owner_a, gradient_block_owner, mid, gathered, first, rest
     )
     return precond_grad, jnp.swapaxes(store_a, 0, 1)[None, None], store_g[None, None]
 

time: 82 us -> 81.5 us (level)
  transfers between devices with their start and end apart: 17 -> 17, of which waited for: 8 -> 8; matrix products, arithmetic and copies ran while one was open for 1% -> 1% of each run, Pallas kernels for 6% -> 5%
where the time goes in v6:
time: 81.5 us; the launch traced here: 81.3 us
  starting transfers between devices  30 us (37%)
  waiting for transfers between devices  26.4 us (32%)
  Pallas kernels  20 us (25%)
  other arithmetic  1.99 us (2%)
  local copies, waits for them, and re-layouts  1.97 us (2%)
  between operations  0.95 us (1%)
    ppermute x3, starting transfers between devices, shards(): lax.ppermute(narrow(message(t)), 'dp', along_z(2 * t))  10.6 us
    pallas_call x1, Pallas kernels, inverse_roots(): pl.pallas_call(roots_kernel, in_specs=[whole], out_specs=whole, out_shape...  8.34 us
    ppermute x2, waiting for transfers between devices, shards(): lax.ppermute(tails, ('dp', 'grp'), pairs)  7.71 us
    pallas_call x2, Pallas kernels, covariances(): pl.pallas_call(functools.partial(cov_kernel, scale), grid_spec=pltpu.Pref...  7.35 us
    ppermute x3, starting transfers between devices, shards(): lax.ppermute(packed, 'dp', along_z(2 * t))  6.48 us
    ppermute x3, waiting for transfers between devices, shards(): lax.ppermute(packed, 'dp', along_z(2 * t))  5.72 us
    ppermute x2, starting transfers between devices, shards(): lax.ppermute(tails, ('dp', 'grp'), pairs)  5.55 us
    ppermute x1, waiting for transfers between devices, shards(): got_y = lax.ppermute(narrow(other[0]), 'dp', OVER_Y)  5.03 us
  transfers between devices with their start and end apart: 17, of which 8 were waited for; matrix products, arithmetic and copies ran while one was open for 1% of the time, Pallas kernels for 5%

profile of v6, /device:TPU:30, one launch (start us, length us, event | category | flops | bytes accessed | tf_op | source)
XLA Modules:
  0.0 81.3 jit_solution(14327339282598755560)
XLA Ops:
  0.7 1.6 %copy-done = bf16[4,512,512]{2,1,0:T(8,128)(2,1)S(1)} copy-done((bf16[4,512,512]{2,1,0:T(8,128)(2,1)S(1)}, bf16[4,512,512]{2,1,0:T(8,128)(2,1)}, u32[]{:S(2)}) %copy-start) | copy-done | bytes 2097176
  2.3 3.7 %covariances.3 = f32[2,2,2,352,128]{4,3,2,1,0:T(8,128)S(1)} custom-call(s32[2]{0:T(128)S(1)} %pad_add_fusion.1.at_ref, bf16[4,1376,512]{2,1,0:T(8,128)(2,1)} %bitcast.32, bf16[4,512,512]{2,1,0:T(8,128)(2,1)S(1)} %copy-done), custom_call_target="tpu_custom_call" | custom-call | flops 10000 | bytes 10000 | tf_op jit(solution)/shard_map/covariances/pallas_call | solution.py:105
  6.2 3.6 %covariances.2 = f32[2,2,2,352,128]{4,3,2,1,0:T(8,128)S(1)} custom-call(s32[2]{0:T(128)S(1)} %pad_add_fusion.at_ref, bf16[4,1376,512]{2,1,0:T(8,128)(2,1)} %bitcast.33, bf16[4,512,512]{2,1,0:T(8,128)(2,1)S(1)} %copy-done.1), custom_call_target="tpu_custom_call" | custom-call | flops 10000 | bytes 10000 | tf_op jit(solution)/shard_map/covariances/pallas_call | solution.py:105
  9.9 1.5 %dynamic-slice_add_fusion = (f32[1,2,2,352,128]{4,3,2,1,0:T(8,128)S(1)}, f32[1,2,2,352,128]{4,3,2,1,0:T(8,128)S(1)}) fusion(f32[2,2,2,352,128]{4,3,2,1,0:T(8,128)} %collective-permute-done, s32[]{:T(128)S(6)} %select_n.20, f32[2,2,2,352,128]{4,3,2,1,0:T(8,128)S(1)} %covariances.2, s32[]{:T(128)S(6)} %select_n.19), kind=kLoop, calls=%fused_computation | loop fusion | flops 360448 | bytes 4325384 | tf_op jit(solution)/shard_map/add | solution.py:352
  11.5 2.0 %collective-permute-start.3 = (f16[2,352,128]{2,1,0:T(8,128)(2,1)S(1)}, f16[2,352,128]{2,1,0:T(8,128)(2,1)S(1)}, u32[]{:S(2)}, u32[]{:S(2)}) collective-permute-start(f16[2,352,128]{2,1,0:T(8,128)(2,1)S(1)} %fusion.7), channel_id=1, source_target_pairs={{0,32},{8,40},{16,48},{24,56},{32,0},{40,8},{48,16},{56,24},{64,96... | collective-permute-start | bytes 540680 | tf_op jit(solution)/shard_map/ppermute | solution.py:357
  14.3 0.8 %collective-permute-start.2 = (f16[2,352,128]{2,1,0:T(8,128)(2,1)S(1)}, f16[2,352,128]{2,1,0:T(8,128)(2,1)S(1)}, u32[]{:S(2)}, u32[]{:S(2)}) collective-permute-start(f16[2,352,128]{2,1,0:T(8,128)(2,1)S(1)} %get-tuple-element.16), channel_id=1, source_target_pairs={{0,48},{8,56},{16,32},{24,40},{32,16},{40,24},{48,0},{56,8},{64,11... | collective-permute-start | bytes 540680 | tf_op jit(solution)/shard_map/ppermute | solution.py:355
  15.1 3.9 %collective-permute-done.3 = f16[2,352,128]{2,1,0:T(8,128)(2,1)S(1)} collective-permute-done((f16[2,352,128]{2,1,0:T(8,128)(2,1)S(1)}, f16[2,352,128]{2,1,0:T(8,128)(2,1)S(1)}, u32[]{:S(2)}, u32[]{:S(2)}) %collective-permute-start.3) | collective-permute-done | bytes 180256 | tf_op jit(solution)/shard_map/ppermute | solution.py:357
  19.0 5.0 %collective-permute-done.1 = f16[2,352,128]{2,1,0:T(8,128)(2,1)S(1)} collective-permute-done((f16[2,352,128]{2,1,0:T(8,128)(2,1)S(1)}, f16[2,352,128]{2,1,0:T(8,128)(2,1)S(1)}, u32[]{:S(2)}, u32[]{:S(2)}) %collective-permute-start.1) | collective-permute-done | bytes 180256 | tf_op jit(solution)/shard_map/ppermute | solution.py:356
  24.2 6.4 %collective-permute-start.5 = (f16[208,128]{1,0:T(8,128)(2,1)S(1)}, f16[208,128]{1,0:T(8,128)(2,1)S(1)}, u32[]{:S(2)}, u32[]{:S(2)}) collective-permute-start(f16[208,128]{1,0:T(8,128)(2,1)S(1)} %fusion.14), channel_id=1, source_target_pairs={{0,128},{8,136},{16,144},{24,152},{32,160},{40,168},{48,176},{56,1... | collective-permute-start | bytes 159752 | tf_op jit(solution)/shard_map/ppermute | solution.py:366
  30.7 1.6 %collective-permute-start.4 = (f16[208,128]{1,0:T(8,128)(2,1)S(1)}, f16[208,128]{1,0:T(8,128)(2,1)S(1)}, u32[]{:S(2)}, u32[]{:S(2)}) collective-permute-start(f16[208,128]{1,0:T(8,128)(2,1)S(1)} %get-tuple-element.23), channel_id=1, source_target_pairs={{0,64},{8,72},{16,80},{24,88},{32,96},{40,104},{48,112},{56,120},{... | collective-permute-start | bytes 159752 | tf_op jit(solution)/shard_map/ppermute | solution.py:366
  32.2 2.7 %collective-permute-start.6 = (f16[208,128]{1,0:T(8,128)(2,1)S(1)}, f16[208,128]{1,0:T(8,128)(2,1)S(1)}, u32[]{:S(2)}, u32[]{:S(2)}) collective-permute-start(f16[208,128]{1,0:T(8,128)(2,1)S(1)} %get-tuple-element.24), channel_id=1, source_target_pairs={{0,192},{8,200},{16,208},{24,216},{32,224},{40,232},{48,240},{56,2... | collective-permute-start | bytes 159752 | tf_op jit(solution)/shard_map/ppermute | solution.py:366
  34.9 2.2 %collective-permute-done.4 = f16[208,128]{1,0:T(8,128)(2,1)S(1)} collective-permute-done((f16[208,128]{1,0:T(8,128)(2,1)S(1)}, f16[208,128]{1,0:T(8,128)(2,1)S(1)}, u32[]{:S(2)}, u32[]{:S(2)}) %collective-permute-start.4) | collective-permute-done | bytes 53280 | tf_op jit(solution)/shard_map/ppermute | solution.py:366
  37.8 8.3 %inverse_roots.1 = bf16[176,128]{1,0:T(8,128)(2,1)S(1)} custom-call(f32[208,128]{1,0:T(8,128)S(1)} %fusion.12.total_ref), custom_call_target="tpu_custom_call" | custom-call | flops 10000 | bytes 10000 | tf_op jit(solution)/shard_map/inverse_roots/pallas_call | solution.py:176
  46.1 4.0 %collective-permute-start.9 = (bf16[176,128]{1,0:T(8,128)(2,1)S(1)}, bf16[176,128]{1,0:T(8,128)(2,1)S(1)}, u32[]{:S(2)}, u32[]{:S(2)}) collective-permute-start(bf16[176,128]{1,0:T(8,128)(2,1)S(1)} %inverse_roots.1), channel_id=1, source_target_pairs={{0,192},{8,200},{16,208},{24,216},{32,224},{40,232},{48,240},{56,2... | collective-permute-start | bytes 135176 | tf_op jit(solution)/shard_map/ppermute | solution.py:370
  50.1 0.8 collective-permute-start.8
  50.9 1.7 %collective-permute-start.7 = (bf16[176,128]{1,0:T(8,128)(2,1)S(1)}, bf16[176,128]{1,0:T(8,128)(2,1)S(1)}, u32[]{:S(2)}, u32[]{:S(2)}) collective-permute-start(bf16[176,128]{1,0:T(8,128)(2,1)S(1)} %inverse_roots.1), channel_id=1, source_target_pairs={{0,64},{8,72},{16,80},{24,88},{32,96},{40,104},{48,112},{56,120},{... | collective-permute-start | bytes 135176 | tf_op jit(solution)/shard_map/ppermute | solution.py:370
  52.6 5.7 %collective-permute-done.8 = bf16[176,128]{1,0:T(8,128)(2,1)S(1)} collective-permute-done((bf16[176,128]{1,0:T(8,128)(2,1)S(1)}, bf16[176,128]{1,0:T(8,128)(2,1)S(1)}, u32[]{:S(2)}, u32[]{:S(2)}) %collective-permute-start.8) | collective-permute-done | bytes 45088 | tf_op jit(solution)/shard_map/ppermute | solution.py:370
  59.0 1.4 %collective-permute-start.14 = (bf16[704,128]{1,0:T(8,128)(2,1)S(1)}, bf16[704,128]{1,0:T(8,128)(2,1)S(1)}, u32[]{:S(2)}, u32[]{:S(2)}) collective-permute-start(bf16[704,128]{1,0:T(8,128)(2,1)S(1)} %pad_maximum_fusion.1), channel_id=1, source_target_pairs={{0,32},{8,40},{16,48},{24,56},{32,0},{40,8},{48,16},{56,24},{64,96... | collective-permute-start | bytes 540680 | tf_op jit(solution)/shard_map/ppermute | solution.py:374
  60.4 1.5 %collective-permute-start.13 = (bf16[704,128]{1,0:T(8,128)(2,1)S(1)}, bf16[704,128]{1,0:T(8,128)(2,1)S(1)}, u32[]{:S(2)}, u32[]{:S(2)}) collective-permute-start(bf16[704,128]{1,0:T(8,128)(2,1)S(1)} %pad_maximum_fusion.1), channel_id=1, source_target_pairs={{0,16},{8,24},{16,0},{24,8},{32,48},{40,56},{48,32},{56,40},{64,80... | collective-permute-start | bytes 540680 | tf_op jit(solution)/shard_map/ppermute | solution.py:373
  62.2 1.1 %collective-permute-done.10.first_ref = bf16[704,128]{1,0:T(8,128)(2,1)S(1)} collective-permute-done((bf16[704,128]{1,0:T(8,128)(2,1)S(1)}, bf16[704,128]{1,0:T(8,128)(2,1)S(1)}, u32[]{:S(2)}, u32[]{:S(2)}) %collective-permute-start.10) | collective-permute-done | bytes 180256 | tf_op jit(solution)/shard_map/ppermute | solution.py:376
  63.8 5.1 %collective-permute-start.11 = (bf16[144,128]{1,0:T(8,128)(2,1)S(1)}, bf16[144,128]{1,0:T(8,128)(2,1)S(1)}, u32[]{:S(2)}, u32[]{:S(2)}) collective-permute-start(bf16[144,128]{1,0:T(8,128)(2,1)S(1)} %concatenate.30), channel_id=1, source_target_pairs={{0,5},{1,38},{2,67},{3,97},{4,132},{5,167},{6,194},{7,224},{8,13},... | collective-permute-start | bytes 110600 | tf_op jit(solution)/shard_map/ppermute | solution.py:377
  69.2 6.7 %collective-permute-done.12.odd_ref = bf16[144,128]{1,0:T(8,128)(2,1)S(1)} collective-permute-done((bf16[144,128]{1,0:T(8,128)(2,1)S(1)}, bf16[144,128]{1,0:T(8,128)(2,1)S(1)}, u32[]{:S(2)}, u32[]{:S(2)}) %collective-permute-start.12) | collective-permute-done | bytes 36896 | tf_op jit(solution)/shard_map/ppermute | solution.py:377
  75.9 1.0 %collective-permute-done.11.even_ref = bf16[144,128]{1,0:T(8,128)(2,1)S(1)} collective-permute-done((bf16[144,128]{1,0:T(8,128)(2,1)S(1)}, bf16[144,128]{1,0:T(8,128)(2,1)S(1)}, u32[]{:S(2)}, u32[]{:S(2)}) %collective-permute-start.11) | collective-permute-done | bytes 36896 | tf_op jit(solution)/shard_map/ppermute | solution.py:377
  77.7 3.6 %apply_roots.1 = (bf16[4,1376,128]{2,1,0:T(8,128)(2,1)}, bf16[172,2,172]{2,1,0:T(2,128)(2,1)}, bf16[2,128,128]{2,1,0:T(8,128)(2,1)}) custom-call(s32[4,8]{1,0:T(4,128)S(1)} %copy-done.2, s32[4,4]{1,0:T(4,128)S(1)} %copy-done.3, f32[4,1376,128]{2,1,0:T(8,128)S(1)} %multiply_right.1.mid_ref, bf16[2816,128]{1,0:T(8,128)(2,1)S(1)} %constant_dynamic-update-slice_fusion.own_ref, ...), custom_call_target="tpu_custom_call" | custom-call | flops 10000 | bytes 10000 | tf_op jit(solution)/shard_map/apply_roots/pallas_call | solution.py:284
  (55 shorter events, 4.3 us)
Async XLA Ops:
  0.7 1.6 %copy-start = (bf16[4,512,512]{2,1,0:T(8,128)(2,1)S(1)}, bf16[4,512,512]{2,1,0:T(8,128)(2,1)}, u32[]{:S(2)}) copy-start(bf16[4,512,512]{2,1,0:T(8,128)(2,1)} %g_ref.3) | copy-start | bytes 6291460
  2.3 3.9 %copy-start.1 = (bf16[4,512,512]{2,1,0:T(8,128)(2,1)S(1)}, bf16[4,512,512]{2,1,0:T(8,128)(2,1)}, u32[]{:S(2)}) copy-start(bf16[4,512,512]{2,1,0:T(8,128)(2,1)} %g_ref.3) | copy-start | bytes 6291460
  6.0 3.9 %collective-permute-start = (f32[2,2,2,352,128]{4,3,2,1,0:T(8,128)S(1)}, f32[2,2,2,352,128]{4,3,2,1,0:T(8,128)}, u32[]{:S(2)}, u32[]{:S(2)}) collective-permute-start(f32[2,2,2,352,128]{4,3,2,1,0:T(8,128)S(1)} %covariances.3), channel_id=1, source_target_pairs={{0,8},{8,0},{16,24},{24,16},{32,40},{40,32},{48,56},{56,48},{64,72... | collective-permute-start | bytes 4325384 | tf_op jit(solution)/shard_map/ppermute | solution.py:347
  11.5 7.5 %collective-permute-start.3 = (f16[2,352,128]{2,1,0:T(8,128)(2,1)S(1)}, f16[2,352,128]{2,1,0:T(8,128)(2,1)S(1)}, u32[]{:S(2)}, u32[]{:S(2)}) collective-permute-start(f16[2,352,128]{2,1,0:T(8,128)(2,1)S(1)} %fusion.7), channel_id=1, source_target_pairs={{0,32},{8,40},{16,48},{24,56},{32,0},{40,8},{48,16},{56,24},{64,96... | collective-permute-start | bytes 540680 | tf_op jit(solution)/shard_map/ppermute | solution.py:357
  13.5 10.5 %collective-permute-start.1 = (f16[2,352,128]{2,1,0:T(8,128)(2,1)S(1)}, f16[2,352,128]{2,1,0:T(8,128)(2,1)S(1)}, u32[]{:S(2)}, u32[]{:S(2)}) collective-permute-start(f16[2,352,128]{2,1,0:T(8,128)(2,1)S(1)} %get-tuple-element.15), channel_id=1, source_target_pairs={{0,16},{8,24},{16,0},{24,8},{32,48},{40,56},{48,32},{56,40},{64,80... | collective-permute-start | bytes 540680 | tf_op jit(solution)/shard_map/ppermute | solution.py:356
  14.3 9.8 %collective-permute-start.2 = (f16[2,352,128]{2,1,0:T(8,128)(2,1)S(1)}, f16[2,352,128]{2,1,0:T(8,128)(2,1)S(1)}, u32[]{:S(2)}, u32[]{:S(2)}) collective-permute-start(f16[2,352,128]{2,1,0:T(8,128)(2,1)S(1)} %get-tuple-element.16), channel_id=1, source_target_pairs={{0,48},{8,56},{16,32},{24,40},{32,16},{40,24},{48,0},{56,8},{64,11... | collective-permute-start | bytes 540680 | tf_op jit(solution)/shard_map/ppermute | solution.py:355
  24.2 10.6 %collective-permute-start.5 = (f16[208,128]{1,0:T(8,128)(2,1)S(1)}, f16[208,128]{1,0:T(8,128)(2,1)S(1)}, u32[]{:S(2)}, u32[]{:S(2)}) collective-permute-start(f16[208,128]{1,0:T(8,128)(2,1)S(1)} %fusion.14), channel_id=1, source_target_pairs={{0,128},{8,136},{16,144},{24,152},{32,160},{40,168},{48,176},{56,1... | collective-permute-start | bytes 159752 | tf_op jit(solution)/shard_map/ppermute | solution.py:366
  30.7 6.4 %collective-permute-start.4 = (f16[208,128]{1,0:T(8,128)(2,1)S(1)}, f16[208,128]{1,0:T(8,128)(2,1)S(1)}, u32[]{:S(2)}, u32[]{:S(2)}) collective-permute-start(f16[208,128]{1,0:T(8,128)(2,1)S(1)} %get-tuple-element.23), channel_id=1, source_target_pairs={{0,64},{8,72},{16,80},{24,88},{32,96},{40,104},{48,112},{56,120},{... | collective-permute-start | bytes 159752 | tf_op jit(solution)/shard_map/ppermute | solution.py:366
  32.2 5.5 %collective-permute-start.6 = (f16[208,128]{1,0:T(8,128)(2,1)S(1)}, f16[208,128]{1,0:T(8,128)(2,1)S(1)}, u32[]{:S(2)}, u32[]{:S(2)}) collective-permute-start(f16[208,128]{1,0:T(8,128)(2,1)S(1)} %get-tuple-element.24), channel_id=1, source_target_pairs={{0,192},{8,200},{16,208},{24,216},{32,224},{40,232},{48,240},{56,2... | collective-permute-start | bytes 159752 | tf_op jit(solution)/shard_map/ppermute | solution.py:366
  46.1 6.5 %collective-permute-start.9 = (bf16[176,128]{1,0:T(8,128)(2,1)S(1)}, bf16[176,128]{1,0:T(8,128)(2,1)S(1)}, u32[]{:S(2)}, u32[]{:S(2)}) collective-permute-start(bf16[176,128]{1,0:T(8,128)(2,1)S(1)} %inverse_roots.1), channel_id=1, source_target_pairs={{0,192},{8,200},{16,208},{24,216},{32,224},{40,232},{48,240},{56,2... | collective-permute-start | bytes 135176 | tf_op jit(solution)/shard_map/ppermute | solution.py:370
  50.1 8.2 %collective-permute-start.8 = (bf16[176,128]{1,0:T(8,128)(2,1)S(1)}, bf16[176,128]{1,0:T(8,128)(2,1)S(1)}, u32[]{:S(2)}, u32[]{:S(2)}) collective-permute-start(bf16[176,128]{1,0:T(8,128)(2,1)S(1)} %inverse_roots.1), channel_id=1, source_target_pairs={{0,128},{8,136},{16,144},{24,152},{32,160},{40,168},{48,176},{56,1... | collective-permute-start | bytes 135176 | tf_op jit(solution)/shard_map/ppermute | solution.py:370
  50.9 7.4 %collective-permute-start.7 = (bf16[176,128]{1,0:T(8,128)(2,1)S(1)}, bf16[176,128]{1,0:T(8,128)(2,1)S(1)}, u32[]{:S(2)}, u32[]{:S(2)}) collective-permute-start(bf16[176,128]{1,0:T(8,128)(2,1)S(1)} %inverse_roots.1), channel_id=1, source_target_pairs={{0,64},{8,72},{16,80},{24,88},{32,96},{40,104},{48,112},{56,120},{... | collective-permute-start | bytes 135176 | tf_op jit(solution)/shard_map/ppermute | solution.py:370
  52.6 24.3 %copy-start.4 = (bf16[4,1376,128]{2,1,0:T(8,128)(2,1)S(1)}, bf16[4,1376,128]{2,1,0:T(8,128)(2,1)}, u32[]{:S(2)}) copy-start(bf16[4,1376,128]{2,1,0:T(8,128)(2,1)} %w_ref.1) | copy-start | bytes 4227076
  58.4 10.6 %collective-permute-start.15 = (bf16[704,128]{1,0:T(8,128)(2,1)S(1)}, bf16[704,128]{1,0:T(8,128)(2,1)S(1)}, u32[]{:S(2)}, u32[]{:S(2)}) collective-permute-start(bf16[704,128]{1,0:T(8,128)(2,1)S(1)} %pad_maximum_fusion.1), channel_id=1, source_target_pairs={{0,48},{8,56},{16,32},{24,40},{32,16},{40,24},{48,0},{56,8},{64,11... | collective-permute-start | bytes 540680 | tf_op jit(solution)/shard_map/ppermute | solution.py:375
  59.0 9.9 %collective-permute-start.14 = (bf16[704,128]{1,0:T(8,128)(2,1)S(1)}, bf16[704,128]{1,0:T(8,128)(2,1)S(1)}, u32[]{:S(2)}, u32[]{:S(2)}) collective-permute-start(bf16[704,128]{1,0:T(8,128)(2,1)S(1)} %pad_maximum_fusion.1), channel_id=1, source_target_pairs={{0,32},{8,40},{16,48},{24,56},{32,0},{40,8},{48,16},{56,24},{64,96... | collective-permute-start | bytes 540680 | tf_op jit(solution)/shard_map/ppermute | solution.py:374
  60.4 8.5 %collective-permute-start.13 = (bf16[704,128]{1,0:T(8,128)(2,1)S(1)}, bf16[704,128]{1,0:T(8,128)(2,1)S(1)}, u32[]{:S(2)}, u32[]{:S(2)}) collective-permute-start(bf16[704,128]{1,0:T(8,128)(2,1)S(1)} %pad_maximum_fusion.1), channel_id=1, source_target_pairs={{0,16},{8,24},{16,0},{24,8},{32,48},{40,56},{48,32},{56,40},{64,80... | collective-permute-start | bytes 540680 | tf_op jit(solution)/shard_map/ppermute | solution.py:373
  61.9 1.4 %collective-permute-start.10 = (bf16[704,128]{1,0:T(8,128)(2,1)S(1)}, bf16[704,128]{1,0:T(8,128)(2,1)S(1)}, u32[]{:S(2)}, u32[]{:S(2)}) collective-permute-start(bf16[704,128]{1,0:T(8,128)(2,1)S(1)} %pad_maximum_fusion.1), channel_id=1, source_target_pairs={{0,8},{8,0},{16,24},{24,16},{32,40},{40,32},{48,56},{56,48},{64,72... | collective-permute-start | bytes 540680 | tf_op jit(solution)/shard_map/ppermute | solution.py:376
  63.4 12.5 %collective-permute-start.12 = (bf16[144,128]{1,0:T(8,128)(2,1)S(1)}, bf16[144,128]{1,0:T(8,128)(2,1)S(1)}, u32[]{:S(2)}, u32[]{:S(2)}) collective-permute-start(bf16[144,128]{1,0:T(8,128)(2,1)S(1)} %concatenate.30), channel_id=1, source_target_pairs={{0,3},{1,36},{2,65},{3,98},{4,130},{5,165},{6,192},{7,227},{8,11},... | collective-permute-start | bytes 110600 | tf_op jit(solution)/shard_map/ppermute | solution.py:377
  63.8 13.1 %collective-permute-start.11 = (bf16[144,128]{1,0:T(8,128)(2,1)S(1)}, bf16[144,128]{1,0:T(8,128)(2,1)S(1)}, u32[]{:S(2)}, u32[]{:S(2)}) collective-permute-start(bf16[144,128]{1,0:T(8,128)(2,1)S(1)} %concatenate.30), channel_id=1, source_target_pairs={{0,5},{1,38},{2,67},{3,97},{4,132},{5,167},{6,194},{7,224},{8,13},... | collective-permute-start | bytes 110600 | tf_op jit(solution)/shard_map/ppermute | solution.py:377
  69.0 8.7 %collective-permute-start.16 = (bf16[2112,128]{1,0:T(8,128)(2,1)S(1)}, bf16[2112,128]{1,0:T(8,128)(2,1)S(1)}, u32[]{:S(2)}, u32[]{:S(2)}) collective-permute-start(bf16[2112,128]{1,0:T(8,128)(2,1)S(1)} %pad_maximum_fusion), channel_id=1, source_target_pairs={{0,8},{8,0},{16,24},{24,16},{32,40},{40,32},{48,56},{56,48},{64,72... | collective-permute-start | bytes 1622024 | tf_op jit(solution)/shard_map/ppermute | solution.py:379
  69.2 8.5 %copy-start.2 = (s32[4,8]{1,0:T(4,128)S(1)}, s32[4,8]{1,0:T(4,128)}, u32[]{:S(2)}) copy-start(s32[4,8]{1,0:T(4,128)} %oa_ref.1) | copy-start | bytes 388
  69.2 8.5 %copy-start.3 = (s32[4,4]{1,0:T(4,128)S(1)}, s32[4,4]{1,0:T(4,128)}, u32[]{:S(2)}) copy-start(s32[4,4]{1,0:T(4,128)} %og_ref.1) | copy-start | bytes 196
